TPU v7x, 32 devices: a whole 2x2x4 slice. The times are simulated.
32 devices in a mesh: expo: 4 (over y, core), patch: 8 (over z, x).
Axes of the slice: x: 2, y: 2, z: 4, core: 2. Of those that a mesh axis runs over, the one named last changes fastest.
Arguments:
- images: bfloat16 [384, 512, 512], P(('expo', 'patch')), may hold values from -120 to 120
- block_weight: bfloat16 [384], P(('expo', 'patch')), may hold values from 0.049804688 to 0.5
- block_patch: int32 [384, 1], P(('expo', 'patch')), may hold values from 0 to 7; in each aligned block of 12 rows (0 to 11, 12 to 23, ...) at most 2 rows name the same one
- block_offset: int32 [384, 2], P(('expo', 'patch')), may hold values from 0 to 768
- kernel_index: int32 [384], P(('expo', 'patch')), may hold values from 0 to 188
- coef_table: float32 [189, 3], replicated, may hold values from 0.5 to 2
Outputs:
- coadd_map: float32 [8, 1024, 1024], P('patch', 'expo')
- weight_map: float32 [8, 1024, 1024], P('patch', 'expo')
Inputs may be any that keep to these rules, and one draw needn't show every extreme that they name: `block_patch`: the 12 blocks of one device name one patch at most 2 times; in every draw some device names some patch exactly 2 times.
All inputs are finite; a program needn't handle non-finite values.
Results may differ from a plain program's by a relative error of at most 0.0043.
Values may be sent and summed in bfloat16 or wider, within the bound.
No kernel may reach another device: no remote copies, remote signals or barrier semaphores. Data moves between devices by JAX's collectives and lax.ppermute only.
A program may use at most 128 MiB of HBM per device.

v0:
```python
import jax
import jax.numpy as jnp
from jax import lax
from jax.sharding import PartitionSpec as P

BLOCK = 512
KHALF = 10
BASES = 3
CAP = 2
SIDE = 1024
MARGIN = 128
PGX = 4


SIGMAS = (0.8, 1.6, 3.2)
weight_floor = 0.5


def shifted(block, axis, distance):
    devices = range(lax.axis_size(axis))
    route = [(i - distance, i) for i in devices if i - distance in devices]
    return lax.ppermute(block, axis, route)


def gauss_taps(half_width):
    offsets = jnp.arange(-half_width, half_width + 1).astype(jnp.float32)
    profiles = []
    for sigma_value in SIGMAS:
        profile = jnp.exp(-offsets * offsets / (2.0 * sigma_value * sigma_value))
        profiles.append(profile / jnp.sum(profile))
    return jnp.stack(profiles).astype(jnp.bfloat16)


def tap_matrices(half_width, length):
    filter_taps = gauss_taps(half_width)
    places = jnp.arange(length)
    distance = places[:, None] - places[None, :] + half_width
    picker = (distance[:, :, None] == jnp.arange(2 * half_width + 1)[None, None, :]).astype(
        jnp.bfloat16
    )
    return jnp.einsum(
        "abt,nt->nab", picker, filter_taps, preferred_element_type=jnp.float32
    ).astype(jnp.bfloat16)


def lookup_coefs(indices, lookup_table):
    onehot = (indices[:, None] == jnp.arange(lookup_table.shape[0])[None, :]).astype(jnp.float32)
    return jnp.dot(onehot, lookup_table, precision=lax.Precision.HIGHEST)


def smooth_blocks(pixels, coefficients, tap_mats):
    block_count = pixels.shape[0]

    def one_pair(packed):
        tile_set, weights_c = packed
        spread = jnp.einsum("brj,njc->brnc", tile_set, tap_mats, preferred_element_type=jnp.float32)
        scaled = (spread * weights_c[:, None, :, None]).astype(jnp.bfloat16)
        merged = jnp.einsum("nrj,bjnc->brc", tap_mats, scaled, preferred_element_type=jnp.float32)
        return merged.astype(jnp.bfloat16)

    result = lax.map(
        one_pair,
        (
            pixels.reshape(block_count // 2, 2, BLOCK, BLOCK),
            coefficients.reshape(block_count // 2, 2, BASES),
        ),
    )
    return result.reshape(block_count, BLOCK, BLOCK)


def slot_numbers(destinations):
    ranks = jnp.arange(destinations.shape[1])
    before = ranks[None, :] < ranks[:, None]
    matches = destinations[:, :, None] == destinations[:, None, :]
    return jnp.sum(jnp.where(matches & before[None], 1, 0), axis=2).astype(jnp.int32)


def pull_side(strip, distance_by):
    return shifted(strip, "patch", distance_by)


def pull_row(strip, distance_by):
    return shifted(strip, "patch", distance_by)


def on_device(images, block_weight, block_patch, block_offset, kernel_index, coef_table):
    patch_count = lax.axis_size("patch")
    block_count = images.shape[0]
    slots_total = patch_count * CAP
    tap_mats = tap_matrices(KHALF, BLOCK)
    my_patch = lax.axis_index("patch")
    plane_count = 2
    all_dest, all_offset = (
        lax.all_gather(block_patch, "patch", axis=0, tiled=True),
        lax.all_gather(block_offset, "patch", axis=0, tiled=True),
    )
    own_dest = block_patch[:, 0]
    own_slot = slot_numbers(own_dest.reshape(1, block_count))[0]
    send_index = own_dest * CAP + own_slot
    payload = smooth_blocks(images, lookup_coefs(kernel_index, coef_table), tap_mats)
    send_pixels = jnp.zeros((slots_total, BLOCK, BLOCK), jnp.bfloat16).at[send_index].set(payload)
    send_pixels = send_pixels.reshape(patch_count, CAP, BLOCK, BLOCK)
    send_weight = (
        jnp.zeros((slots_total,), jnp.bfloat16)
        .at[send_index]
        .set(block_weight)
        .reshape(patch_count, CAP)
    )
    got_pixels, got_weight = (
        lax.all_to_all(send_pixels, "patch", split_axis=0, concat_axis=0, tiled=True),
        lax.all_to_all(send_weight, "patch", split_axis=0, concat_axis=0, tiled=True),
    )
    got_pixels = got_pixels.reshape(slots_total, BLOCK, BLOCK)
    got_weight = got_weight.reshape(slots_total)
    dest_table = all_dest.reshape(patch_count, block_count)
    all_slot = slot_numbers(dest_table)
    sources = jnp.arange(patch_count, dtype=jnp.int32)
    target = jnp.where(
        dest_table == my_patch, sources[:, None] * CAP + all_slot, slots_total
    ).reshape(-1)
    slot_offset = jnp.zeros((slots_total, 2), jnp.int32).at[target].set(all_offset, mode="drop")
    extent = SIDE + 2 * MARGIN

    def place(slot_pos, canvas_in):
        row_start = slot_offset[slot_pos, 0]
        col_start = slot_offset[slot_pos, 1]
        plane_start = jnp.zeros((), jnp.int32)
        weight_now = got_weight[slot_pos].astype(jnp.float32)
        layers = [
            weight_now * got_pixels[slot_pos].astype(jnp.float32),
            jnp.broadcast_to(weight_now, (BLOCK, BLOCK)),
        ]
        update = jnp.stack(layers[:plane_count])
        region = lax.dynamic_slice(
            canvas_in, (plane_start, row_start, col_start), (plane_count, BLOCK, BLOCK)
        )
        return lax.dynamic_update_slice(
            canvas_in, region + update, (plane_start, row_start, col_start)
        )

    canvas = lax.fori_loop(
        0, slots_total, place, jnp.zeros((plane_count, extent, extent), jnp.float32)
    )
    column = my_patch % PGX
    left_ok = (column > 0).astype(jnp.float32)
    right_ok = (column < PGX - 1).astype(jnp.float32)
    from_right = pull_side(canvas[:, :, 0:MARGIN], -1) * right_ok
    from_left = pull_side(canvas[:, :, SIDE + MARGIN :], 1) * left_ok
    canvas = canvas.at[:, :, SIDE : SIDE + MARGIN].add(from_right)
    canvas = canvas.at[:, :, MARGIN : 2 * MARGIN].add(from_left)
    from_below = pull_row(canvas[:, 0:MARGIN, :], -PGX)
    from_above = pull_row(canvas[:, SIDE + MARGIN :, :], PGX)
    canvas = canvas.at[:, SIDE : SIDE + MARGIN, :].add(from_below)
    canvas = canvas.at[:, MARGIN : 2 * MARGIN, :].add(from_above)
    interior = canvas[:, MARGIN : MARGIN + SIDE, MARGIN : MARGIN + SIDE]
    shares = lax.psum_scatter(interior, "expo", scatter_dimension=1, tiled=True)
    weight_map = shares[1]
    coadd_map = shares[0] / jnp.maximum(weight_map, weight_floor)
    return (coadd_map[None], weight_map[None])


def solution(mesh):
    return jax.shard_map(
        on_device,
        mesh=mesh,
        in_specs=(
            P(("expo", "patch"), None, None),
            P(("expo", "patch")),
            P(("expo", "patch"), None),
            P(("expo", "patch"), None),
            P(("expo", "patch")),
            P(),
        ),
        out_specs=(P("patch", "expo", None), P("patch", "expo", None)),
        check_vma=False,
    )
```

profile of v0, /device:TPU:0, one launch (start us, length us, event | category | flops | bytes accessed | tf_op | source)
XLA Modules:
  0.0 934.3 jit_solution(15294227200211250166)
XLA Ops:
  26.7 34.1 %while.27 = (s32[]{:T(128)}, bf16[6,2,512,512]{2,3,1,0:T(8,128)(2,1)}, bf16[6,2,512,512]{3,2,1,0:T(8,128)(2,1)}, bf16[3,512,512]{2,1,0:T(8,128)(2,1)S(1)}, f32[6,2,3]{2,1,0:T(2,128)S(1)}, /*index=5*/s32[]{:T(128)}) while((s32[]{:T(128)}, bf16[6,2,512,512]{2,3,1,0:T(8,128)(2,1)}, bf16[6,2,512,512]{3,2,1,0:T(8,128)(2,1)}, ...), condition=%wide.region_8.9_spmd, body=%wide.region_7.8_spmd.sunk | while | flops 3224895488 | bytes 5245057 | solution.py:61
  73.5 16.1 %scatter_fusion = bf16[16,512,512]{2,1,0:T(8,128)(2,1)} fusion(bf16[16,512,512]{2,1,0:T(8,128)(2,1)} %broadcast_in_dim.64, s32[12]{0:T(128)S(1)} %fusion.40, bf16[12,512,512]{2,1,0:T(8,128)(2,1)} %copy.42), kind=kCustom, calls=%fused_computation.2 | custom fusion | bytes 18874416 | tf_op jit(solution)/shard_map/scatter | solution.py:101
  97.2 181.4 %all-reduce.1 = s32[96]{0:T(128)S(1)} all-reduce(s32[96]{0:T(128)S(1)} %bitcast_dynamic-update-slice_fusion), channel_id=1, replica_groups=mesh['expo'=4,'patch'=8] {'patch'}, use_global_device_ids=true, to_apply=%add.1 | all-reduce | flops 96 | bytes 768
  279.3 18.6 %all-gather = s32[8,12,2]{1,2,0:T(2,128)S(1)} all-gather(s32[1,12,2]{1,2,0:T(2,128)S(1)} %bitcast.93), channel_id=1, replica_groups=mesh['expo'=4,'patch'=8] {'patch'}, dimensions={0}, use_global_device_ids=true | all-gather | bytes 864 | tf_op jit(solution)/shard_map/all_gather | solution.py:95
  304.7 379.7 %while.28 = (s32[]{:T(128)}, f32[2,1280,1280]{2,1,0:T(8,128)}, s32[16,2]{0,1:T(2,128)S(1)}, bf16[16]{0:T(256)(128)(2,1)S(1)}, bf16[16,512,512]{2,1,0:T(8,128)(2,1)}, /*index=5*/s32[]{:T(128)}, s32[]{:T(128)}, s32[]{:T(128)}) while((s32[]{:T(128)}, f32[2,1280,1280]{2,1,0:T(8,128)}, s32[16,2]{0,1:T(2,128)S(1)}, bf16[16]{0:T(256)(128)(2,1)S(1)}, ...), condition=%wide.region_11.12_spmd, body=%wide.region_10.11_spmd.sunk | while | flops 1048585 | bytes 11010267 | solution.py:141
  314.0 14.5 %dynamic_update_slice.15 = f32[2,1280,1280]{2,1,0:T(8,128)} dynamic-update-slice(f32[2,1280,1280]{2,1,0:T(8,128)} %get-tuple-element.341, f32[2,512,512]{2,1,0:T(8,128)S(1)} %pad_add_fusion.2, s32[]{:T(128)} %constant.183.clone.1..sunk, s32[]{:T(128)S(6)} %select_n.85, s32[]{:T(128)S(6)} %select_n.86) | dynamic-update-slice | bytes 4194308 | tf_op jit(solution)/shard_map/while/body/eval_jaxpr/dynamic_update_slice | solution.py:137
  337.9 14.5 %dynamic_update_slice.15 = f32[2,1280,1280]{2,1,0:T(8,128)} dynamic-update-slice(f32[2,1280,1280]{2,1,0:T(8,128)} %get-tuple-element.341, f32[2,512,512]{2,1,0:T(8,128)S(1)} %pad_add_fusion.2, s32[]{:T(128)} %constant.183.clone.1..sunk, s32[]{:T(128)S(6)} %select_n.85, s32[]{:T(128)S(6)} %select_n.86) | dynamic-update-slice | bytes 4194308 | tf_op jit(solution)/shard_map/while/body/eval_jaxpr/dynamic_update_slice | solution.py:137
  361.7 14.3 %dynamic_update_slice.15 = f32[2,1280,1280]{2,1,0:T(8,128)} dynamic-update-slice(f32[2,1280,1280]{2,1,0:T(8,128)} %get-tuple-element.341, f32[2,512,512]{2,1,0:T(8,128)S(1)} %pad_add_fusion.2, s32[]{:T(128)} %constant.183.clone.1..sunk, s32[]{:T(128)S(6)} %select_n.85, s32[]{:T(128)S(6)} %select_n.86) | dynamic-update-slice | bytes 4194308 | tf_op jit(solution)/shard_map/while/body/eval_jaxpr/dynamic_update_slice | solution.py:137
  408.9 14.3 %dynamic_update_slice.15 = f32[2,1280,1280]{2,1,0:T(8,128)} dynamic-update-slice(f32[2,1280,1280]{2,1,0:T(8,128)} %get-tuple-element.341, f32[2,512,512]{2,1,0:T(8,128)S(1)} %pad_add_fusion.2, s32[]{:T(128)} %constant.183.clone.1..sunk, s32[]{:T(128)S(6)} %select_n.85, s32[]{:T(128)S(6)} %select_n.86) | dynamic-update-slice | bytes 4194308 | tf_op jit(solution)/shard_map/while/body/eval_jaxpr/dynamic_update_slice | solution.py:137
  432.5 14.5 %dynamic_update_slice.15 = f32[2,1280,1280]{2,1,0:T(8,128)} dynamic-update-slice(f32[2,1280,1280]{2,1,0:T(8,128)} %get-tuple-element.341, f32[2,512,512]{2,1,0:T(8,128)S(1)} %pad_add_fusion.2, s32[]{:T(128)} %constant.183.clone.1..sunk, s32[]{:T(128)S(6)} %select_n.85, s32[]{:T(128)S(6)} %select_n.86) | dynamic-update-slice | bytes 4194308 | tf_op jit(solution)/shard_map/while/body/eval_jaxpr/dynamic_update_slice | solution.py:137
  456.4 14.4 %dynamic_update_slice.15 = f32[2,1280,1280]{2,1,0:T(8,128)} dynamic-update-slice(f32[2,1280,1280]{2,1,0:T(8,128)} %get-tuple-element.341, f32[2,512,512]{2,1,0:T(8,128)S(1)} %pad_add_fusion.2, s32[]{:T(128)} %constant.183.clone.1..sunk, s32[]{:T(128)S(6)} %select_n.85, s32[]{:T(128)S(6)} %select_n.86) | dynamic-update-slice | bytes 4194308 | tf_op jit(solution)/shard_map/while/body/eval_jaxpr/dynamic_update_slice | solution.py:137
  480.2 14.5 %dynamic_update_slice.15 = f32[2,1280,1280]{2,1,0:T(8,128)} dynamic-update-slice(f32[2,1280,1280]{2,1,0:T(8,128)} %get-tuple-element.341, f32[2,512,512]{2,1,0:T(8,128)S(1)} %pad_add_fusion.2, s32[]{:T(128)} %constant.183.clone.1..sunk, s32[]{:T(128)S(6)} %select_n.85, s32[]{:T(128)S(6)} %select_n.86) | dynamic-update-slice | bytes 4194308 | tf_op jit(solution)/shard_map/while/body/eval_jaxpr/dynamic_update_slice | solution.py:137
  527.5 14.5 %dynamic_update_slice.15 = f32[2,1280,1280]{2,1,0:T(8,128)} dynamic-update-slice(f32[2,1280,1280]{2,1,0:T(8,128)} %get-tuple-element.341, f32[2,512,512]{2,1,0:T(8,128)S(1)} %pad_add_fusion.2, s32[]{:T(128)} %constant.183.clone.1..sunk, s32[]{:T(128)S(6)} %select_n.85, s32[]{:T(128)S(6)} %select_n.86) | dynamic-update-slice | bytes 4194308 | tf_op jit(solution)/shard_map/while/body/eval_jaxpr/dynamic_update_slice | solution.py:137
  551.4 14.3 %dynamic_update_slice.15 = f32[2,1280,1280]{2,1,0:T(8,128)} dynamic-update-slice(f32[2,1280,1280]{2,1,0:T(8,128)} %get-tuple-element.341, f32[2,512,512]{2,1,0:T(8,128)S(1)} %pad_add_fusion.2, s32[]{:T(128)} %constant.183.clone.1..sunk, s32[]{:T(128)S(6)} %select_n.85, s32[]{:T(128)S(6)} %select_n.86) | dynamic-update-slice | bytes 4194308 | tf_op jit(solution)/shard_map/while/body/eval_jaxpr/dynamic_update_slice | solution.py:137
  575.1 14.5 %dynamic_update_slice.15 = f32[2,1280,1280]{2,1,0:T(8,128)} dynamic-update-slice(f32[2,1280,1280]{2,1,0:T(8,128)} %get-tuple-element.341, f32[2,512,512]{2,1,0:T(8,128)S(1)} %pad_add_fusion.2, s32[]{:T(128)} %constant.183.clone.1..sunk, s32[]{:T(128)S(6)} %select_n.85, s32[]{:T(128)S(6)} %select_n.86) | dynamic-update-slice | bytes 4194308 | tf_op jit(solution)/shard_map/while/body/eval_jaxpr/dynamic_update_slice | solution.py:137
  599.0 14.4 %dynamic_update_slice.15 = f32[2,1280,1280]{2,1,0:T(8,128)} dynamic-update-slice(f32[2,1280,1280]{2,1,0:T(8,128)} %get-tuple-element.341, f32[2,512,512]{2,1,0:T(8,128)S(1)} %pad_add_fusion.2, s32[]{:T(128)} %constant.183.clone.1..sunk, s32[]{:T(128)S(6)} %select_n.85, s32[]{:T(128)S(6)} %select_n.86) | dynamic-update-slice | bytes 4194308 | tf_op jit(solution)/shard_map/while/body/eval_jaxpr/dynamic_update_slice | solution.py:137
  622.7 14.2 %dynamic_update_slice.15 = f32[2,1280,1280]{2,1,0:T(8,128)} dynamic-update-slice(f32[2,1280,1280]{2,1,0:T(8,128)} %get-tuple-element.341, f32[2,512,512]{2,1,0:T(8,128)S(1)} %pad_add_fusion.2, s32[]{:T(128)} %constant.183.clone.1..sunk, s32[]{:T(128)S(6)} %select_n.85, s32[]{:T(128)S(6)} %select_n.86) | dynamic-update-slice | bytes 4194308 | tf_op jit(solution)/shard_map/while/body/eval_jaxpr/dynamic_update_slice | solution.py:137
  646.2 14.3 %dynamic_update_slice.15 = f32[2,1280,1280]{2,1,0:T(8,128)} dynamic-update-slice(f32[2,1280,1280]{2,1,0:T(8,128)} %get-tuple-element.341, f32[2,512,512]{2,1,0:T(8,128)S(1)} %pad_add_fusion.2, s32[]{:T(128)} %constant.183.clone.1..sunk, s32[]{:T(128)S(6)} %select_n.85, s32[]{:T(128)S(6)} %select_n.86) | dynamic-update-slice | bytes 4194308 | tf_op jit(solution)/shard_map/while/body/eval_jaxpr/dynamic_update_slice | solution.py:137
  669.9 14.5 %dynamic_update_slice.15 = f32[2,1280,1280]{2,1,0:T(8,128)} dynamic-update-slice(f32[2,1280,1280]{2,1,0:T(8,128)} %get-tuple-element.341, f32[2,512,512]{2,1,0:T(8,128)S(1)} %pad_add_fusion.2, s32[]{:T(128)} %constant.183.clone.1..sunk, s32[]{:T(128)S(6)} %select_n.85, s32[]{:T(128)S(6)} %select_n.86) | dynamic-update-slice | bytes 4194308 | tf_op jit(solution)/shard_map/while/body/eval_jaxpr/dynamic_update_slice | solution.py:137
  687.1 26.8 %collective-permute-done = f32[2,1280,128]{2,1,0:T(8,128)S(1)} collective-permute-done((f32[2,1280,128]{2,1,0:T(8,128)S(1)}, f32[2,1280,128]{2,1,0:T(8,128)S(1)}, u32[]{:S(2)}, u32[]{:S(2)}) %collective-permute-start) | collective-permute-done | bytes 1310752 | tf_op jit(solution)/shard_map/ppermute | solution.py:22
  719.2 24.1 %collective-permute-done.1 = f32[2,1280,128]{2,1,0:T(8,128)S(1)} collective-permute-done((f32[2,1280,128]{2,1,0:T(8,128)}, f32[2,1280,128]{2,1,0:T(8,128)S(1)}, u32[]{:S(2)}, u32[]{:S(2)}) %collective-permute-start.1) | collective-permute-done | bytes 1310752 | tf_op jit(solution)/shard_map/ppermute | solution.py:22
  748.7 60.6 %collective-permute-done.2 = f32[2,128,1280]{2,1,0:T(8,128)S(1)} collective-permute-done((f32[2,128,1280]{2,1,0:T(8,128)S(1)}, f32[2,128,1280]{2,1,0:T(8,128)S(1)}, u32[]{:S(2)}, u32[]{:S(2)}) %collective-permute-start.2) | collective-permute-done | bytes 1310752 | tf_op jit(solution)/shard_map/ppermute | solution.py:22
  813.8 26.6 %collective-permute-done.3 = f32[2,128,1280]{2,1,0:T(8,128)S(1)} collective-permute-done((f32[2,128,1280]{2,1,0:T(8,128)S(1)}, f32[2,128,1280]{2,1,0:T(8,128)S(1)}, u32[]{:S(2)}, u32[]{:S(2)}) %collective-permute-start.3) | collective-permute-done | bytes 1310752 | tf_op jit(solution)/shard_map/ppermute | solution.py:22
  851.3 73.1 %reduce-scatter.2.cloned.1.call-done = f32[2,256,1024]{2,1,0:T(8,128)} async-done(((f32[2,1024,1024]{2,1,0:T(8,128)}), f32[2,256,1024]{2,1,0:T(8,128)}) %reduce-scatter.2.cloned.1.call-update) | async-done | bytes 2097168 | tf_op jit(solution)/shard_map/reduce_scatter | solution.py:156
  (146 shorter events, 218.2 us)
Async XLA Ops:
  7.2 19.2 %copy-start = (f32[189,3]{0,1:T(4,128)S(1)}, f32[189,3]{0,1:T(4,128)}, u32[]{:S(2)}) copy-start(f32[189,3]{0,1:T(4,128)} %param.23) | copy-start | bytes 6808
  7.2 19.1 %copy-start.3 = (s32[12]{0:T(128)S(1)}, s32[12]{0:T(128)}, u32[]{:S(2)}) copy-start(s32[12]{0:T(128)} %param.22) | copy-start | bytes 148
  10.4 79.2 %all-to-all-start = ((bf16[8,1,2]{2,1,0:T(2,128)(2,1)}), bf16[8,1,2]{2,1,0:T(2,128)(2,1)S(1)}, u32[]{:S(2)}, u32[]{:S(2)}) async-start(bf16[8,1,2]{2,1,0:T(2,128)(2,1)} %all_to_all.12), calls=%async_computation | async-start | bytes 8192 | tf_op jit(solution)/shard_map/all_to_all | solution.py:111
  89.6 6.2 copy-start.5
  89.6 7.5 copy-start.4
  89.6 189.7 %copy-start.2 = (s32[12,2]{0,1:T(2,128)S(1)}, s32[12,2]{0,1:T(2,128)}, u32[]{:S(2)}) copy-start(s32[12,2]{0,1:T(2,128)} %param.21) | copy-start | bytes 292
  89.6 209.5 %all-to-all-start.1 = ((bf16[8,2,512,512]{3,2,1,0:T(8,128)(2,1)}), bf16[8,2,512,512]{3,2,1,0:T(8,128)(2,1)}, u32[]{:S(2)}, u32[]{:S(2)}) async-start(bf16[8,2,512,512]{3,2,1,0:T(8,128)(2,1)} %bitcast.91), calls=%async_computation.1 | async-start | bytes 16777216 | tf_op jit(solution)/shard_map/all_to_all | solution.py:110
  95.8 828.6 %reduce-scatter.2.cloned.1.call-start = ((), (), s32[]{:S(2)}) async-start(), calls=%async_computation.3 | async-start | bytes 10485760 | tf_op jit(solution)/shard_map/reduce_scatter | solution.py:156
  685.8 28.1 %collective-permute-start = (f32[2,1280,128]{2,1,0:T(8,128)S(1)}, f32[2,1280,128]{2,1,0:T(8,128)S(1)}, u32[]{:S(2)}, u32[]{:S(2)}) collective-permute-start(f32[2,1280,128]{2,1,0:T(8,128)S(1)} %slice.118), channel_id=1, source_target_pairs={{1,0},{2,1},{3,2},{4,3},{5,4},{6,5},{7,6},{9,8},{10,9},{11,10},{12... | collective-permute-start | bytes 3932168 | tf_op jit(solution)/shard_map/ppermute | solution.py:22
  717.6 25.7 %collective-permute-start.1 = (f32[2,1280,128]{2,1,0:T(8,128)}, f32[2,1280,128]{2,1,0:T(8,128)S(1)}, u32[]{:S(2)}, u32[]{:S(2)}) collective-permute-start(f32[2,1280,128]{2,1,0:T(8,128)} %get-tuple-element.244), channel_id=1, source_target_pairs={{0,1},{1,2},{2,3},{3,4},{4,5},{5,6},{6,7},{8,9},{9,10},{10,11},{11... | collective-permute-start | bytes 3932168 | tf_op jit(solution)/shard_map/ppermute | solution.py:22
  747.4 61.9 %collective-permute-start.2 = (f32[2,128,1280]{2,1,0:T(8,128)S(1)}, f32[2,128,1280]{2,1,0:T(8,128)S(1)}, u32[]{:S(2)}, u32[]{:S(2)}) collective-permute-start(f32[2,128,1280]{2,1,0:T(8,128)S(1)} %slice.130), channel_id=1, source_target_pairs={{4,0},{5,1},{6,2},{7,3},{12,8},{13,9},{14,10},{15,11},{20,16},{21,... | collective-permute-start | bytes 3932168 | tf_op jit(solution)/shard_map/ppermute | solution.py:22
  812.3 28.1 %collective-permute-start.3 = (f32[2,128,1280]{2,1,0:T(8,128)S(1)}, f32[2,128,1280]{2,1,0:T(8,128)S(1)}, u32[]{:S(2)}, u32[]{:S(2)}) collective-permute-start(f32[2,128,1280]{2,1,0:T(8,128)S(1)} %get-tuple-element.242), channel_id=1, source_target_pairs={{0,4},{1,5},{2,6},{3,7},{8,12},{9,13},{10,14},{11,15},{16,20},{17,... | collective-permute-start | bytes 3932168 | tf_op jit(solution)/shard_map/ppermute | solution.py:22
  851.3 76.2 %copy-start.1 = (f32[189,3]{0,1:T(4,128)S(1)}, f32[189,3]{0,1:T(4,128)}, u32[]{:S(2)}) copy-start(f32[189,3]{0,1:T(4,128)} %param.23) | copy-start | bytes 6808
Sparse Core Ops, SparseCore 0:
  851.4 72.9 reduce-scatter.1
where the time goes:
time: 942 us; the launch traced here: 934 us
  local copies, waits for them, and re-layouts  300 us (32%)
  waiting for transfers between devices  211 us (22%)
  blocking collectives  200 us (21%)
  other arithmetic  78.9 us (8%)
  loops' own time  72.1 us (8%)
  matrix products  38.6 us (4%)
  starting transfers between devices  19.1 us (2%)
  between operations  14.9 us (2%)
    dynamic_update_slice x16, local copies, waits for them, and re-layouts, place(): lax.dynamic_update_slice(canvas_in, region + update, (plane_start, row_st...  230 us
    unnamed x1, blocking collectives  181 us
    ppermute x4, waiting for transfers between devices, shifted(): return lax.ppermute(block, axis, route)  138 us
    reduce_scatter x1, waiting for transfers between devices, on_device(): shares = lax.psum_scatter(interior, 'expo', scatter_dimension=1, tiled=True)  73.1 us
    another operation x1, loops' own time, on_device(): lax.fori_loop(0, slots_total, place, jnp.zeros((plane_count, extent, exte...  72.1 us
    add x16, other arithmetic, place(): region + update  38.8 us
    dot_general x6, matrix products, one_pair(): jnp.einsum('nrj,bjnc->brc', tap_mats, scaled, preferred_element_type=jnp....  34.1 us
    mul x16, other arithmetic, place(): weight_now * got_pixels[slot_pos].astype(jnp.float32)  18.9 us
  transfers between devices with their start and end apart: 7, of which 5 were waited for; matrix products, arithmetic and copies ran while one was open for 8% of the time, Pallas kernels for 0%

commit v1 on v0

v1 whole, which is shorter than its diff:
```python
import functools

import jax
import jax.numpy as jnp
from jax import lax
from jax.experimental import pallas as pl
from jax.experimental.pallas import tpu as pltpu
from jax.sharding import PartitionSpec as P

BLOCK = 512
KHALF = 10
BASES = 3
SIDE = 1024
MARGIN = 128
PGX = 4
SIGMAS = (0.8, 1.6, 3.2)
weight_floor = 0.5

LANES = 128
HALF = BLOCK // 2
PAD = 16
COL_PAD = BLOCK // LANES
TILE_COLS = SIDE // LANES
QUARTER_COLS = 2 * TILE_COLS
COL_TILES = QUARTER_COLS + 2 * COL_PAD
ROW_PAD = HALF + PAD


def band_rows(row_ids):
    offsets = jnp.arange(-KHALF, KHALF + 1).astype(jnp.float32)
    distance = (jnp.arange(BLOCK)[None, :] - row_ids[:, None]).astype(jnp.float32)
    rows = []
    for sigma in SIGMAS:
        total = jnp.sum(jnp.exp(-offsets * offsets / (2.0 * sigma * sigma)))
        taps = jnp.exp(-distance * distance / (2.0 * sigma * sigma)) / total
        rows.append(jnp.where(jnp.abs(distance) <= KHALF, taps, 0.0))
    return jnp.stack(rows).astype(jnp.bfloat16)


def quarter_kernel(geom, sources, has_start, split, *refs):
    stripe, slots = geom
    groups = HALF // stripe
    window = stripe + PAD
    refs = list(refs)
    where_ref = refs.pop(0)
    table_ref = refs.pop(0)
    images = [refs.pop(0) for _ in range(sources)]
    metas = [refs.pop(0) for _ in range(sources)]
    band_ref, wrap_ref = refs.pop(0), refs.pop(0)
    start_ref = refs.pop(0) if has_start else None
    outs = [refs.pop(0) for _ in range(2 if split else 1)]
    canvas, tile_buf, spread, chosen, sems = refs
    quarter, core, row_at, col_at = where_ref[0], where_ref[1], where_ref[2], where_ref[3]
    rows = slots * stripe
    inner = pl.ds(ROW_PAD, rows)

    if has_start:
        canvas[COL_PAD : COL_PAD + QUARTER_COLS, inner, :] = start_ref[...]
    else:
        canvas[COL_PAD : COL_PAD + QUARTER_COLS, inner, :] = jnp.zeros(
            (QUARTER_COLS, rows, LANES), jnp.float32
        )

    for image_ref, meta_ref in zip(images, metas):
        count_all = image_ref.shape[0]

        def corner(i, meta_ref=meta_ref):
            patch = meta_ref[i, 0].astype(jnp.int32)
            row = (patch // PGX) * SIDE + meta_ref[i, 1].astype(jnp.int32) - MARGIN
            col = (patch % PGX) * SIDE + meta_ref[i, 2].astype(jnp.int32) - MARGIN
            return row - (quarter // 2) * SIDE, col - (quarter % 2) * (2 * SIDE)

        def scan(i, count):
            row, col = corner(i)
            hit = (row > -BLOCK) & (row < SIDE) & (col > -BLOCK) & (col < 2 * SIDE)
            chosen[count] = i
            return count + hit.astype(jnp.int32)

        count = lax.fori_loop(0, count_all, scan, jnp.int32(0))

        def fetch(i, image_ref=image_ref):
            slot = lax.rem(i, 2)
            return pltpu.make_async_copy(
                image_ref.at[chosen[i]], tile_buf.at[slot], sems.at[slot]
            )

        @pl.when(count > 0)
        def _():
            fetch(0).start()

        def body(i, carry, meta_ref=meta_ref):
            @pl.when(i + 1 < count)
            def _():
                fetch(i + 1).start()

            fetch(i).wait()
            k = chosen[i]
            row, col = corner(k)
            kernel = meta_ref[k, 3].astype(jnp.int32)
            weight = meta_ref[k, 4]
            col_tile = (col + BLOCK) // LANES
            shift = col + BLOCK - col_tile * LANES
            stripe_at = (row + BLOCK) // stripe
            rho = row + BLOCK - stripe_at * stripe
            stripe_at = stripe_at - BLOCK // stripe
            parted = (stripe_at + core + 2 * BLOCK) % 2 == 0
            slot_row = jnp.where(
                parted, (stripe_at - core) // 2, (stripe_at + 1 - core) // 2
            ) * stripe
            first = jnp.where(parted, 2 * stripe - rho, stripe - rho)
            first_at = pl.multiple_of((first // PAD) * PAD, PAD)
            delta = first - first_at
            pixels = tile_buf[lax.rem(i, 2)]
            lane = lax.broadcasted_iota(jnp.int32, (window, LANES), 1)
            local = lax.broadcasted_iota(jnp.int32, (window, LANES), 0) - delta
            valid = (local >= 0) & (local < stripe)
            split_at = jnp.where(parted, rho, stripe)
            upper = valid & (local < split_at)
            lower = valid & (local >= split_at)
            for g in range(groups):
                for b in range(BASES):
                    down = jnp.dot(
                        wrap_ref[b, g, pl.ds(first_at, window), :],
                        pixels,
                        preferred_element_type=jnp.float32,
                    )
                    spread[:, b * BLOCK : (b + 1) * BLOCK] = (
                        down * table_ref[kernel, b]
                    ).astype(jnp.bfloat16)
                merged = jnp.dot(spread[...], band_ref[...], preferred_element_type=jnp.float32)
                merged = merged.astype(jnp.bfloat16).astype(jnp.float32) * weight
                turned = [
                    pltpu.roll(merged[:, j * LANES : (j + 1) * LANES], shift, 1)
                    for j in range(COL_PAD)
                ]
                base = ROW_PAD + slot_row + g * stripe - delta
                upper_at = jnp.where(parted, base + stripe, base)
                pieces = []
                for j in range(COL_PAD + 1):
                    left = turned[j - 1] if j > 0 else 0.0
                    right = turned[j] if j < COL_PAD else 0.0
                    pieces.append(jnp.where(lane < shift, left, right))
                for j, piece in enumerate(pieces):
                    at = (col_tile + j, pl.ds(upper_at, window), slice(None))
                    canvas[at] = canvas[at] + jnp.where(upper, piece, 0.0)

                @pl.when(parted)
                def _():
                    for j, piece in enumerate(pieces):
                        at = (col_tile + j, pl.ds(base, window), slice(None))
                        canvas[at] = canvas[at] + jnp.where(lower, piece, 0.0)

            return carry

        lax.fori_loop(0, count, body, 0)

    if not split:
        outs[0][...] = canvas[COL_PAD : COL_PAD + QUARTER_COLS, inner, :]
        return

    mixed = slots == 2
    for kind, out in enumerate(outs):
        for i in range(slots):
            slot = row_at ^ (slots - 1 - i)
            side = col_at if kind == 1 else 1 - col_at
            if mixed:
                odd = core == 1
                slot = jnp.where(odd, row_at ^ (1 - kind), slot)
                side = jnp.where(odd, col_at ^ (1 - i), side)
            at = pl.multiple_of(ROW_PAD + slot * stripe, PAD)
            for j in range(TILE_COLS):
                piece = canvas[COL_PAD + side * TILE_COLS + j, pl.ds(at, stripe), :]
                out[i, :, j * LANES : (j + 1) * LANES] = piece.astype(out.dtype)


def make_quarter(geom, where, table, images, metas, bands, start, split):
    stripe, slots = geom
    rows = slots * stripe
    smem = pl.BlockSpec(memory_space=pltpu.SMEM)
    vmem = pl.BlockSpec(memory_space=pltpu.VMEM)
    hbm = pl.BlockSpec(memory_space=pl.ANY)
    sources = len(images)
    has_start = start is not None
    if split:
        out_shape = [
            jax.ShapeDtypeStruct((slots, stripe, SIDE), jnp.bfloat16),
            jax.ShapeDtypeStruct((slots, stripe, SIDE), jnp.float32),
        ]
    else:
        out_shape = [jax.ShapeDtypeStruct((QUARTER_COLS, rows, LANES), jnp.float32)]
    blocks = sum(image.shape[0] for image in images) // 3
    return pl.pallas_call(
        functools.partial(quarter_kernel, geom, sources, has_start, split),
        out_shape=out_shape,
        in_specs=[smem, smem]
        + [hbm] * sources
        + [smem] * sources
        + [vmem, vmem]
        + ([vmem] if has_start else []),
        out_specs=[vmem] * len(out_shape),
        scratch_shapes=[
            pltpu.VMEM((COL_TILES, 2 * ROW_PAD + rows, LANES), jnp.float32),
            pltpu.VMEM((2, BLOCK, BLOCK), jnp.bfloat16),
            pltpu.VMEM((stripe + PAD, BASES * BLOCK), jnp.bfloat16),
            pltpu.SMEM((max(image.shape[0] for image in images) + 1,), jnp.int32),
            pltpu.SemaphoreType.DMA((2,)),
        ],
        compiler_params=pltpu.CompilerParams(vmem_limit_bytes=48 * 1024 * 1024),
        cost_estimate=pl.CostEstimate(
            flops=blocks * 4 * BASES * HALF * BLOCK * BLOCK,
            bytes_accessed=blocks * BLOCK * BLOCK * 2 + 8 * 1024 * 1024,
            transcendentals=0,
        ),
    )(where, table, *images, *metas, *bands, *([start] if has_start else []))


def on_device(
    expo_count, patch_count, images, block_weight, block_patch, block_offset, kernel_index, coef_table
):
    stripe = SIDE // expo_count
    slots = expo_count // 2
    depth = patch_count // 2
    mixed = slots == 2
    geom = (stripe, slots)
    expo, patch = lax.axis_index("expo"), lax.axis_index("patch")
    core, row_at = expo % 2, expo // 2
    col_at, layer = patch % 2, patch // 2
    everyone = [(e, p) for e in range(expo_count) for p in range(patch_count)]

    def swap(value, partner):
        route = []
        for e, p in everyone:
            to_e, to_p = partner(e, p)
            route.append((e * patch_count + p, to_e * patch_count + to_p))
        return lax.ppermute(value, ("expo", "patch"), route)

    meta = jnp.concatenate(
        [
            block_patch.astype(jnp.float32),
            block_offset.astype(jnp.float32),
            kernel_index[:, None].astype(jnp.float32),
            block_weight[:, None].astype(jnp.float32),
        ],
        axis=1,
    )
    twin_meta = swap(meta, lambda e, p: (e ^ 1, p))
    twin_images = swap(images, lambda e, p: (e ^ 1, p))

    band = band_rows(jnp.arange(BLOCK)).reshape(BASES * BLOCK, BLOCK)
    groups = HALF // stripe
    span = 3 * stripe + PAD
    wrap_ids = (
        jnp.arange(groups)[:, None] * 2 * stripe + (jnp.arange(span) % (2 * stripe))[None, :]
    ).reshape(-1)
    wrap = band_rows(wrap_ids).reshape(BASES, groups, span, BLOCK)
    bands = (band, wrap)

    def place(step):
        return jnp.stack([layer ^ step, core, row_at, col_at]).astype(jnp.int32)

    quarter = functools.partial(make_quarter, geom)
    steps = list(range(depth))[::-1]
    early = {}
    for step in steps[:2]:
        early[step] = quarter(place(step), coef_table, [images], [meta], bands, None, False)[0]

    def first_partner(e, p):
        if mixed and e % 2 == 1:
            return e ^ 2, p
        return e, p ^ 1

    arrived = []
    for step in steps:
        if step in early:
            leave, stay = quarter(
                place(step), coef_table, [twin_images], [twin_meta], bands, early[step], True
            )
        else:
            leave, stay = quarter(
                place(step), coef_table, [images, twin_images], [meta, twin_meta], bands, None, True
            )
        got = swap(leave, first_partner)
        total = stay[slots - 1] + got[slots - 1].astype(jnp.float32)
        for hop in range(1, slots):
            part = (stay[slots - 1 - hop] + got[slots - 1 - hop].astype(jnp.float32)).astype(
                jnp.bfloat16
            )

            def second_partner(e, p, hop=hop):
                if mixed and e % 2 == 1:
                    return e, p ^ 1
                return e ^ (2 * hop), p

            total = total + swap(part, second_partner).astype(jnp.float32)
        if step > 0:
            moved = swap(total.astype(jnp.bfloat16), lambda e, p, step=step: (e, p ^ (2 * step)))
            arrived.append(moved)
        else:
            arrived.append(total)

    lists = jnp.concatenate([meta, twin_meta], axis=0)
    reach = 2
    while reach < expo_count:
        lists = jnp.concatenate([lists, swap(lists, lambda e, p, r=reach: (e ^ r, p))], axis=0)
        reach *= 2
    reach = 1
    while reach < patch_count:
        lists = jnp.concatenate([lists, swap(lists, lambda e, p, r=reach: (e, p ^ r))], axis=0)
        reach *= 2
    ids = lists[:, :3].astype(jnp.int32)
    top = (ids[:, 0] // PGX) * SIDE + ids[:, 1] - MARGIN
    left = (ids[:, 0] % PGX) * SIDE + ids[:, 2] - MARGIN
    my_row = (patch // PGX) * SIDE + expo * stripe + jnp.arange(stripe)
    my_col = (patch % PGX) * SIDE + jnp.arange(SIDE)
    row_gap = my_row[:, None] - top[None, :]
    col_gap = my_col[None, :] - left[:, None]
    row_in = jnp.where((row_gap >= 0) & (row_gap < BLOCK), lists[:, 4][None, :], 0.0)
    col_in = (col_gap >= 0) & (col_gap < BLOCK)
    weight_map = jnp.dot(
        row_in.astype(jnp.bfloat16),
        col_in.astype(jnp.bfloat16),
        preferred_element_type=jnp.float32,
    )

    numerator = arrived[-1]
    for value in arrived[:-1]:
        numerator = numerator + value.astype(jnp.float32)
    coadd_map = numerator / jnp.maximum(weight_map, weight_floor)
    return (coadd_map[None], weight_map[None])


def solution(mesh):
    return jax.shard_map(
        functools.partial(on_device, mesh.shape["expo"], mesh.shape["patch"]),
        mesh=mesh,
        in_specs=(
            P(("expo", "patch"), None, None),
            P(("expo", "patch")),
            P(("expo", "patch"), None),
            P(("expo", "patch"), None),
            P(("expo", "patch")),
            P(),
        ),
        out_specs=(P("patch", "expo", None), P("patch", "expo", None)),
        check_vma=False,
    )
```

time: 942 us -> 184 us (0.20)
  the two profiles are of different devices: /device:TPU:0 before, /device:TPU:12 now
where the time goes in v1:
time: 184 us; the launch traced here: 182 us
  Pallas kernels  72.6 us (39%)
  waiting for transfers between devices  61.7 us (34%)
  starting transfers between devices  21 us (11%)
  other arithmetic  21 us (11%)
  local copies, waits for them, and re-layouts  4.37 us (2%)
    pallas_call x6, Pallas kernels, make_quarter(): pl.pallas_call(functools.partial(quarter_kernel, geom, sources, has_start...  72.6 us
    ppermute x17, waiting for transfers between devices, swap(): return lax.ppermute(value, ('expo', 'patch'), route)  61.7 us
    ppermute x17, starting transfers between devices, swap(): return lax.ppermute(value, ('expo', 'patch'), route)  21 us
    convert_element_type x3, other arithmetic, on_device(): total.astype(jnp.bfloat16)  3.94 us
    convert_element_type x4, other arithmetic, on_device(): (stay[slots - 1 - hop] + got[slots - 1 - hop].astype(jnp.float32)).astype...  3.75 us
  transfers between devices with their start and end apart: 17, of which 7 were waited for; matrix products, arithmetic and copies ran while one was open for 12% of the time, Pallas kernels for 34%

profile of v1, /device:TPU:12, one launch (start us, length us, event | category | flops | bytes accessed | tf_op | source)
XLA Modules:
  0.0 182.5 jit_solution(17748996059407148384)
XLA Ops:
  8.3 2.0 %select_convert_fusion.3 = (bf16[1,512,512]{2,1,0:T(8,128)(2,1)S(1)}, bf16[1,512,512]{2,1,0:T(8,128)(2,1)S(1)}) fusion(f32[]{:T(128)} %exponential_reduce_fusion, f32[]{:T(128)} %exponential_reduce_fusion.1), kind=kLoop, calls=%fused_computation.29 | loop fusion | flops 3670016 | bytes 1048584 | tf_op jit(solution)/shard_map/convert.9
  10.5 3.1 %fusion.11 = (bf16[1,1,784,512]{3,2,1,0:T(8,128)(2,1)S(1)}, bf16[1,1,784,512]{3,2,1,0:T(8,128)(2,1)S(1)}, bf16[1,1,784,512]{3,2,1,0:T(8,128)(2,1)S(1)}) fusion(f32[]{:T(128)} %exponential_reduce_fusion.2, s32[784]{0:T(1024)S(1)} %add_select_fusion, f32[]{:T(128)} %exponential_reduce_fusion, f32[]{:T(128)} %exponential_reduce_fusion.1), kind=kLoop, calls=%fused_computation.34 | loop fusion | flops 7225344 | bytes 2411596 | tf_op jit(solution)/shard_map/stack | solution.py:37
  13.9 12.6 %shard_map.80.refs_6_ = f32[16,512,128]{2,1,0:T(8,128)} custom-call(s32[4]{0:T(128)S(1)} %get-tuple-element.26.refs_0_, f32[189,3]{1,0:T(8,128)S(1)} %copy.32.refs_1_, bf16[12,512,512]{2,1,0:T(8,128)(2,1)} %refs_2_.7, f32[12,5]{1,0:T(8,128)S(1)} %pad_maximum_fusion.2.refs_4_.refs_3_, bf16[1536,512]{1,0:T(8,128)(2,1)S(1)} %bitcast.54, ...), custom_call_target="tpu_custom_call" | custom-call | flops 3221225472 | bytes 10485760 | tf_op jit(solution)/shard_map/pallas_call | solution.py:192
  26.9 3.5 %collective-permute-done.13 = f32[24,5]{0,1:T(8,128)S(1)} collective-permute-done((f32[24,5]{0,1:T(8,128)S(1)}, f32[24,5]{0,1:T(8,128)S(1)}, u32[]{:S(2)}, u32[]{:S(2)}) %collective-permute-start.13) | collective-permute-done | bytes 512 | tf_op jit(solution)/shard_map/ppermute | solution.py:235
  30.5 1.5 collective-permute-start.14
  31.9 1.4 copy-done.2
  33.4 13.9 %shard_map.78.refs_6_ = f32[16,512,128]{2,1,0:T(8,128)} custom-call(s32[4]{0:T(128)S(1)} %get-tuple-element.25.refs_0_, f32[189,3]{1,0:T(8,128)S(1)} %copy.32.refs_1_, bf16[12,512,512]{2,1,0:T(8,128)(2,1)} %refs_2_.7, f32[12,5]{1,0:T(8,128)S(1)} %pad_maximum_fusion.2.refs_4_.refs_3_, bf16[1536,512]{1,0:T(8,128)(2,1)S(1)} %bitcast.55, ...), custom_call_target="tpu_custom_call" | custom-call | flops 3221225472 | bytes 10485760 | tf_op jit(solution)/shard_map/pallas_call | solution.py:192
  47.4 3.6 %collective-permute-done.15 = f32[96,5]{0,1:T(8,128)S(1)} collective-permute-done((f32[96,5]{0,1:T(8,128)S(1)}, f32[96,5]{0,1:T(8,128)S(1)}, u32[]{:S(2)}, u32[]{:S(2)}) %collective-permute-start.15) | collective-permute-done | bytes 1952 | tf_op jit(solution)/shard_map/ppermute | solution.py:235
  51.1 4.5 %collective-permute-done.16 = f32[192,5]{0,1:T(8,128)S(1)} collective-permute-done((f32[192,5]{0,1:T(8,128)S(1)}, f32[192,5]{0,1:T(8,128)S(1)}, u32[]{:S(2)}, u32[]{:S(2)}) %collective-permute-start.16) | collective-permute-done | bytes 3872 | tf_op jit(solution)/shard_map/ppermute | solution.py:235
  55.7 1.4 copy-done.3
  57.1 10.9 %shard_map.82 = (bf16[2,256,1024]{2,1,0:T(8,128)(2,1)S(1)}, f32[2,256,1024]{2,1,0:T(8,128)S(1)}) custom-call(s32[4]{0:T(128)S(1)} %get-tuple-element.27.refs_0_, f32[189,3]{1,0:T(8,128)S(1)} %copy.32.refs_1_, bf16[12,512,512]{2,1,0:T(8,128)(2,1)} %refs_2_.7, bf16[12,512,512]{2,1,0:T(8,128)(2,1)} %collective-permute-done.refs_3_.refs_2_, ...), custom_call_target="tpu_custom_call" | custom-call | flops 6442450944 | bytes 12582912 | tf_op jit(solution)/shard_map/pallas_call | solution.py:192
  68.1 1.8 collective-permute-start.10
  69.8 8.9 %shard_map.81 = (bf16[2,256,1024]{2,1,0:T(8,128)(2,1)S(1)}, f32[2,256,1024]{2,1,0:T(8,128)S(1)}) custom-call(s32[4]{0:T(128)S(1)} %get-tuple-element.26.refs_0_, f32[189,3]{1,0:T(8,128)S(1)} %copy.32.refs_1_, bf16[12,512,512]{2,1,0:T(8,128)(2,1)} %collective-permute-done.refs_3_.refs_2_, f32[12,5]{1,0:T(8,128)S(1)} %collective-permute-done.1.refs_5_.refs_3_, ...), custom_call_target="tpu_custom_call" | custom-call | flops 3221225472 | bytes 10485760 | tf_op jit(solution)/shard_map/pallas_call | solution.py:192
  79.1 11.6 %shard_map.79 = (bf16[2,256,1024]{2,1,0:T(8,128)(2,1)S(1)}, f32[2,256,1024]{2,1,0:T(8,128)S(1)}) custom-call(s32[4]{0:T(128)S(1)} %get-tuple-element.25.refs_0_, f32[189,3]{1,0:T(8,128)S(1)} %copy.32.refs_1_, bf16[12,512,512]{2,1,0:T(8,128)(2,1)} %collective-permute-done.refs_3_.refs_2_, f32[12,5]{1,0:T(8,128)S(1)} %collective-permute-done.1.refs_5_.refs_3_, ...), custom_call_target="tpu_custom_call" | custom-call | flops 3221225472 | bytes 10485760 | tf_op jit(solution)/shard_map/pallas_call | solution.py:192
  90.7 3.0 %collective-permute-start.4 = (bf16[2,256,1024]{2,1,0:T(8,128)(2,1)S(1)}, bf16[2,256,1024]{2,1,0:T(8,128)(2,1)}, u32[]{:S(2)}, u32[]{:S(2)}) collective-permute-start(bf16[2,256,1024]{2,1,0:T(8,128)(2,1)S(1)} %get-tuple-element.13), channel_id=1, source_target_pairs={{0,1},{1,0},{2,3},{3,2},{4,5},{5,4},{6,7},{7,6},{8,24},{9,25},{10,... | collective-permute-start | bytes 3145736 | tf_op jit(solution)/shard_map/ppermute | solution.py:235
  93.7 14.6 %shard_map.77 = (bf16[2,256,1024]{2,1,0:T(8,128)(2,1)S(1)}, f32[2,256,1024]{2,1,0:T(8,128)S(1)}) custom-call(s32[4]{0:T(128)S(1)} %get-tuple-element.24.refs_0_, f32[189,3]{1,0:T(8,128)S(1)} %copy.32.refs_1_, bf16[12,512,512]{2,1,0:T(8,128)(2,1)} %refs_2_.7, bf16[12,512,512]{2,1,0:T(8,128)(2,1)} %collective-permute-done.refs_3_.refs_2_, ...), custom_call_target="tpu_custom_call" | custom-call | flops 6442450944 | bytes 12582912 | tf_op jit(solution)/shard_map/pallas_call | solution.py:192
  111.4 1.7 collective-permute-start.8
  114.7 19.7 %collective-permute-done.2 = bf16[2,256,1024]{2,1,0:T(8,128)(2,1)S(1)} collective-permute-done((bf16[2,256,1024]{2,1,0:T(8,128)(2,1)S(1)}, bf16[2,256,1024]{2,1,0:T(8,128)(2,1)S(1)}, u32[]{:S(2)}, u32[]{:S(2)}) %collective-permute-start.2) | collective-permute-done | bytes 1048608 | tf_op jit(solution)/shard_map/ppermute | solution.py:235
  136.0 4.9 %collective-permute-start.12 = (bf16[256,1024]{1,0:T(8,128)(2,1)S(1)}, bf16[256,1024]{1,0:T(8,128)(2,1)S(1)}, u32[]{:S(2)}, u32[]{:S(2)}) collective-permute-start(bf16[256,1024]{1,0:T(8,128)(2,1)S(1)} %fusion.3), channel_id=1, source_target_pairs={{0,2},{1,3},{2,0},{3,1},{4,6},{5,7},{6,4},{7,5},{8,10},{9,11},{10,... | collective-permute-start | bytes 1572872 | tf_op jit(solution)/shard_map/ppermute | solution.py:235
  142.2 5.5 %collective-permute-start.9 = (bf16[256,1024]{1,0:T(8,128)(2,1)S(1)}, bf16[256,1024]{1,0:T(8,128)(2,1)S(1)}, u32[]{:S(2)}, u32[]{:S(2)}) collective-permute-start(bf16[256,1024]{1,0:T(8,128)(2,1)S(1)} %fusion.4), channel_id=1, source_target_pairs={{0,4},{1,5},{2,6},{3,7},{4,0},{5,1},{6,2},{7,3},{8,12},{9,13},{10,... | collective-permute-start | bytes 1572872 | tf_op jit(solution)/shard_map/ppermute | solution.py:235
  150.5 5.3 %collective-permute-done.12 = bf16[256,1024]{1,0:T(8,128)(2,1)S(1)} collective-permute-done((bf16[256,1024]{1,0:T(8,128)(2,1)S(1)}, bf16[256,1024]{1,0:T(8,128)(2,1)S(1)}, u32[]{:S(2)}, u32[]{:S(2)}) %collective-permute-start.12) | collective-permute-done | bytes 524320 | tf_op jit(solution)/shard_map/ppermute | solution.py:235
  155.8 17.9 %collective-permute-done.9 = bf16[256,1024]{1,0:T(8,128)(2,1)S(1)} collective-permute-done((bf16[256,1024]{1,0:T(8,128)(2,1)S(1)}, bf16[256,1024]{1,0:T(8,128)(2,1)S(1)}, u32[]{:S(2)}, u32[]{:S(2)}) %collective-permute-start.9) | collective-permute-done | bytes 524320 | tf_op jit(solution)/shard_map/ppermute | solution.py:235
  173.6 7.2 %collective-permute-done.6 = bf16[256,1024]{1,0:T(8,128)(2,1)S(1)} collective-permute-done((bf16[256,1024]{1,0:T(8,128)(2,1)S(1)}, bf16[256,1024]{1,0:T(8,128)(2,1)S(1)}, u32[]{:S(2)}, u32[]{:S(2)}) %collective-permute-start.6) | collective-permute-done | bytes 524320 | tf_op jit(solution)/shard_map/ppermute | solution.py:235
  180.9 1.6 fusion.10
  (71 shorter events, 19.4 us)
Async XLA Ops:
  0.6 55.1 %collective-permute-start = (bf16[12,512,512]{2,1,0:T(8,128)(2,1)}, bf16[12,512,512]{2,1,0:T(8,128)(2,1)}, u32[]{:S(2)}, u32[]{:S(2)}) collective-permute-start(bf16[12,512,512]{2,1,0:T(8,128)(2,1)} %refs_2_.7), channel_id=1, source_target_pairs={{0,8},{1,9},{2,10},{3,11},{4,12},{5,13},{6,14},{7,15},{8,0},{9,1},... | collective-permute-start | bytes 18874376 | tf_op jit(solution)/shard_map/ppermute | solution.py:235
  3.8 22.8 %collective-permute-start.1 = (f32[12,5]{1,0:T(8,128)S(1)}, f32[12,5]{1,0:T(8,128)S(1)}, u32[]{:S(2)}, u32[]{:S(2)}) collective-permute-start(f32[12,5]{1,0:T(8,128)S(1)} %pad_maximum_fusion.2.refs_4_.refs_3_), channel_id=1, source_target_pairs={{0,8},{1,9},{2,10},{3,11},{4,12},{5,13},{6,14},{7,15},{8,0},{9,1},... | collective-permute-start | bytes 728 | tf_op jit(solution)/shard_map/ppermute | solution.py:235
  10.5 3.4 %copy-start.1 = (bf16[3,512,512]{2,1,0:T(8,128)(2,1)}, bf16[3,512,512]{2,1,0:T(8,128)(2,1)S(1)}, u32[]{:S(2)}) copy-start(bf16[3,512,512]{2,1,0:T(8,128)(2,1)S(1)} %pad_maximum_fusion.1) | copy-start | bytes 4718596
  13.9 18.1 %copy-start = (bf16[3,1,784,512]{3,2,1,0:T(8,128)(2,1)}, bf16[3,1,784,512]{3,2,1,0:T(8,128)(2,1)S(1)}, u32[]{:S(2)}) copy-start(bf16[3,1,784,512]{3,2,1,0:T(8,128)(2,1)S(1)} %pad_maximum_fusion.refs_7_.refs_5_) | copy-start | bytes 7225348
  26.8 3.6 %collective-permute-start.13 = (f32[24,5]{0,1:T(8,128)S(1)}, f32[24,5]{0,1:T(8,128)S(1)}, u32[]{:S(2)}, u32[]{:S(2)}) collective-permute-start(f32[24,5]{0,1:T(8,128)S(1)} %pad_maximum_fusion.3), channel_id=1, source_target_pairs={{0,16},{1,17},{2,18},{3,19},{4,20},{5,21},{6,22},{7,23},{8,24},{9,... | collective-permute-start | bytes 1448 | tf_op jit(solution)/shard_map/ppermute | solution.py:235
  30.5 16.8 %collective-permute-start.14 = (f32[48,5]{0,1:T(8,128)S(1)}, f32[48,5]{0,1:T(8,128)S(1)}, u32[]{:S(2)}, u32[]{:S(2)}) collective-permute-start(f32[48,5]{0,1:T(8,128)S(1)} %pad_maximum_fusion.4), channel_id=1, source_target_pairs={{0,1},{1,0},{2,3},{3,2},{4,5},{5,4},{6,7},{7,6},{8,9},{9,8},{10,11... | collective-permute-start | bytes 2888 | tf_op jit(solution)/shard_map/ppermute | solution.py:235
  31.9 1.4 copy-start.2
  47.4 3.6 %collective-permute-start.15 = (f32[96,5]{0,1:T(8,128)S(1)}, f32[96,5]{0,1:T(8,128)S(1)}, u32[]{:S(2)}, u32[]{:S(2)}) collective-permute-start(f32[96,5]{0,1:T(8,128)S(1)} %pad_maximum_fusion.5), channel_id=1, source_target_pairs={{0,2},{1,3},{2,0},{3,1},{4,6},{5,7},{6,4},{7,5},{8,10},{9,11},{10,... | collective-permute-start | bytes 5768 | tf_op jit(solution)/shard_map/ppermute | solution.py:235
  51.1 4.6 %collective-permute-start.16 = (f32[192,5]{0,1:T(8,128)S(1)}, f32[192,5]{0,1:T(8,128)S(1)}, u32[]{:S(2)}, u32[]{:S(2)}) collective-permute-start(f32[192,5]{0,1:T(8,128)S(1)} %concatenate.34), channel_id=1, source_target_pairs={{0,4},{1,5},{2,6},{3,7},{4,0},{5,1},{6,2},{7,3},{8,12},{9,13},{10,... | collective-permute-start | bytes 11528 | tf_op jit(solution)/shard_map/ppermute | solution.py:235
  55.7 1.4 copy-start.3
  57.1 12.7 %copy-start.4 = (bf16[3,512,512]{2,1,0:T(8,128)(2,1)S(1)}, bf16[3,512,512]{2,1,0:T(8,128)(2,1)}, u32[]{:S(2)}) copy-start(bf16[3,512,512]{2,1,0:T(8,128)(2,1)} %copy-done.1) | copy-start | bytes 4718596
  68.1 40.4 %collective-permute-start.10 = (bf16[2,256,1024]{2,1,0:T(8,128)(2,1)S(1)}, bf16[2,256,1024]{2,1,0:T(8,128)(2,1)}, u32[]{:S(2)}, u32[]{:S(2)}) collective-permute-start(bf16[2,256,1024]{2,1,0:T(8,128)(2,1)S(1)} %get-tuple-element.17), channel_id=1, source_target_pairs={{0,1},{1,0},{2,3},{3,2},{4,5},{5,4},{6,7},{7,6},{8,24},{9,25},{10,... | collective-permute-start | bytes 3145736 | tf_op jit(solution)/shard_map/ppermute | solution.py:235
  78.7 31.4 %collective-permute-start.7 = (bf16[2,256,1024]{2,1,0:T(8,128)(2,1)S(1)}, bf16[2,256,1024]{2,1,0:T(8,128)(2,1)}, u32[]{:S(2)}, u32[]{:S(2)}) collective-permute-start(bf16[2,256,1024]{2,1,0:T(8,128)(2,1)S(1)} %get-tuple-element.15), channel_id=1, source_target_pairs={{0,1},{1,0},{2,3},{3,2},{4,5},{5,4},{6,7},{7,6},{8,24},{9,25},{10,... | collective-permute-start | bytes 3145736 | tf_op jit(solution)/shard_map/ppermute | solution.py:235
  90.7 22.3 %collective-permute-start.4 = (bf16[2,256,1024]{2,1,0:T(8,128)(2,1)S(1)}, bf16[2,256,1024]{2,1,0:T(8,128)(2,1)}, u32[]{:S(2)}, u32[]{:S(2)}) collective-permute-start(bf16[2,256,1024]{2,1,0:T(8,128)(2,1)S(1)} %get-tuple-element.13), channel_id=1, source_target_pairs={{0,1},{1,0},{2,3},{3,2},{4,5},{5,4},{6,7},{7,6},{8,24},{9,25},{10,... | collective-permute-start | bytes 3145736 | tf_op jit(solution)/shard_map/ppermute | solution.py:235
  108.3 26.2 %collective-permute-start.2 = (bf16[2,256,1024]{2,1,0:T(8,128)(2,1)S(1)}, bf16[2,256,1024]{2,1,0:T(8,128)(2,1)S(1)}, u32[]{:S(2)}, u32[]{:S(2)}) collective-permute-start(bf16[2,256,1024]{2,1,0:T(8,128)(2,1)S(1)} %get-tuple-element.11), channel_id=1, source_target_pairs={{0,1},{1,0},{2,3},{3,2},{4,5},{5,4},{6,7},{7,6},{8,24},{9,25},{10,... | collective-permute-start | bytes 3145736 | tf_op jit(solution)/shard_map/ppermute | solution.py:235
  109.7 25.0 %collective-permute-start.11 = (bf16[256,1024]{1,0:T(8,128)(2,1)S(1)}, bf16[256,1024]{1,0:T(8,128)(2,1)S(1)}, u32[]{:S(2)}, u32[]{:S(2)}) collective-permute-start(bf16[256,1024]{1,0:T(8,128)(2,1)S(1)} %fusion.21), channel_id=1, source_target_pairs={{0,16},{1,17},{2,18},{3,19},{4,20},{5,21},{6,22},{7,23},{8,9},{9,8... | collective-permute-start | bytes 1572872 | tf_op jit(solution)/shard_map/ppermute | solution.py:235
  111.4 29.5 %collective-permute-start.8 = (bf16[256,1024]{1,0:T(8,128)(2,1)S(1)}, bf16[256,1024]{1,0:T(8,128)(2,1)S(1)}, u32[]{:S(2)}, u32[]{:S(2)}) collective-permute-start(bf16[256,1024]{1,0:T(8,128)(2,1)S(1)} %fusion.20), channel_id=1, source_target_pairs={{0,16},{1,17},{2,18},{3,19},{4,20},{5,21},{6,22},{7,23},{8,9},{9,8... | collective-permute-start | bytes 1572872 | tf_op jit(solution)/shard_map/ppermute | solution.py:235
  114.3 33.4 %collective-permute-start.5 = (bf16[256,1024]{1,0:T(8,128)(2,1)S(1)}, bf16[256,1024]{1,0:T(8,128)(2,1)S(1)}, u32[]{:S(2)}, u32[]{:S(2)}) collective-permute-start(bf16[256,1024]{1,0:T(8,128)(2,1)S(1)} %fusion.19), channel_id=1, source_target_pairs={{0,16},{1,17},{2,18},{3,19},{4,20},{5,21},{6,22},{7,23},{8,9},{9,8... | collective-permute-start | bytes 1572872 | tf_op jit(solution)/shard_map/ppermute | solution.py:235
  134.6 15.9 %collective-permute-start.3 = (bf16[256,1024]{1,0:T(8,128)(2,1)S(1)}, bf16[256,1024]{1,0:T(8,128)(2,1)S(1)}, u32[]{:S(2)}, u32[]{:S(2)}) collective-permute-start(bf16[256,1024]{1,0:T(8,128)(2,1)S(1)} %fusion.18), channel_id=1, source_target_pairs={{0,16},{1,17},{2,18},{3,19},{4,20},{5,21},{6,22},{7,23},{8,9},{9,8... | collective-permute-start | bytes 1572872 | tf_op jit(solution)/shard_map/ppermute | solution.py:235
  136.0 19.8 %collective-permute-start.12 = (bf16[256,1024]{1,0:T(8,128)(2,1)S(1)}, bf16[256,1024]{1,0:T(8,128)(2,1)S(1)}, u32[]{:S(2)}, u32[]{:S(2)}) collective-permute-start(bf16[256,1024]{1,0:T(8,128)(2,1)S(1)} %fusion.3), channel_id=1, source_target_pairs={{0,2},{1,3},{2,0},{3,1},{4,6},{5,7},{6,4},{7,5},{8,10},{9,11},{10,... | collective-permute-start | bytes 1572872 | tf_op jit(solution)/shard_map/ppermute | solution.py:235
  142.2 31.4 %collective-permute-start.9 = (bf16[256,1024]{1,0:T(8,128)(2,1)S(1)}, bf16[256,1024]{1,0:T(8,128)(2,1)S(1)}, u32[]{:S(2)}, u32[]{:S(2)}) collective-permute-start(bf16[256,1024]{1,0:T(8,128)(2,1)S(1)} %fusion.4), channel_id=1, source_target_pairs={{0,4},{1,5},{2,6},{3,7},{4,0},{5,1},{6,2},{7,3},{8,12},{9,13},{10,... | collective-permute-start | bytes 1572872 | tf_op jit(solution)/shard_map/ppermute | solution.py:235
  149.1 31.8 %collective-permute-start.6 = (bf16[256,1024]{1,0:T(8,128)(2,1)S(1)}, bf16[256,1024]{1,0:T(8,128)(2,1)S(1)}, u32[]{:S(2)}, u32[]{:S(2)}) collective-permute-start(bf16[256,1024]{1,0:T(8,128)(2,1)S(1)} %fusion.5), channel_id=1, source_target_pairs={{0,6},{1,7},{2,4},{3,5},{4,2},{5,3},{6,0},{7,1},{8,14},{9,15},{10,... | collective-permute-start | bytes 1572872 | tf_op jit(solution)/shard_map/ppermute | solution.py:235
  150.5 32.0 %copy-start.5 = (f32[256,1024]{1,0:T(8,128)}, f32[256,1024]{1,0:T(8,128)S(1)}, u32[]{:S(2)}) copy-start(f32[256,1024]{1,0:T(8,128)S(1)} %fusion.1) | copy-start | bytes 3145732

commit v2 on v1

v2 whole, which is shorter than its diff:
```python
import functools

import jax
import jax.numpy as jnp
import ml_dtypes
import numpy as np
from jax import lax
from jax.experimental import pallas as pl
from jax.experimental.pallas import tpu as pltpu
from jax.sharding import PartitionSpec as P

BLOCK = 512
KHALF = 10
BASES = 3
SIDE = 1024
MARGIN = 128
PGX = 4
PGX_BITS = 2
SIGMAS = (0.8, 1.6, 3.2)
weight_floor = 0.5

LANES = 128
HALF = BLOCK // 2
PAD = 16
BATCH = 4
FIELD_ROWS = 16
COL_PAD = BLOCK // LANES
TILE_COLS = SIDE // LANES
QUARTER_COLS = 2 * TILE_COLS
COL_TILES = QUARTER_COLS + 2 * COL_PAD


def taps_at(basis, distance):
    offsets = np.arange(-KHALF, KHALF + 1).astype(np.float32)
    taps = []
    for sigma in SIGMAS:
        profile = np.exp(-offsets * offsets / np.float32(2.0 * sigma * sigma))
        taps.append(profile / np.sum(profile, dtype=np.float32))
    taps = np.stack(taps).astype(ml_dtypes.bfloat16)
    inside = np.abs(distance) <= KHALF
    found = taps[basis, np.where(inside, distance + KHALF, 0)]
    return np.where(inside, found, np.zeros((), ml_dtypes.bfloat16))


def geometry(stripe):
    groups = HALF // stripe
    gap = PAD if groups == 1 else 2 * PAD
    window = stripe + PAD + gap
    parts = 2 if groups == 1 else 1
    group_rows = PAD + 2 * stripe + gap + stripe + 2 * PAD
    row_pad = HALF + PAD + gap
    return groups, gap, window, parts, group_rows, row_pad


def make_bands(stripe):
    _, _, window, parts, _, _ = geometry(stripe)
    height = window // parts
    row, col = np.indices((BASES * height, height + 2 * PAD))
    down = taps_at(row // height, col - row % height - PAD)
    row, col = np.indices((BASES * BLOCK, 6 * LANES))
    side = col // (2 * LANES)
    col = col - side * LANES
    mine = (col >= 192).astype(np.int32) + (col >= 320) == side
    across = np.where(mine, taps_at(row // BLOCK, col - row % BLOCK), 0)
    return jnp.asarray(down, jnp.bfloat16), jnp.asarray(across, jnp.bfloat16)


def quarter_kernel(geom, step, sources, has_start, split, waits, has_fields, *refs):
    stripe, slots = geom
    groups, gap, window, parts, group_rows, row_pad = geometry(stripe)
    height = window // parts
    refs = list(refs)
    table_ref, where_refs, weight_ref = refs.pop(0), [refs.pop(0) for _ in range(3)], refs.pop(0)
    patch_ref, offset_ref, index_ref = where_refs
    images = [refs.pop(0) for _ in range(sources)]
    band_hbm = [refs.pop(0), refs.pop(0)]
    start_ref = refs.pop(0) if has_start else None
    refs = refs[waits:]
    fields_ref = refs.pop(0) if has_fields else None
    outs = [refs.pop(0) for _ in range(2 if split else 1)]
    token_ref = refs.pop(0)
    canvas, tile_buf, spread, down_ref, band_ref, chosen, sems, side_sems = refs[:8]
    stages = refs[8:]
    expo, place_at = lax.axis_index("expo"), lax.axis_index("patch")
    core, row_at, col_at, quarter = expo & 1, expo >> 1, place_at & 1, (place_at >> 1) ^ step
    rows = slots * stripe
    per_source = images[0].shape[0]

    def canvas_copies(other, out):
        copies = []
        for n in range(4):
            cols = QUARTER_COLS // 4
            mine = canvas.at[pl.ds(COL_PAD + n * cols, cols), pl.ds(row_pad, rows), :]
            far = other.at[pl.ds(n * cols, cols)]
            ends = (mine, far) if out else (far, mine)
            copies.append(pltpu.make_async_copy(*ends, side_sems.at[2 + n]))
        return copies


    loads = [
        pltpu.make_async_copy(band_hbm[0], down_ref, side_sems.at[0]),
        pltpu.make_async_copy(band_hbm[1], band_ref, side_sems.at[1]),
    ]
    if has_start:
        loads += canvas_copies(start_ref, False)
    if has_fields:
        loads.append(
            pltpu.make_async_copy(
                fields_ref, outs[0].at[pl.ds(rows, FIELD_ROWS)], side_sems.at[6]
            )
        )
    token_ref[0, 0] = 0.0
    for load in loads:
        load.start()

    stripe_bits = stripe.bit_length() - 1
    row_shift = BLOCK - MARGIN - (quarter >> 1) * SIDE
    col_shift = BLOCK - MARGIN - (quarter & 1) * (2 * SIDE)

    def corner(i):
        patch = patch_ref[0, i]
        row = (patch >> PGX_BITS) * SIDE + offset_ref[0, i] + row_shift
        col = (patch & (PGX - 1)) * SIDE + offset_ref[1, i] + col_shift
        return (row >> stripe_bits) - BLOCK // stripe, row & (stripe - 1), col

    def scan(i, count):
        stripe_at, rho, col = corner(i)
        lowest = jnp.maximum(stripe_at, 0)
        lowest = lowest + ((lowest + core) & 1)
        highest = stripe_at + BLOCK // stripe - (rho == 0).astype(jnp.int32)
        hit = (lowest <= jnp.minimum(highest, 2 * slots - 1)) & (col > 0) & (col < BLOCK + 2 * SIDE)
        chosen[count] = i
        return count + hit.astype(jnp.int32)

    count = lax.fori_loop(0, sources * per_source, scan, jnp.int32(0))

    def pieces_of(g):
        top, base = 2 * stripe * g, group_rows * g
        early = PAD if g > 0 else 0
        late = PAD if g < groups - 1 else 0
        again = base + PAD + 2 * stripe + gap
        return [
            (top - early, early + 2 * stripe + late, base + PAD - early),
            (top - early, early + stripe + PAD, again - early),
        ]

    def fetch(i, slot, act):
        k = chosen[i]
        for n, image_ref in enumerate(images):

            @pl.when((k >= n * per_source) & (k < (n + 1) * per_source))
            def _():
                for g in range(groups):
                    for c, (top, size, to) in enumerate(pieces_of(g)):
                        act(
                            pltpu.make_async_copy(
                                image_ref.at[k - n * per_source, pl.ds(top, size), :],
                                tile_buf.at[slot, pl.ds(to, size), :],
                                sems.at[slot, 2 * g + c],
                            )
                        )

    def start(i, slot):
        @pl.when(i < count)
        def _():
            fetch(i, slot, lambda copy: copy.start())

    for slot in range(4):
        for g in range(groups):
            base = group_rows * g
            again = base + PAD + 2 * stripe + gap
            for top, bottom in (
                (base, base + PAD),
                (base + PAD + 2 * stripe, again),
                (again + stripe + PAD, base + group_rows),
            ):
                tile_buf[slot, top:bottom, :] = jnp.zeros((bottom - top, BLOCK), tile_buf.dtype)
    start(0, 0)
    start(1, 1)
    if not has_start:
        canvas[COL_PAD : COL_PAD + QUARTER_COLS, row_pad : row_pad + rows, :] = jnp.zeros(
            (QUARTER_COLS, rows, LANES), jnp.float32
        )
    for load in loads:
        load.wait()

    def place(i):
        k = chosen[i]
        stripe_at, rho, col = corner(k)
        col_tile = col >> 7
        shift = col & (LANES - 1)
        parted = ((stripe_at + core) & 1) == 0
        slot_row = stripe * ((stripe_at + 1 - core) >> 1)
        first = jnp.where(parted, 2 * stripe - rho, stripe - rho)
        first_at = pl.multiple_of((first >> 4) << 4, PAD)
        delta = first - first_at
        return k, rho, col_tile, shift, parted, slot_row, first_at, delta

    def down_pass(info, slot, half):
        k, first_at = info[0], info[6]
        kernel = index_ref[k]
        scales = [table_ref[b, kernel] * weight_ref[k] for b in range(BASES)]
        for g in range(groups):
            for part in range(parts):
                at = pl.multiple_of(g * group_rows + first_at + part * height, PAD)
                result = jnp.dot(
                    down_ref[...],
                    tile_buf[slot, pl.ds(at, height + 2 * PAD), :],
                    preferred_element_type=jnp.float32,
                )
                for b in range(BASES):
                    spread[
                        half * groups + g,
                        part * height : (part + 1) * height,
                        b * BLOCK : (b + 1) * BLOCK,
                    ] = (result[b * height : (b + 1) * height] * scales[b]).astype(jnp.bfloat16)

    def across_pass(info, half):
        k, rho, col_tile, shift, parted, slot_row, first_at, delta = info
        lane = lax.broadcasted_iota(jnp.int32, (window, LANES), 1)
        local = lax.broadcasted_iota(jnp.int32, (window, LANES), 0) - delta
        split_at = jnp.where(parted, rho, stripe)
        last = jnp.where(parted, stripe + gap, stripe)
        valid = (local >= 0) & (
            (local < split_at) | ((local >= rho + gap) & (local < last))
        )
        for g in range(groups):
            wide = []
            for side in range(3):
                acc = None
                for b in range(BASES):
                    lo = LANES * side
                    term = jnp.dot(
                        spread[half * groups + g, :, b * BLOCK + lo : b * BLOCK + lo + 256],
                        band_ref[b * BLOCK + lo : b * BLOCK + lo + 256, 256 * side : 256 * side + 256],
                        preferred_element_type=jnp.float32,
                    )
                    acc = term if acc is None else acc + term
                wide.append(acc)
            merged = jnp.concatenate(
                [
                    wide[0][:, :LANES],
                    wide[0][:, LANES:] + wide[1][:, :LANES],
                    wide[1][:, LANES:] + wide[2][:, :LANES],
                    wide[2][:, LANES:],
                ],
                axis=1,
            )
            turned = [
                pltpu.roll(merged[:, j * LANES : (j + 1) * LANES], shift, 1)
                for j in range(COL_PAD)
            ]
            base = row_pad + slot_row + g * stripe - delta
            upper_at = jnp.where(parted, base + stripe, base)
            lower_at = jnp.where(parted, base - gap, base)
            pieces = []
            for j in range(COL_PAD + 1):
                left = turned[j - 1] if j > 0 else 0.0
                right = turned[j] if j < COL_PAD else 0.0
                pieces.append(jnp.where(valid, jnp.where(lane < shift, left, right), 0.0))
            for top in range(0, window, 8 * BATCH):
                spots, sums = [], []
                for row in range(top, min(top + 8 * BATCH, window), 8):
                    at = row + jnp.where(row < split_at + delta, upper_at, lower_at)
                    for j in range(COL_PAD + 1):
                        spot = (col_tile + j, pl.ds(at, 8), slice(None))
                        spots.append(spot)
                        sums.append(canvas[spot] + pieces[j][row : row + 8])
                for spot, value in zip(spots, sums):
                    canvas[spot] = value

    def pair(n, carry):
        slot = 2 * (n & 1)
        start(2 * n + 2, 2 - slot)
        start(2 * n + 3, 3 - slot)
        infos = [place(2 * n), place(2 * n + 1)]
        for half in range(2):
            fetch(2 * n + half, slot + half, lambda copy: copy.wait())
        for half in range(2):
            down_pass(infos[half], slot + half, half)
        for half in range(2):
            across_pass(infos[half], half)
        return carry

    lax.fori_loop(0, count >> 1, pair, 0)

    @pl.when((count & 1) == 1)
    def _():
        last = count - 1
        slot = last & 3
        info = place(last)
        fetch(last, slot, lambda copy: copy.wait())
        down_pass(info, slot, 0)
        across_pass(info, 0)

    if not split:
        stores = canvas_copies(outs[0], True)
        for store in stores:
            store.start()
        for store in stores:
            store.wait()
        return

    mixed = slots == 2
    stores = []
    for kind, out in enumerate(outs):
        for i in range(slots):
            slot = row_at ^ (slots - 1 - i)
            side = col_at if kind == 1 else 1 - col_at
            if mixed:
                odd = core == 1
                slot = jnp.where(odd, row_at ^ (1 - kind), slot)
                side = jnp.where(odd, col_at ^ (1 - i), side)
            at = pl.multiple_of(row_pad + slot * stripe, PAD)
            for j in range(TILE_COLS):
                piece = canvas[COL_PAD + side * TILE_COLS + j, pl.ds(at, stripe), :]
                stages[kind][i, :, j * LANES : (j + 1) * LANES] = piece.astype(out.dtype)
            place_out = out.at[pl.ds(i * stripe, stripe)]
            store = pltpu.make_async_copy(
                stages[kind].at[i], place_out, side_sems.at[kind * slots + i]
            )
            store.start()
            stores.append(store)
    for store in stores:
        store.wait()


def make_quarter(geom, step, table, images, lists, bands, start=None, split=True, after=(), fields=None):
    stripe, slots = geom
    groups, gap, window, parts, group_rows, row_pad = geometry(stripe)
    rows = slots * stripe
    smem = pl.BlockSpec(memory_space=pltpu.SMEM)
    hbm = pl.BlockSpec(memory_space=pl.ANY)
    sources = len(images)
    has_start = start is not None
    extra = 0 if fields is None else FIELD_ROWS
    if split:
        out_shape = [
            jax.ShapeDtypeStruct((rows + extra, SIDE), jnp.bfloat16),
            jax.ShapeDtypeStruct((rows, SIDE), jnp.float32),
        ]
    else:
        out_shape = [jax.ShapeDtypeStruct((QUARTER_COLS, rows, LANES), jnp.float32)]
    stages = [pltpu.VMEM((slots, stripe, SIDE), item.dtype) for item in out_shape] if split else []
    token = jax.ShapeDtypeStruct((1, 1), jnp.float32)
    return pl.pallas_call(
        functools.partial(quarter_kernel, geom, step, sources, has_start, split, len(after), fields is not None),
        out_shape=out_shape + [token],
        in_specs=[smem] * 5
        + [hbm] * sources
        + [hbm, hbm]
        + ([hbm] if has_start else [])
        + [hbm] * (len(after) + (fields is not None)),
        out_specs=[hbm] * len(out_shape) + [smem],
        scratch_shapes=[
            pltpu.VMEM((COL_TILES, 2 * row_pad + rows, LANES), jnp.float32),
            pltpu.VMEM((4, groups * group_rows, BLOCK), jnp.bfloat16),
            pltpu.VMEM((2 * groups, window, BASES * BLOCK), jnp.bfloat16),
            pltpu.VMEM(bands[0].shape, jnp.bfloat16),
            pltpu.VMEM(bands[1].shape, jnp.bfloat16),
            pltpu.SMEM((sources * images[0].shape[0] + 1,), jnp.int32),
            pltpu.SemaphoreType.DMA((4, 2 * groups)),
            pltpu.SemaphoreType.DMA((max(7, 2 * slots),)),
        ]
        + stages,
        compiler_params=pltpu.CompilerParams(vmem_limit_bytes=60 * 1024 * 1024),
        cost_estimate=pl.CostEstimate(flops=1 << 20, bytes_accessed=1 << 20, transcendentals=0),
    )(table, *lists, *images, *bands, *([start] if has_start else []), *after, *([] if fields is None else [fields]))


def on_device(
    expo_count, patch_count, images, block_weight, block_patch, block_offset, kernel_index, coef_table
):
    stripe = SIDE // expo_count
    slots = expo_count // 2
    depth = patch_count // 2
    mixed = slots == 2
    expo, patch = lax.axis_index("expo"), lax.axis_index("patch")
    everyone = [(e, p) for e in range(expo_count) for p in range(patch_count)]

    def swap(value, partner):
        route = []
        for e, p in everyone:
            to_e, to_p = partner(e, p)
            route.append((e * patch_count + p, to_e * patch_count + to_p))
        return lax.ppermute(value, ("expo", "patch"), route)

    def twin(e, p):
        return e ^ 1, p

    def first_partner(e, p):
        if mixed and e % 2 == 1:
            return e ^ 2, p
        return e, p ^ 1

    twin_images = swap(images, twin)
    weights = block_weight.astype(jnp.float32)
    own = (block_patch.T, block_offset.T, kernel_index, weights)
    lists = jnp.stack(
        [block_patch[:, 0], block_offset[:, 0], block_offset[:, 1], kernel_index]
    ).astype(jnp.float32)
    lists = jnp.concatenate([lists, weights[None]], axis=0)
    twin_lists = swap(lists, twin)
    lists = jnp.concatenate([lists, twin_lists], axis=1)

    def unpack(known):
        ids = known[:4].astype(jnp.int32)
        return ids[:1], ids[1:3], ids[3], known[4]

    other, both = unpack(twin_lists), unpack(lists)

    ids = lists[:3].astype(jnp.int32)
    top = (ids[0] // PGX) * SIDE + ids[1]
    left = (ids[0] % PGX) * SIDE + ids[2]
    digits = jnp.stack([top // LANES, top % LANES, left // LANES, left % LANES])
    fields = jnp.concatenate([digits.astype(jnp.bfloat16), lists[4:].astype(jnp.bfloat16)], axis=0)

    def full(known):
        return jnp.pad(known, ((0, FIELD_ROWS - known.shape[0]), (0, SIDE - known.shape[1])))

    def below(value, known):
        return value if known is None else jnp.concatenate([value, full(known)], axis=0)

    def known_in(value, count):
        return value[-FIELD_ROWS:][: fields.shape[0], :count]

    table = coef_table.T
    bands = make_bands(stripe)

    def quarter(step, *args, **kwargs):
        return make_quarter((stripe, slots), step, table, *args, **kwargs)

    def second_hops(stay, got, token, known):
        def add(n):
            rows = slice(n * stripe, (n + 1) * stripe)
            return stay[rows] + got[rows].astype(jnp.float32)

        total = add(slots - 1)
        parts = [
            below((add(slots - 1 - hop) + token).astype(jnp.bfloat16), known)
            for hop in range(1, slots)
        ]
        return total, parts

    def second_swap(parts):
        received = []
        for hop, part in enumerate(parts, 1):

            def partner(e, p, hop=hop):
                if mixed and e % 2 == 1:
                    return e, p ^ 1
                return e ^ (2 * hop), p

            received.append(swap(part, partner))
        return received

    steps = list(range(depth))[::-1]
    early = quarter(
        steps[0], [images], own, bands, split=False
    )[0]
    leave, stay, _ = quarter(
        steps[0], [twin_images], other, bands, start=early, fields=full(fields)
    )

    def finish(entry, token=0.0):
        _, total, received = entry
        for value in received:
            total = total + value[:stripe].astype(jnp.float32)
        return total + token

    def advance(entry, token, known=None):
        number, kept, arrival = entry
        total, parts = second_hops(kept, arrival, token, known)
        return (number, total, second_swap(parts)), parts

    carried, neighbour = {}, []

    def forward(number, total, known=None):
        for value in carried.pop(number, []):
            total = total + value[:stripe].astype(jnp.float32)
        if number == 0:
            return total
        low = number & -number
        sent = below(total.astype(jnp.bfloat16), known)
        moved = swap(sent, lambda e, p: (e, p ^ (2 * low)))
        carried.setdefault(number ^ low, []).append(moved)
        if known is not None:
            neighbour.append(known_in(moved, known.shape[1]))
        return sent

    firsts, seconds, result, known = [], [], None, fields
    for step in steps:
        firsts.append((step, stay, swap(leave, first_partner)))
        if step == 0:
            break
        after = [leave]
        if len(firsts) > 1:
            if seconds:
                entry = seconds.pop(0)
                lists_now = None
                if entry[0] == depth - 1:
                    more = [known_in(value, known.shape[1]) for value in entry[2]]
                    known = lists_now = jnp.concatenate([known] + more, axis=1)
                after.append(forward(entry[0], finish(entry, token), lists_now))
            lists_now = None
            if firsts[0][0] == depth - 1:
                more = known_in(firsts[0][2], known.shape[1])
                known = lists_now = jnp.concatenate([known, more], axis=1)
            entry, parts = advance(firsts.pop(0), token, lists_now)
            seconds.append(entry)
            after += parts
        leave, stay, token = quarter(step - 1, [images, twin_images], both, bands, after=after)
        token = token[0, 0]
    known = jnp.concatenate([known] + neighbour, axis=1)
    while firsts or seconds:
        entry = seconds.pop(0)
        result = forward(entry[0], finish(entry, token))
        if firsts:
            seconds.append(advance(firsts.pop(0), token)[0])
    reach = 4
    while reach < patch_count:
        known = jnp.concatenate([known, swap(known, lambda e, p, r=reach: (e, p ^ r))], axis=1)
        reach *= 2

    places = known[:4].astype(jnp.int32)
    top = places[0] * LANES + places[1] - MARGIN
    left = places[2] * LANES + places[3] - MARGIN
    my_row = (patch // PGX) * SIDE + expo * stripe + jnp.arange(stripe)
    my_col = (patch % PGX) * SIDE + jnp.arange(SIDE)
    row_gap = my_row[:, None] - top[None, :]
    col_gap = my_col[None, :] - left[:, None]
    row_in = jnp.where((row_gap >= 0) & (row_gap < BLOCK), known[4][None, :], 0.0)
    col_in = (col_gap >= 0) & (col_gap < BLOCK)
    weight_map = jnp.dot(
        row_in.astype(jnp.bfloat16),
        col_in.astype(jnp.bfloat16),
        preferred_element_type=jnp.float32,
    )

    coadd_map = result / jnp.maximum(weight_map, weight_floor)
    return (coadd_map[None], weight_map[None])


def solution(mesh):
    return jax.shard_map(
        functools.partial(on_device, mesh.shape["expo"], mesh.shape["patch"]),
        mesh=mesh,
        in_specs=(
            P(("expo", "patch"), None, None),
            P(("expo", "patch")),
            P(("expo", "patch"), None),
            P(("expo", "patch"), None),
            P(("expo", "patch")),
            P(),
        ),
        out_specs=(P("patch", "expo", None), P("patch", "expo", None)),
        check_vma=False,
    )
```

time: 184 us -> 128 us (0.70)
  the two profiles are of different devices: /device:TPU:12 before, /device:TPU:0 now
where the time goes in v2:
time: 128 us; the launch traced here: 126 us
  Pallas kernels  52.5 us (41%)
  waiting for transfers between devices  24.2 us (19%)
  starting transfers between devices  21.6 us (17%)
  other arithmetic  19.5 us (15%)
  local copies, waits for them, and re-layouts  6.75 us (5%)
    pallas_call x5, Pallas kernels, make_quarter(): pl.pallas_call(functools.partial(quarter_kernel, geom, step, sources, has...  52.5 us
    ppermute x14, waiting for transfers between devices, swap(): return lax.ppermute(value, ('expo', 'patch'), route)  24.2 us
    ppermute x14, starting transfers between devices, swap(): return lax.ppermute(value, ('expo', 'patch'), route)  21.6 us
    convert_element_type x4, other arithmetic, second_hops(): (add(slots - 1 - hop) + token).astype(jnp.bfloat16)  7.25 us
    convert_element_type x3, other arithmetic, forward(): sent = below(total.astype(jnp.bfloat16), known)  6.77 us
    broadcast_in_dim x1, other arithmetic, on_device(): return (coadd_map[None], weight_map[None])  3.12 us
  transfers between devices with their start and end apart: 14, of which 5 were waited for; matrix products, arithmetic and copies ran while one was open for 17% of the time, Pallas kernels for 34%

profile of v2, /device:TPU:0, one launch (start us, length us, event | category | flops | bytes accessed | tf_op | source)
XLA Modules:
  0.0 126.2 jit_solution(14432719989799624618)
XLA Ops:
  2.6 1.2 fusion.43
  3.9 7.1 %shard_map.95 = (f32[16,512,128]{2,1,0:T(8,128)}, f32[1,1]{1,0:T(1,128)}) custom-call(f32[3,189]{1,0:T(4,128)} %bitcast.25, s32[1,12]{1,0:T(1,128)} %bitcast.33, s32[2,12]{1,0:T(2,128)} %bitcast.30, s32[12]{0:T(128)} %refs_3_.1, f32[12]{0:T(128)} %get-tuple-element.40.refs_4_, bf16[12,512,512]{2,1,0:T(8,128)(2,1)} %refs_5_.7, ...), custom_call_target="tpu_custom_call" | custom-call | flops 1048576 | bytes 1048576 | tf_op jit(solution)/shard_map/pallas_call | solution.py:346
  13.6 9.1 %shard_map.96 = (bf16[528,1024]{1,0:T(8,128)(2,1)}, f32[512,1024]{1,0:T(8,128)}, f32[1,1]{1,0:T(1,128)}) custom-call(f32[3,189]{1,0:T(4,128)} %bitcast.26, s32[1,12]{1,0:T(1,128)} %get-tuple-element.35.refs_1_, s32[2,12]{1,0:T(2,128)} %slice.146.refs_2_, s32[12]{0:T(128)} %get-tuple-element.34.refs_3_, f32[12]{0:T(128)} %slice_bitcast_fusion.refs_4_, ...), custom_call_target="tpu_custom_call" | custom-call | flops 1048576 | bytes 1048576 | tf_op jit(solution)/shard_map/pallas_call | solution.py:346
  22.7 3.0 %collective-permute-start.2 = (bf16[528,1024]{1,0:T(8,128)(2,1)}, bf16[528,1024]{1,0:T(8,128)(2,1)S(1)}, u32[]{:S(2)}, u32[]{:S(2)}) collective-permute-start(bf16[528,1024]{1,0:T(8,128)(2,1)} %get-tuple-element.15.refs_9_), channel_id=1, source_target_pairs={{0,1},{1,0},{2,3},{3,2},{4,5},{5,4},{6,7},{7,6},{8,24},{9,25},{10,... | collective-permute-start | bytes 3244040 | tf_op jit(solution)/shard_map/ppermute | solution.py:386
  27.4 12.7 %shard_map.97 = (bf16[512,1024]{1,0:T(8,128)(2,1)}, f32[512,1024]{1,0:T(8,128)}, f32[1,1]{1,0:T(1,128)}) custom-call(f32[3,189]{1,0:T(4,128)} %bitcast.27, s32[1,24]{1,0:T(1,128)} %get-tuple-element.33.refs_1_, s32[2,24]{1,0:T(2,128)} %slice.141.refs_2_, s32[24]{0:T(128)} %get-tuple-element.32.refs_3_, f32[24]{0:T(128)} %slice_bitcast_fusion.5.refs_4_, ...), custom_call_target="tpu_custom_call" | custom-call | flops 1048576 | bytes 1048576 | tf_op jit(solution)/shard_map/pallas_call | solution.py:346
  42.1 1.8 %collective-permute-start.3 = (bf16[272,1024]{1,0:T(8,128)(2,1)S(1)}, bf16[272,1024]{1,0:T(8,128)(2,1)S(1)}, u32[]{:S(2)}, u32[]{:S(2)}) collective-permute-start(bf16[272,1024]{1,0:T(8,128)(2,1)S(1)} %pad_maximum_fusion.refs_10_), channel_id=1, source_target_pairs={{0,16},{1,17},{2,18},{3,19},{4,20},{5,21},{6,22},{7,23},{8,9},{9,8... | collective-permute-start | bytes 1671176 | tf_op jit(solution)/shard_map/ppermute | solution.py:386
  44.6 11.9 %shard_map.98 = (bf16[512,1024]{1,0:T(8,128)(2,1)}, f32[512,1024]{1,0:T(8,128)}, f32[1,1]{1,0:T(1,128)}) custom-call(f32[3,189]{1,0:T(4,128)} %bitcast.28, s32[1,24]{1,0:T(1,128)} %get-tuple-element.33.refs_1_, s32[2,24]{1,0:T(2,128)} %slice.141.refs_2_, s32[24]{0:T(128)} %get-tuple-element.32.refs_3_, f32[24]{0:T(128)} %slice_bitcast_fusion.5.refs_4_, ...), custom_call_target="tpu_custom_call" | custom-call | flops 1048576 | bytes 1048576 | tf_op jit(solution)/shard_map/pallas_call | solution.py:346
  57.7 2.2 %add_convert_fusion.5 = bf16[256,1024]{1,0:T(8,128)(2,1)S(1)} fusion(f32[512,1024]{1,0:T(8,128)} %get-tuple-element.17, bf16[272,1024]{1,0:T(8,128)(2,1)S(1)} %collective-permute-done.3, bf16[528,1024]{1,0:T(8,128)(2,1)} %copy-done.7, f32[]{:T(128)} %bitcast.12), kind=kLoop, calls=%fused_computation.10 | loop fusion | flops 1572864 | bytes 2621444 | tf_op jit(solution)/shard_map/convert_element_type | solution.py:484
  60.0 6.5 %collective-permute-start.8 = (bf16[272,1024]{1,0:T(8,128)(2,1)S(1)}, bf16[272,1024]{1,0:T(8,128)(2,1)}, u32[]{:S(2)}, u32[]{:S(2)}) collective-permute-start(bf16[272,1024]{1,0:T(8,128)(2,1)S(1)} %pad_maximum_fusion.1.refs_10_), channel_id=1, source_target_pairs={{0,2},{1,3},{2,0},{3,1},{4,6},{5,7},{6,4},{7,5},{8,10},{9,11},{10,... | collective-permute-start | bytes 1671176 | tf_op jit(solution)/shard_map/ppermute | solution.py:386
  66.4 1.8 %add_convert_fusion.4.refs_11_ = bf16[256,1024]{1,0:T(8,128)(2,1)S(1)} fusion(f32[512,1024]{1,0:T(8,128)S(1)} %copy-done.3, bf16[512,1024]{1,0:T(8,128)(2,1)} %collective-permute-done.4, f32[]{:T(128)} %bitcast.12), kind=kLoop, calls=%fused_computation.9 | loop fusion | flops 1048576 | bytes 2097156 | tf_op jit(solution)/shard_map/convert_element_type | solution.py:440
  69.1 11.6 %shard_map.99 = (bf16[512,1024]{1,0:T(8,128)(2,1)}, f32[512,1024]{1,0:T(8,128)}, f32[1,1]{1,0:T(1,128)}) custom-call(f32[3,189]{1,0:T(4,128)} %bitcast.29, s32[1,24]{1,0:T(1,128)} %get-tuple-element.33.refs_1_, s32[2,24]{1,0:T(2,128)} %slice.141.refs_2_, s32[24]{0:T(128)} %get-tuple-element.32.refs_3_, f32[24]{0:T(128)} %slice_bitcast_fusion.5.refs_4_, ...), custom_call_target="tpu_custom_call" | custom-call | flops 1048576 | bytes 1048576 | tf_op jit(solution)/shard_map/pallas_call | solution.py:346
  80.7 1.8 %collective-permute-start.5 = (bf16[512,1024]{1,0:T(8,128)(2,1)}, bf16[512,1024]{1,0:T(8,128)(2,1)}, u32[]{:S(2)}, u32[]{:S(2)}) collective-permute-start(bf16[512,1024]{1,0:T(8,128)(2,1)} %get-tuple-element.23), channel_id=1, source_target_pairs={{0,1},{1,0},{2,3},{3,2},{4,5},{5,4},{6,7},{7,6},{8,24},{9,25},{10,... | collective-permute-start | bytes 3145736 | tf_op jit(solution)/shard_map/ppermute | solution.py:386
  82.5 2.9 %add_convert_fusion.1 = bf16[256,1024]{1,0:T(8,128)(2,1)} fusion(f32[512,1024]{1,0:T(8,128)} %get-tuple-element.25, bf16[512,1024]{1,0:T(8,128)(2,1)} %collective-permute-done.10, f32[]{:T(128)} %bitcast.13), kind=kLoop, calls=%fused_computation.6 | loop fusion | flops 1048576 | bytes 2097156 | tf_op jit(solution)/shard_map/convert_element_type | solution.py:440
  85.4 1.1 collective-permute-start.11
  87.1 1.6 %collective-permute-start.13 = (bf16[5,192]{1,0:T(8,128)(2,1)S(1)}, bf16[5,192]{1,0:T(8,128)(2,1)S(1)}, u32[]{:S(2)}, u32[]{:S(2)}) collective-permute-start(bf16[5,192]{1,0:T(8,128)(2,1)S(1)} %pad_maximum_fusion.4), channel_id=1, source_target_pairs={{0,4},{1,5},{2,6},{3,7},{4,0},{5,1},{6,2},{7,3},{8,12},{9,13},{10,... | collective-permute-start | bytes 5768 | tf_op jit(solution)/shard_map/ppermute | solution.py:386
  88.7 2.2 %add_convert_fusion.2 = bf16[256,1024]{1,0:T(8,128)(2,1)S(1)} fusion(bf16[256,1024]{1,0:T(8,128)(2,1)} %collective-permute-done.7, f32[512,1024]{1,0:T(8,128)S(1)} %copy-done.3, bf16[272,1024]{1,0:T(8,128)(2,1)} %collective-permute-done.8, bf16[512,1024]{1,0:T(8,128)(2,1)} %collective-permute-done.4, f32[]{:T(128)} %bitcast.13), kind=kLoop, calls=%fused_computation.7 | loop fusion | flops 2097152 | bytes 3145732 | tf_op jit(solution)/shard_map/convert_element_type | solution.py:484
  91.0 1.4 %collective-permute-start.9 = (bf16[256,1024]{1,0:T(8,128)(2,1)S(1)}, bf16[256,1024]{1,0:T(8,128)(2,1)S(1)}, u32[]{:S(2)}, u32[]{:S(2)}) collective-permute-start(bf16[256,1024]{1,0:T(8,128)(2,1)S(1)} %add_convert_fusion.2), channel_id=1, source_target_pairs={{0,4},{1,5},{2,6},{3,7},{4,0},{5,1},{6,2},{7,3},{8,12},{9,13},{10,... | collective-permute-start | bytes 1572872 | tf_op jit(solution)/shard_map/ppermute | solution.py:386
  92.5 6.4 %collective-permute-done.11 = bf16[256,1024]{1,0:T(8,128)(2,1)} collective-permute-done((bf16[256,1024]{1,0:T(8,128)(2,1)}, bf16[256,1024]{1,0:T(8,128)(2,1)}, u32[]{:S(2)}, u32[]{:S(2)}) %collective-permute-start.11) | collective-permute-done | bytes 524320 | tf_op jit(solution)/shard_map/ppermute | solution.py:386
  98.8 2.3 %add_convert_fusion = bf16[256,1024]{1,0:T(8,128)(2,1)S(1)} fusion(bf16[256,1024]{1,0:T(8,128)(2,1)} %collective-permute-done.11, f32[512,1024]{1,0:T(8,128)} %get-tuple-element.25, bf16[512,1024]{1,0:T(8,128)(2,1)} %collective-permute-done.10, f32[]{:T(128)} %bitcast.13), kind=kLoop, calls=%fused_computation.5 | loop fusion | flops 1572864 | bytes 2621444 | tf_op jit(solution)/shard_map/convert_element_type | solution.py:484
  101.5 1.8 %add_convert_fusion.3 = bf16[256,1024]{1,0:T(8,128)(2,1)S(1)} fusion(f32[512,1024]{1,0:T(8,128)S(1)} %copy-done.5, bf16[512,1024]{1,0:T(8,128)(2,1)} %collective-permute-done.5, f32[]{:T(128)} %bitcast.13), kind=kLoop, calls=%fused_computation.8 | loop fusion | flops 1048576 | bytes 2097156 | tf_op jit(solution)/shard_map/convert_element_type | solution.py:440
  103.3 2.2 %collective-permute-start.6 = (bf16[256,1024]{1,0:T(8,128)(2,1)S(1)}, bf16[256,1024]{1,0:T(8,128)(2,1)S(1)}, u32[]{:S(2)}, u32[]{:S(2)}) collective-permute-start(bf16[256,1024]{1,0:T(8,128)(2,1)S(1)} %add_convert_fusion.3), channel_id=1, source_target_pairs={{0,16},{1,17},{2,18},{3,19},{4,20},{5,21},{6,22},{7,23},{8,9},{9,8... | collective-permute-start | bytes 1572872 | tf_op jit(solution)/shard_map/ppermute | solution.py:386
  106.3 10.3 %collective-permute-done.9 = bf16[256,1024]{1,0:T(8,128)(2,1)S(1)} collective-permute-done((bf16[256,1024]{1,0:T(8,128)(2,1)S(1)}, bf16[256,1024]{1,0:T(8,128)(2,1)S(1)}, u32[]{:S(2)}, u32[]{:S(2)}) %collective-permute-start.9) | collective-permute-done | bytes 524320 | tf_op jit(solution)/shard_map/ppermute | solution.py:386
  116.6 6.4 %collective-permute-done.12 = bf16[256,1024]{1,0:T(8,128)(2,1)S(1)} collective-permute-done((bf16[256,1024]{1,0:T(8,128)(2,1)S(1)}, bf16[256,1024]{1,0:T(8,128)(2,1)S(1)}, u32[]{:S(2)}, u32[]{:S(2)}) %collective-permute-start.12) | collective-permute-done | bytes 524320 | tf_op jit(solution)/shard_map/ppermute | solution.py:386
  123.0 3.1 %divide_bitcast_fusion = f32[1,256,1024]{2,1,0:T(8,128)} fusion(f32[256,1024]{1,0:T(8,128)S(1)} %fusion.1, bf16[256,1024]{1,0:T(8,128)(2,1)S(1)} %collective-permute-done.12, bf16[256,1024]{1,0:T(8,128)(2,1)S(1)} %collective-permute-done.9, bf16[256,1024]{1,0:T(8,128)(2,1)S(1)} %collective-permute-done.6, f32[512,1024]{1,0:T(8,128)S(1)} %copy-done.5, ...), kind=kLoop, calls=%fused_computation.4 | loop fusion | flops 2883584 | bytes 5242884 | tf_op jit(solution)/shard_map/broadcast_in_dim | solution.py:541
  (67 shorter events, 12.9 us)
Async XLA Ops:
  0.6 12.9 %collective-permute-start.1 = (bf16[12,512,512]{2,1,0:T(8,128)(2,1)}, bf16[12,512,512]{2,1,0:T(8,128)(2,1)}, u32[]{:S(2)}, u32[]{:S(2)}) collective-permute-start(bf16[12,512,512]{2,1,0:T(8,128)(2,1)} %refs_5_.7), channel_id=1, source_target_pairs={{0,8},{1,9},{2,10},{3,11},{4,12},{5,13},{6,14},{7,15},{8,0},{9,1},... | collective-permute-start | bytes 18874376 | tf_op jit(solution)/shard_map/ppermute | solution.py:386
  3.8 7.3 %collective-permute-start = (f32[5,12]{1,0:T(8,128)S(1)}, f32[5,12]{1,0:T(8,128)S(1)}, u32[]{:S(2)}, u32[]{:S(2)}) collective-permute-start(f32[5,12]{1,0:T(8,128)S(1)} %pad_maximum_fusion.2), channel_id=1, source_target_pairs={{0,8},{1,9},{2,10},{3,11},{4,12},{5,13},{6,14},{7,15},{8,0},{9,1},... | collective-permute-start | bytes 728 | tf_op jit(solution)/shard_map/ppermute | solution.py:386
  22.7 17.4 %collective-permute-start.2 = (bf16[528,1024]{1,0:T(8,128)(2,1)}, bf16[528,1024]{1,0:T(8,128)(2,1)S(1)}, u32[]{:S(2)}, u32[]{:S(2)}) collective-permute-start(bf16[528,1024]{1,0:T(8,128)(2,1)} %get-tuple-element.15.refs_9_), channel_id=1, source_target_pairs={{0,1},{1,0},{2,3},{3,2},{4,5},{5,4},{6,7},{7,6},{8,24},{9,25},{10,... | collective-permute-start | bytes 3244040 | tf_op jit(solution)/shard_map/ppermute | solution.py:386
  27.4 13.8 %copy-start.4 = (f32[512,1024]{1,0:T(8,128)S(1)}, f32[512,1024]{1,0:T(8,128)}, u32[]{:S(2)}) copy-start(f32[512,1024]{1,0:T(8,128)} %get-tuple-element.17) | copy-start | bytes 6291460
  40.1 1.0 copy-start.7
  42.0 2.6 %copy-start.1 = (bf16[272,1024]{1,0:T(8,128)(2,1)}, bf16[272,1024]{1,0:T(8,128)(2,1)S(1)}, u32[]{:S(2)}) copy-start(bf16[272,1024]{1,0:T(8,128)(2,1)S(1)} %pad_maximum_fusion.refs_10_) | copy-start | bytes 1671172
  42.1 15.6 %collective-permute-start.3 = (bf16[272,1024]{1,0:T(8,128)(2,1)S(1)}, bf16[272,1024]{1,0:T(8,128)(2,1)S(1)}, u32[]{:S(2)}, u32[]{:S(2)}) collective-permute-start(bf16[272,1024]{1,0:T(8,128)(2,1)S(1)} %pad_maximum_fusion.refs_10_), channel_id=1, source_target_pairs={{0,16},{1,17},{2,18},{3,19},{4,20},{5,21},{6,22},{7,23},{8,9},{9,8... | collective-permute-start | bytes 1671176 | tf_op jit(solution)/shard_map/ppermute | solution.py:386
  43.9 22.5 %collective-permute-start.4 = (bf16[512,1024]{1,0:T(8,128)(2,1)}, bf16[512,1024]{1,0:T(8,128)(2,1)}, u32[]{:S(2)}, u32[]{:S(2)}) collective-permute-start(bf16[512,1024]{1,0:T(8,128)(2,1)} %get-tuple-element.16.refs_9_), channel_id=1, source_target_pairs={{0,1},{1,0},{2,3},{3,2},{4,5},{5,4},{6,7},{7,6},{8,24},{9,25},{10,... | collective-permute-start | bytes 3145736 | tf_op jit(solution)/shard_map/ppermute | solution.py:386
  56.5 9.9 %copy-start.3 = (f32[512,1024]{1,0:T(8,128)S(1)}, f32[512,1024]{1,0:T(8,128)}, u32[]{:S(2)}) copy-start(f32[512,1024]{1,0:T(8,128)} %get-tuple-element.21) | copy-start | bytes 6291460
  56.5 26.0 %collective-permute-start.10 = (bf16[512,1024]{1,0:T(8,128)(2,1)}, bf16[512,1024]{1,0:T(8,128)(2,1)}, u32[]{:S(2)}, u32[]{:S(2)}) collective-permute-start(bf16[512,1024]{1,0:T(8,128)(2,1)} %get-tuple-element.19.refs_9_), channel_id=1, source_target_pairs={{0,1},{1,0},{2,3},{3,2},{4,5},{5,4},{6,7},{7,6},{8,24},{9,25},{10,... | collective-permute-start | bytes 3145736 | tf_op jit(solution)/shard_map/ppermute | solution.py:386
  60.0 9.0 %copy-start = (bf16[272,1024]{1,0:T(8,128)(2,1)}, bf16[272,1024]{1,0:T(8,128)(2,1)S(1)}, u32[]{:S(2)}) copy-start(bf16[272,1024]{1,0:T(8,128)(2,1)S(1)} %pad_maximum_fusion.1.refs_10_) | copy-start | bytes 1671172
  60.0 26.5 %collective-permute-start.8 = (bf16[272,1024]{1,0:T(8,128)(2,1)S(1)}, bf16[272,1024]{1,0:T(8,128)(2,1)}, u32[]{:S(2)}, u32[]{:S(2)}) collective-permute-start(bf16[272,1024]{1,0:T(8,128)(2,1)S(1)} %pad_maximum_fusion.1.refs_10_), channel_id=1, source_target_pairs={{0,2},{1,3},{2,0},{3,1},{4,6},{5,7},{6,4},{7,5},{8,10},{9,11},{10,... | collective-permute-start | bytes 1671176 | tf_op jit(solution)/shard_map/ppermute | solution.py:386
  68.3 0.8 copy-start.2
  68.3 20.4 %collective-permute-start.7 = (bf16[256,1024]{1,0:T(8,128)(2,1)S(1)}, bf16[256,1024]{1,0:T(8,128)(2,1)}, u32[]{:S(2)}, u32[]{:S(2)}) collective-permute-start(bf16[256,1024]{1,0:T(8,128)(2,1)S(1)} %add_convert_fusion.4.refs_11_), channel_id=1, source_target_pairs={{0,16},{1,17},{2,18},{3,19},{4,20},{5,21},{6,22},{7,23},{8,9},{9,8... | collective-permute-start | bytes 1572872 | tf_op jit(solution)/shard_map/ppermute | solution.py:386
  80.7 20.8 %collective-permute-start.5 = (bf16[512,1024]{1,0:T(8,128)(2,1)}, bf16[512,1024]{1,0:T(8,128)(2,1)}, u32[]{:S(2)}, u32[]{:S(2)}) collective-permute-start(bf16[512,1024]{1,0:T(8,128)(2,1)} %get-tuple-element.23), channel_id=1, source_target_pairs={{0,1},{1,0},{2,3},{3,2},{4,5},{5,4},{6,7},{7,6},{8,24},{9,25},{10,... | collective-permute-start | bytes 3145736 | tf_op jit(solution)/shard_map/ppermute | solution.py:386
  85.4 13.5 %collective-permute-start.11 = (bf16[256,1024]{1,0:T(8,128)(2,1)}, bf16[256,1024]{1,0:T(8,128)(2,1)}, u32[]{:S(2)}, u32[]{:S(2)}) collective-permute-start(bf16[256,1024]{1,0:T(8,128)(2,1)} %add_convert_fusion.1), channel_id=1, source_target_pairs={{0,16},{1,17},{2,18},{3,19},{4,20},{5,21},{6,22},{7,23},{8,9},{9,8... | collective-permute-start | bytes 1572872 | tf_op jit(solution)/shard_map/ppermute | solution.py:386
  87.1 5.2 %collective-permute-start.13 = (bf16[5,192]{1,0:T(8,128)(2,1)S(1)}, bf16[5,192]{1,0:T(8,128)(2,1)S(1)}, u32[]{:S(2)}, u32[]{:S(2)}) collective-permute-start(bf16[5,192]{1,0:T(8,128)(2,1)S(1)} %pad_maximum_fusion.4), channel_id=1, source_target_pairs={{0,4},{1,5},{2,6},{3,7},{4,0},{5,1},{6,2},{7,3},{8,12},{9,13},{10,... | collective-permute-start | bytes 5768 | tf_op jit(solution)/shard_map/ppermute | solution.py:386
  90.9 10.6 %copy-start.5 = (f32[512,1024]{1,0:T(8,128)S(1)}, f32[512,1024]{1,0:T(8,128)}, u32[]{:S(2)}) copy-start(f32[512,1024]{1,0:T(8,128)} %get-tuple-element.22) | copy-start | bytes 6291460
  91.0 25.7 %collective-permute-start.9 = (bf16[256,1024]{1,0:T(8,128)(2,1)S(1)}, bf16[256,1024]{1,0:T(8,128)(2,1)S(1)}, u32[]{:S(2)}, u32[]{:S(2)}) collective-permute-start(bf16[256,1024]{1,0:T(8,128)(2,1)S(1)} %add_convert_fusion.2), channel_id=1, source_target_pairs={{0,4},{1,5},{2,6},{3,7},{4,0},{5,1},{6,2},{7,3},{8,12},{9,13},{10,... | collective-permute-start | bytes 1572872 | tf_op jit(solution)/shard_map/ppermute | solution.py:386
  101.2 21.9 %collective-permute-start.12 = (bf16[256,1024]{1,0:T(8,128)(2,1)S(1)}, bf16[256,1024]{1,0:T(8,128)(2,1)S(1)}, u32[]{:S(2)}, u32[]{:S(2)}) collective-permute-start(bf16[256,1024]{1,0:T(8,128)(2,1)S(1)} %add_convert_fusion), channel_id=1, source_target_pairs={{0,2},{1,3},{2,0},{3,1},{4,6},{5,7},{6,4},{7,5},{8,10},{9,11},{10,... | collective-permute-start | bytes 1572872 | tf_op jit(solution)/shard_map/ppermute | solution.py:386
  103.3 19.8 %collective-permute-start.6 = (bf16[256,1024]{1,0:T(8,128)(2,1)S(1)}, bf16[256,1024]{1,0:T(8,128)(2,1)S(1)}, u32[]{:S(2)}, u32[]{:S(2)}) collective-permute-start(bf16[256,1024]{1,0:T(8,128)(2,1)S(1)} %add_convert_fusion.3), channel_id=1, source_target_pairs={{0,16},{1,17},{2,18},{3,19},{4,20},{5,21},{6,22},{7,23},{8,9},{9,8... | collective-permute-start | bytes 1572872 | tf_op jit(solution)/shard_map/ppermute | solution.py:386
  106.3 19.9 %copy-start.6 = (f32[256,1024]{1,0:T(8,128)}, f32[256,1024]{1,0:T(8,128)S(1)}, u32[]{:S(2)}) copy-start(f32[256,1024]{1,0:T(8,128)S(1)} %fusion.1) | copy-start | bytes 3145732

commit v3 on v2

--- a/solution.py
+++ b/solution.py
@@ -23,6 +23,8 @@
 HALF = BLOCK // 2
 PAD = 16
 BATCH = 4
+STREAMS = 2
+NEW_META = True
 FIELD_ROWS = 16
 COL_PAD = BLOCK // LANES
 TILE_COLS = SIDE // LANES
@@ -57,11 +59,13 @@
     height = window // parts
     row, col = np.indices((BASES * height, height + 2 * PAD))
     down = taps_at(row // height, col - row % height - PAD)
-    row, col = np.indices((BASES * BLOCK, 6 * LANES))
-    side = col // (2 * LANES)
-    col = col - side * LANES
-    mine = (col >= 192).astype(np.int32) + (col >= 320) == side
-    across = np.where(mine, taps_at(row // BLOCK, col - row % BLOCK), 0)
+    row, col = np.indices((2 * LANES, 2 * LANES))
+    across = []
+    for side, (low, high) in enumerate(((0, 192), (192, 320), (320, BLOCK))):
+        mine = (col + side * LANES >= low) & (col + side * LANES < high)
+        for b in range(BASES):
+            across.append(np.where(mine, taps_at(np.full_like(row, b), col - row), 0))
+    across = np.concatenate(across, axis=0)
     return jnp.asarray(down, jnp.bfloat16), jnp.asarray(across, jnp.bfloat16)
 
 
@@ -70,8 +74,8 @@
     groups, gap, window, parts, group_rows, row_pad = geometry(stripe)
     height = window // parts
     refs = list(refs)
-    table_ref, where_refs, weight_ref = refs.pop(0), [refs.pop(0) for _ in range(3)], refs.pop(0)
-    patch_ref, offset_ref, index_ref = where_refs
+    table_ref = refs.pop(0)
+    lists = [(refs.pop(0), refs.pop(0)) for _ in range(sources)]
     images = [refs.pop(0) for _ in range(sources)]
     band_hbm = [refs.pop(0), refs.pop(0)]
     start_ref = refs.pop(0) if has_start else None
@@ -80,7 +84,8 @@
     outs = [refs.pop(0) for _ in range(2 if split else 1)]
     token_ref = refs.pop(0)
     canvas, tile_buf, spread, down_ref, band_ref, chosen, sems, side_sems = refs[:8]
-    stages = refs[8:]
+    stages = refs[8:10]
+    early_ref = refs[10] if has_start else None
     expo, place_at = lax.axis_index("expo"), lax.axis_index("patch")
     core, row_at, col_at, quarter = expo & 1, expo >> 1, place_at & 1, (place_at >> 1) ^ step
     rows = slots * stripe
@@ -89,20 +94,25 @@
     def canvas_copies(other, out):
         copies = []
         for n in range(4):
-            cols = QUARTER_COLS // 4
-            mine = canvas.at[pl.ds(COL_PAD + n * cols, cols), pl.ds(row_pad, rows), :]
-            far = other.at[pl.ds(n * cols, cols)]
-            ends = (mine, far) if out else (far, mine)
-            copies.append(pltpu.make_async_copy(*ends, side_sems.at[2 + n]))
+            cols = pl.ds(n * (QUARTER_COLS // 4), QUARTER_COLS // 4)
+            far = other.at[cols]
+            if out:
+                mine = canvas.at[pl.ds(COL_PAD + cols.start, cols.size), pl.ds(row_pad, rows), :]
+                copies.append(pltpu.make_async_copy(mine, far, side_sems.at[2 + n]))
+            else:
+                copies.append(pltpu.make_async_copy(far, early_ref.at[cols], side_sems.at[2 + n]))
         return copies
 
-
-    loads = [
-        pltpu.make_async_copy(band_hbm[0], down_ref, side_sems.at[0]),
-        pltpu.make_async_copy(band_hbm[1], band_ref, side_sems.at[1]),
-    ]
+    late = []
+    third = band_ref.shape[0] // 3
+    loads = [pltpu.make_async_copy(band_hbm[0], down_ref, side_sems.at[0])]
+    for n in range(3):
+        part = pl.ds(n * third, third)
+        loads.append(
+            pltpu.make_async_copy(band_hbm[1].at[part], band_ref.at[part], side_sems.at[7 + n])
+        )
     if has_start:
-        loads += canvas_copies(start_ref, False)
+        late = canvas_copies(start_ref, False)
     if has_fields:
         loads.append(
             pltpu.make_async_copy(
@@ -110,29 +120,41 @@
             )
         )
     token_ref[0, 0] = 0.0
-    for load in loads:
+    for load in loads + late:
         load.start()
 
     stripe_bits = stripe.bit_length() - 1
     row_shift = BLOCK - MARGIN - (quarter >> 1) * SIDE
     col_shift = BLOCK - MARGIN - (quarter & 1) * (2 * SIDE)
 
-    def corner(i):
-        patch = patch_ref[0, i]
-        row = (patch >> PGX_BITS) * SIDE + offset_ref[0, i] + row_shift
-        col = (patch & (PGX - 1)) * SIDE + offset_ref[1, i] + col_shift
+    def located(top, left):
+        row, col = top + row_shift, left + col_shift
         return (row >> stripe_bits) - BLOCK // stripe, row & (stripe - 1), col
 
-    def scan(i, count):
-        stripe_at, rho, col = corner(i)
-        lowest = jnp.maximum(stripe_at, 0)
-        lowest = lowest + ((lowest + core) & 1)
-        highest = stripe_at + BLOCK // stripe - (rho == 0).astype(jnp.int32)
-        hit = (lowest <= jnp.minimum(highest, 2 * slots - 1)) & (col > 0) & (col < BLOCK + 2 * SIDE)
-        chosen[count] = i
-        return count + hit.astype(jnp.int32)
-
-    count = lax.fori_loop(0, sources * per_source, scan, jnp.int32(0))
+    def look_up(k, pick):
+        value = pick(lists[0], jnp.minimum(k, per_source - 1))
+        for n in range(1, sources):
+            other = pick(lists[n], jnp.maximum(k - n * per_source, 0))
+            value = jnp.where(k < n * per_source, value, other)
+        return value
+
+    def entry(k, field):
+        return look_up(k, lambda item, i: item[0][field, i])
+
+    count = jnp.int32(0)
+    for n, (place_ref, _) in enumerate(lists):
+
+        def scan(i, count, n=n, place_ref=place_ref):
+            stripe_at, rho, col = located(place_ref[0, i], place_ref[1, i])
+            lowest = jnp.maximum(stripe_at, 0)
+            lowest = lowest + ((lowest + core) & 1)
+            highest = stripe_at + BLOCK // stripe - (rho == 0).astype(jnp.int32)
+            hit = (lowest <= jnp.minimum(highest, 2 * slots - 1)) & (col > 0)
+            hit = hit & (col < BLOCK + 2 * SIDE)
+            chosen[count] = i + n * per_source
+            return count + hit.astype(jnp.int32)
+
+        count = lax.fori_loop(0, per_source, scan, count)
 
     def pieces_of(g):
         top, base = 2 * stripe * g, group_rows * g
@@ -177,16 +199,15 @@
                 tile_buf[slot, top:bottom, :] = jnp.zeros((bottom - top, BLOCK), tile_buf.dtype)
     start(0, 0)
     start(1, 1)
-    if not has_start:
-        canvas[COL_PAD : COL_PAD + QUARTER_COLS, row_pad : row_pad + rows, :] = jnp.zeros(
-            (QUARTER_COLS, rows, LANES), jnp.float32
-        )
+    canvas[COL_PAD : COL_PAD + QUARTER_COLS, row_pad : row_pad + rows, :] = jnp.zeros(
+        (QUARTER_COLS, rows, LANES), jnp.float32
+    )
     for load in loads:
         load.wait()
 
     def place(i):
         k = chosen[i]
-        stripe_at, rho, col = corner(k)
+        stripe_at, rho, col = located(entry(k, 0), entry(k, 1))
         col_tile = col >> 7
         shift = col & (LANES - 1)
         parted = ((stripe_at + core) & 1) == 0
@@ -198,8 +219,9 @@
 
     def down_pass(info, slot, half):
         k, first_at = info[0], info[6]
-        kernel = index_ref[k]
-        scales = [table_ref[b, kernel] * weight_ref[k] for b in range(BASES)]
+        kernel = entry(k, 2)
+        weight = look_up(k, lambda item, i: item[1][i])
+        scales = [table_ref[b, kernel] * weight for b in range(BASES)]
         for g in range(groups):
             for part in range(parts):
                 at = pl.multiple_of(g * group_rows + first_at + part * height, PAD)
@@ -229,10 +251,11 @@
             for side in range(3):
                 acc = None
                 for b in range(BASES):
-                    lo = LANES * side
+                    lo = b * BLOCK + LANES * side
+                    at = (side * BASES + b) * 2 * LANES
                     term = jnp.dot(
-                        spread[half * groups + g, :, b * BLOCK + lo : b * BLOCK + lo + 256],
-                        band_ref[b * BLOCK + lo : b * BLOCK + lo + 256, 256 * side : 256 * side + 256],
+                        spread[half * groups + g, :, lo : lo + 2 * LANES],
+                        band_ref[at : at + 2 * LANES],
                         preferred_element_type=jnp.float32,
                     )
                     acc = term if acc is None else acc + term
@@ -301,6 +324,8 @@
             store.wait()
         return
 
+    for load in late:
+        load.wait()
     mixed = slots == 2
     stores = []
     for kind, out in enumerate(outs):
@@ -314,13 +339,19 @@
             at = pl.multiple_of(row_pad + slot * stripe, PAD)
             for j in range(TILE_COLS):
                 piece = canvas[COL_PAD + side * TILE_COLS + j, pl.ds(at, stripe), :]
+                if has_start:
+                    from_row = pl.multiple_of(slot * stripe, stripe)
+                    piece = piece + early_ref[side * TILE_COLS + j, pl.ds(from_row, stripe), :]
                 stages[kind][i, :, j * LANES : (j + 1) * LANES] = piece.astype(out.dtype)
-            place_out = out.at[pl.ds(i * stripe, stripe)]
-            store = pltpu.make_async_copy(
-                stages[kind].at[i], place_out, side_sems.at[kind * slots + i]
-            )
-            store.start()
-            stores.append(store)
+            for n in range(STREAMS):
+                size = stripe // STREAMS
+                store = pltpu.make_async_copy(
+                    stages[kind].at[i, pl.ds(n * size, size)],
+                    out.at[pl.ds(i * stripe + n * size, size)],
+                    side_sems.at[10 + (kind * slots + i) * STREAMS + n],
+                )
+                store.start()
+                stores.append(store)
     for store in stores:
         store.wait()
 
@@ -346,7 +377,7 @@
     return pl.pallas_call(
         functools.partial(quarter_kernel, geom, step, sources, has_start, split, len(after), fields is not None),
         out_shape=out_shape + [token],
-        in_specs=[smem] * 5
+        in_specs=[smem] * (1 + 2 * sources)
         + [hbm] * sources
         + [hbm, hbm]
         + ([hbm] if has_start else [])
@@ -360,12 +391,100 @@
             pltpu.VMEM(bands[1].shape, jnp.bfloat16),
             pltpu.SMEM((sources * images[0].shape[0] + 1,), jnp.int32),
             pltpu.SemaphoreType.DMA((4, 2 * groups)),
-            pltpu.SemaphoreType.DMA((max(7, 2 * slots),)),
+            pltpu.SemaphoreType.DMA((10 + STREAMS * 2 * slots,)),
         ]
-        + stages,
-        compiler_params=pltpu.CompilerParams(vmem_limit_bytes=60 * 1024 * 1024),
+        + stages
+        + ([pltpu.VMEM((QUARTER_COLS, rows, LANES), jnp.float32)] if has_start else []),
+        compiler_params=pltpu.CompilerParams(vmem_limit_bytes=63 * 1024 * 1024),
         cost_estimate=pl.CostEstimate(flops=1 << 20, bytes_accessed=1 << 20, transcendentals=0),
     )(table, *lists, *images, *bands, *([start] if has_start else []), *after, *([] if fields is None else [fields]))
+
+
+def merge(stripe, jobs, after=()):
+    halves = 2
+    size = stripe // halves
+    operands, plan = [], []
+    for base, row, addends, known in jobs:
+        plan.append((len(operands), row, [start for _, start in addends], known is not None))
+        operands += [base] + [value for value, _ in addends] + ([] if known is None else [known])
+    count = sum(1 + len(starts) for _, _, starts, _ in plan)
+
+    def kernel(*refs):
+        inputs = refs[: len(operands)]
+        outs = refs[len(operands) + len(after) :][: len(jobs)]
+        token_ref = refs[len(operands) + len(after) + len(jobs)]
+        scratch = refs[len(operands) + len(after) + len(jobs) + 1 :]
+        wide, narrow, staged, sems, out_sems = scratch
+        token_ref[0, 0] = 0.0
+        copies, lists, which, where = [], [], 0, 0
+        for n, (at, row, starts, has_known) in enumerate(plan):
+            sources = [(inputs[at], row, wide.at[n])]
+            for m, start in enumerate(starts):
+                sources.append((inputs[at + 1 + m], start, narrow.at[where + m]))
+            where += len(starts)
+            per_half = []
+            for h in range(halves):
+                group = []
+                for m, (ref, start, to) in enumerate(sources):
+                    copy = pltpu.make_async_copy(
+                        ref.at[pl.ds(start + h * size, size)],
+                        to.at[pl.ds(h * size, size)],
+                        sems.at[which + m, h],
+                    )
+                    copy.start()
+                    group.append(copy)
+                per_half.append(group)
+            which += len(sources)
+            copies.append(per_half)
+            if has_known:
+                lists.append(
+                    pltpu.make_async_copy(
+                        inputs[at + 1 + len(starts)],
+                        outs[n].at[pl.ds(stripe, FIELD_ROWS)],
+                        out_sems.at[n, halves],
+                    )
+                )
+                lists[-1].start()
+        where = 0
+        for n, (at, row, starts, has_known) in enumerate(plan):
+            for h in range(halves):
+                for copy in copies[n][h]:
+                    copy.wait()
+                rows = pl.ds(h * size, size)
+                total = wide[n, rows, :]
+                for m in range(len(starts)):
+                    total = total + narrow[where + m, rows, :].astype(jnp.float32)
+                staged[n, rows, :] = total.astype(jnp.bfloat16)
+                store = pltpu.make_async_copy(
+                    staged.at[n, rows], outs[n].at[rows], out_sems.at[n, h]
+                )
+                store.start()
+                lists.append(store)
+            where += len(starts)
+        for copy in lists:
+            copy.wait()
+
+    hbm = pl.BlockSpec(memory_space=pl.ANY)
+    shapes = [
+        jax.ShapeDtypeStruct((stripe + (FIELD_ROWS if has_known else 0), SIDE), jnp.bfloat16)
+        for _, _, _, has_known in plan
+    ]
+    out = pl.pallas_call(
+        kernel,
+        out_shape=shapes + [jax.ShapeDtypeStruct((1, 1), jnp.float32)],
+        in_specs=[hbm] * (len(operands) + len(after)),
+        out_specs=[hbm] * len(shapes) + [pl.BlockSpec(memory_space=pltpu.SMEM)],
+        scratch_shapes=[
+            pltpu.VMEM((len(jobs), stripe, SIDE), jnp.float32),
+            pltpu.VMEM((count - len(jobs), stripe, SIDE), jnp.bfloat16),
+            pltpu.VMEM((len(jobs), stripe, SIDE), jnp.bfloat16),
+            pltpu.SemaphoreType.DMA((count, halves)),
+            pltpu.SemaphoreType.DMA((len(jobs), halves + 1)),
+        ],
+        compiler_params=pltpu.CompilerParams(vmem_limit_bytes=63 * 1024 * 1024),
+        cost_estimate=pl.CostEstimate(flops=0, bytes_accessed=0, transcendentals=0),
+    )(*operands, *after)
+    return out[: len(jobs)], out[-1][0, 0]
 
 
 def on_device(
@@ -395,32 +514,28 @@
 
     twin_images = swap(images, twin)
     weights = block_weight.astype(jnp.float32)
-    own = (block_patch.T, block_offset.T, kernel_index, weights)
-    lists = jnp.stack(
-        [block_patch[:, 0], block_offset[:, 0], block_offset[:, 1], kernel_index]
-    ).astype(jnp.float32)
-    lists = jnp.concatenate([lists, weights[None]], axis=0)
-    twin_lists = swap(lists, twin)
-    lists = jnp.concatenate([lists, twin_lists], axis=1)
-
-    def unpack(known):
-        ids = known[:4].astype(jnp.int32)
-        return ids[:1], ids[1:3], ids[3], known[4]
-
-    other, both = unpack(twin_lists), unpack(lists)
-
-    ids = lists[:3].astype(jnp.int32)
-    top = (ids[0] // PGX) * SIDE + ids[1]
-    left = (ids[0] % PGX) * SIDE + ids[2]
-    digits = jnp.stack([top // LANES, top % LANES, left // LANES, left % LANES])
-    fields = jnp.concatenate([digits.astype(jnp.bfloat16), lists[4:].astype(jnp.bfloat16)], axis=0)
+    places = jnp.stack(
+        [
+            (block_patch[:, 0] // PGX) * SIDE + block_offset[:, 0],
+            (block_patch[:, 0] % PGX) * SIDE + block_offset[:, 1],
+            kernel_index,
+        ]
+    )
+    own = (places, weights)
+    other = (swap(places, twin), swap(weights, twin))
+    both = own + other
+    table = coef_table.T
+    bands = make_bands(stripe)
+
+    def digits(places, weights):
+        parts = [places[0] // LANES, places[0] % LANES, places[1] // LANES, places[1] % LANES]
+        return jnp.stack([part.astype(jnp.bfloat16) for part in parts] + [weights.astype(jnp.bfloat16)])
+
+    fields = jnp.concatenate([digits(*own), digits(*other)], axis=1)
 
     def full(known):
         return jnp.pad(known, ((0, FIELD_ROWS - known.shape[0]), (0, SIDE - known.shape[1])))
 
-    def below(value, known):
-        return value if known is None else jnp.concatenate([value, full(known)], axis=0)
-
     def known_in(value, count):
         return value[-FIELD_ROWS:][: fields.shape[0], :count]
 
@@ -430,20 +545,21 @@
     def quarter(step, *args, **kwargs):
         return make_quarter((stripe, slots), step, table, *args, **kwargs)
 
-    def second_hops(stay, got, token, known):
-        def add(n):
-            rows = slice(n * stripe, (n + 1) * stripe)
-            return stay[rows] + got[rows].astype(jnp.float32)
-
-        total = add(slots - 1)
-        parts = [
-            below((add(slots - 1 - hop) + token).astype(jnp.bfloat16), known)
-            for hop in range(1, slots)
-        ]
-        return total, parts
-
-    def second_swap(parts):
-        received = []
+    def own_job(entry, extra, known=None):
+        _, stay, got, received = entry
+        row = (slots - 1) * stripe
+        addends = [(got, row)] + [(value, 0) for value in received + extra]
+        return stay, row, addends, None if known is None else full(known)
+
+    def part_jobs(entry, known=None):
+        _, stay, got, _ = entry
+        jobs = []
+        for hop in range(1, slots):
+            row = (slots - 1 - hop) * stripe
+            jobs.append((stay, row, [(got, row)], None if known is None else full(known)))
+        return jobs
+
+    def second_swap(entry, parts):
         for hop, part in enumerate(parts, 1):
 
             def partner(e, p, hop=hop):
@@ -451,8 +567,15 @@
                     return e, p ^ 1
                 return e ^ (2 * hop), p
 
-            received.append(swap(part, partner))
-        return received
+            entry[3].append(swap(part, partner))
+
+    carried = {}
+
+    def forward(step, sent):
+        low = step & -step
+        moved = swap(sent, lambda e, p: (e, p ^ (2 * low)))
+        carried.setdefault(step ^ low, []).append(moved)
+        return moved
 
     steps = list(range(depth))[::-1]
     early = quarter(
@@ -462,65 +585,48 @@
         steps[0], [twin_images], other, bands, start=early, fields=full(fields)
     )
 
-    def finish(entry, token=0.0):
-        _, total, received = entry
-        for value in received:
-            total = total + value[:stripe].astype(jnp.float32)
-        return total + token
-
-    def advance(entry, token, known=None):
-        number, kept, arrival = entry
-        total, parts = second_hops(kept, arrival, token, known)
-        return (number, total, second_swap(parts)), parts
-
-    carried, neighbour = {}, []
-
-    def forward(number, total, known=None):
-        for value in carried.pop(number, []):
-            total = total + value[:stripe].astype(jnp.float32)
-        if number == 0:
-            return total
-        low = number & -number
-        sent = below(total.astype(jnp.bfloat16), known)
-        moved = swap(sent, lambda e, p: (e, p ^ (2 * low)))
-        carried.setdefault(number ^ low, []).append(moved)
-        if known is not None:
-            neighbour.append(known_in(moved, known.shape[1]))
-        return sent
-
-    firsts, seconds, result, known = [], [], None, fields
-    for step in steps:
-        firsts.append((step, stay, swap(leave, first_partner)))
-        if step == 0:
-            break
+    known, entries, moved = fields, [], {}
+
+    def add_lists(values):
+        return jnp.concatenate([known] + [known_in(v, known.shape[1]) for v in values], axis=1)
+
+    def send_on(done, entry, after, lists_done=None, lists_entry=None):
+        jobs = [] if done is None else [own_job(done, carried.get(done[0], []), lists_done)]
+        sums, token = merge(stripe, jobs + part_jobs(entry, lists_entry), after)
+        if done is not None:
+            moved[done[0]] = forward(done[0], sums[0])
+        second_swap(entry, sums[len(jobs) :])
+        return sums, token
+
+    for n, step in enumerate(steps):
+        entries.append([step, stay, swap(leave, first_partner), []])
         after = [leave]
-        if len(firsts) > 1:
-            if seconds:
-                entry = seconds.pop(0)
-                lists_now = None
-                if entry[0] == depth - 1:
-                    more = [known_in(value, known.shape[1]) for value in entry[2]]
-                    known = lists_now = jnp.concatenate([known] + more, axis=1)
-                after.append(forward(entry[0], finish(entry, token), lists_now))
-            lists_now = None
-            if firsts[0][0] == depth - 1:
-                more = known_in(firsts[0][2], known.shape[1])
-                known = lists_now = jnp.concatenate([known, more], axis=1)
-            entry, parts = advance(firsts.pop(0), token, lists_now)
-            seconds.append(entry)
-            after += parts
-        leave, stay, token = quarter(step - 1, [images, twin_images], both, bands, after=after)
-        token = token[0, 0]
-    known = jnp.concatenate([known] + neighbour, axis=1)
-    while firsts or seconds:
-        entry = seconds.pop(0)
-        result = forward(entry[0], finish(entry, token))
-        if firsts:
-            seconds.append(advance(firsts.pop(0), token)[0])
-    reach = 4
+        if n == 1:
+            known = add_lists([entries[0][2]])
+            after += send_on(None, entries[0], after, None, known)[0]
+        elif n > 1:
+            done, lists_now = entries[n - 2], None
+            if n < 4:
+                known = lists_now = add_lists(done[3] if n == 2 else carried[done[0]][:1])
+            after += send_on(done, entries[n - 1], after, lists_now)[0]
+        if step:
+            leave, stay, _ = quarter(step - 1, [images, twin_images], both, bands, after=after)
+    done, entry = entries[-2:]
+    sums, _ = merge(stripe, [own_job(done, carried.get(done[0], []))])
+    moved[done[0]] = forward(done[0], sums[0])
+    _, token = send_on(None, entry, sums)
+    known = add_lists([moved[depth - 2]]) + token.astype(jnp.bfloat16)
+    reach = 8
     while reach < patch_count:
         known = jnp.concatenate([known, swap(known, lambda e, p, r=reach: (e, p ^ r))], axis=1)
         reach *= 2
+
+    base, row, addends, _ = own_job(entries[-1], carried[0])
+    result = base[row : row + stripe]
+    for value, start in addends:
+        if value is addends[-1][0]:
+            result = lax.optimization_barrier(result)
+        result = result + value[start : start + stripe].astype(jnp.float32)
 
     places = known[:4].astype(jnp.int32)
     top = places[0] * LANES + places[1] - MARGIN

time: 128 us -> 123 us (0.961)
  Pallas kernels: 52.5 us -> 64.8 us
  other arithmetic: 19.5 us -> 7.3 us
  local copies, waits for them, and re-layouts: 6.75 us -> 3.81 us
  starting transfers between devices: 21.6 us -> 19.4 us
    pallas_call x0 -> x5, Pallas kernels: none -> 15.2 us  [merge(): pl.pallas_call(kernel, out_shape=shapes + [jax.ShapeDtypeStruct((1, 1), j...]
    convert_element_type x11 -> x5, other arithmetic: 14.7 us -> 0.83 us  [digits(): part.astype(jnp.bfloat16)]
    pallas_call x5, Pallas kernels: 52.5 us -> 49.6 us  [make_quarter(): pl.pallas_call(functools.partial(quarter_kernel, geom, step, sources, has...]
    squeeze x4 -> x0, local copies, waits for them, and re-layouts: 2.26 us -> none  [unpack(): return (ids[:1], ids[1:3], ids[3], known[4])]
    ppermute x14, starting transfers between devices: 21.6 us -> 19.4 us  [swap(): return lax.ppermute(value, ('expo', 'patch'), route)]
    broadcast_in_dim x1, other arithmetic: 3.12 us -> 1.25 us  [on_device(): return (coadd_map[None], weight_map[None])]
    concatenate x7 -> x3, other arithmetic: 0.4 us -> 2.19 us  [the longest x2 1.5 us: add_lists(): jnp.concatenate([known] + [known_in(v, known.shape[1]) for v in values],...]
    add x0 -> x2, other arithmetic: none -> 1.66 us  [the longest x1 1.65 us: on_device(): result = result + value[start:start + stripe].astype(jnp.float32)]
  transfers between devices with their start and end apart: 14 -> 14, of which waited for: 5 -> 5; matrix products, arithmetic and copies ran while one was open for 17% -> 8% of each run, Pallas kernels for 34% -> 44%
where the time goes in v3:
time: 123 us; the launch traced here: 122 us
  Pallas kernels  64.8 us (53%)
  waiting for transfers between devices  24.8 us (20%)
  starting transfers between devices  19.4 us (16%)
  other arithmetic  7.3 us (6%)
  local copies, waits for them, and re-layouts  3.81 us (3%)
  between operations  1.51 us (1%)
    pallas_call x5, Pallas kernels, make_quarter(): pl.pallas_call(functools.partial(quarter_kernel, geom, step, sources, has...  49.6 us
    ppermute x14, waiting for transfers between devices, swap(): return lax.ppermute(value, ('expo', 'patch'), route)  24.8 us
    ppermute x14, starting transfers between devices, swap(): return lax.ppermute(value, ('expo', 'patch'), route)  19.4 us
    pallas_call x5, Pallas kernels, merge(): pl.pallas_call(kernel, out_shape=shapes + [jax.ShapeDtypeStruct((1, 1), j...  15.2 us
  transfers between devices with their start and end apart: 14, of which 5 were waited for; matrix products, arithmetic and copies ran while one was open for 8% of the time, Pallas kernels for 44%

profile of v3, /device:TPU:0, one launch (start us, length us, event | category | flops | bytes accessed | tf_op | source)
XLA Modules:
  0.0 122.4 jit_solution(10878509459672174569)
XLA Ops:
  4.5 9.6 %shard_map.95 = (f32[16,512,128]{2,1,0:T(8,128)}, f32[1,1]{1,0:T(1,128)}) custom-call(f32[3,189]{1,0:T(4,128)} %bitcast.35, s32[3,12]{1,0:T(4,128)} %copy-done.5, f32[12]{0:T(128)} %copy-done.7, bf16[12,512,512]{2,1,0:T(8,128)(2,1)} %refs_5_.7, bf16[432,176]{1,0:T(8,128)(2,1)} %constant.132.clone.refs_4_.refs_7_, ...), custom_call_target="tpu_custom_call" | custom-call | flops 1048576 | bytes 1048576 | tf_op jit(solution)/shard_map/pallas_call | solution.py:377
  15.0 10.5 %shard_map.96 = (bf16[528,1024]{1,0:T(8,128)(2,1)}, f32[512,1024]{1,0:T(8,128)}, f32[1,1]{1,0:T(1,128)}) custom-call(f32[3,189]{1,0:T(4,128)} %bitcast.36, s32[3,12]{1,0:T(4,128)} %copy-done.6, f32[12]{0:T(128)} %copy-done.8, bf16[12,512,512]{2,1,0:T(8,128)(2,1)} %collective-permute-done.2.refs_3_.refs_6_, bf16[432,176]{1,0:T(8,128)(2,1)} %constant.132.clone.refs_4_.refs_7_, ...), custom_call_target="tpu_custom_call" | custom-call | flops 1048576 | bytes 1048576 | tf_op jit(solution)/shard_map/pallas_call | solution.py:377
  25.5 1.7 %collective-permute-start.3 = (bf16[528,1024]{1,0:T(8,128)(2,1)}, bf16[528,1024]{1,0:T(8,128)(2,1)}, u32[]{:S(2)}, u32[]{:S(2)}) collective-permute-start(bf16[528,1024]{1,0:T(8,128)(2,1)} %get-tuple-element.20.refs_9_), channel_id=1, source_target_pairs={{0,1},{1,0},{2,3},{3,2},{4,5},{5,4},{6,7},{7,6},{8,24},{9,25},{10,... | collective-permute-start | bytes 3244040 | tf_op jit(solution)/shard_map/ppermute | solution.py:505
  27.2 9.9 %shard_map.97 = (bf16[512,1024]{1,0:T(8,128)(2,1)}, f32[512,1024]{1,0:T(8,128)}, f32[1,1]{1,0:T(1,128)}) custom-call(f32[3,189]{1,0:T(4,128)} %bitcast.37, s32[3,12]{1,0:T(4,128)} %copy-done.5, f32[12]{0:T(128)} %copy-done.7, s32[3,12]{1,0:T(4,128)} %copy-done.6, f32[12]{0:T(128)} %copy-done.8, bf16[12,512,512]{2,1,0:T(8,128)(2,1)} %refs_5_.7, ...), custom_call_target="tpu_custom_call" | custom-call | flops 1048576 | bytes 1048576 | tf_op jit(solution)/shard_map/pallas_call | solution.py:377
  37.1 1.4 %collective-permute-start.5 = (bf16[512,1024]{1,0:T(8,128)(2,1)}, bf16[512,1024]{1,0:T(8,128)(2,1)}, u32[]{:S(2)}, u32[]{:S(2)}) collective-permute-start(bf16[512,1024]{1,0:T(8,128)(2,1)} %get-tuple-element.21.refs_3_.refs_9_), channel_id=1, source_target_pairs={{0,1},{1,0},{2,3},{3,2},{4,5},{5,4},{6,7},{7,6},{8,24},{9,25},{10,... | collective-permute-start | bytes 3145736 | tf_op jit(solution)/shard_map/ppermute | solution.py:505
  38.5 2.5 %collective-permute-done.3.refs_1_ = bf16[528,1024]{1,0:T(8,128)(2,1)} collective-permute-done((bf16[528,1024]{1,0:T(8,128)(2,1)}, bf16[528,1024]{1,0:T(8,128)(2,1)}, u32[]{:S(2)}, u32[]{:S(2)}) %collective-permute-start.3) | collective-permute-done | bytes 1081376 | tf_op jit(solution)/shard_map/ppermute | solution.py:505
  42.4 2.7 %shard_map.98 = (bf16[272,1024]{1,0:T(8,128)(2,1)}, f32[1,1]{1,0:T(1,128)}) custom-call(f32[512,1024]{1,0:T(8,128)} %get-tuple-element.22.refs_0_, bf16[528,1024]{1,0:T(8,128)(2,1)} %collective-permute-done.3.refs_1_, bf16[16,1024]{1,0:T(8,128)(2,1)} %fusion.29.refs_2_, bf16[512,1024]{1,0:T(8,128)(2,1)} %get-tuple-element.21.refs_3_.refs_9_), custom_call_target="tpu_custom_call" | custom-call | tf_op jit(solution)/shard_map/pallas_call | solution.py:472
  45.1 2.7 %collective-permute-start.4 = (bf16[272,1024]{1,0:T(8,128)(2,1)}, bf16[272,1024]{1,0:T(8,128)(2,1)S(1)}, u32[]{:S(2)}, u32[]{:S(2)}) collective-permute-start(bf16[272,1024]{1,0:T(8,128)(2,1)} %get-tuple-element.23.refs_10_), channel_id=1, source_target_pairs={{0,16},{1,17},{2,18},{3,19},{4,20},{5,21},{6,22},{7,23},{8,9},{9,8... | collective-permute-start | bytes 1671176 | tf_op jit(solution)/shard_map/ppermute | solution.py:505
  47.8 9.7 %shard_map.99 = (bf16[512,1024]{1,0:T(8,128)(2,1)}, f32[512,1024]{1,0:T(8,128)}, f32[1,1]{1,0:T(1,128)}) custom-call(f32[3,189]{1,0:T(4,128)} %bitcast.38, s32[3,12]{1,0:T(4,128)} %copy-done.5, f32[12]{0:T(128)} %copy-done.7, s32[3,12]{1,0:T(4,128)} %copy-done.6, f32[12]{0:T(128)} %copy-done.8, bf16[12,512,512]{2,1,0:T(8,128)(2,1)} %refs_5_.7, ...), custom_call_target="tpu_custom_call" | custom-call | flops 1048576 | bytes 1048576 | tf_op jit(solution)/shard_map/pallas_call | solution.py:377
  58.6 3.4 %shard_map.100 = (bf16[272,1024]{1,0:T(8,128)(2,1)}, bf16[256,1024]{1,0:T(8,128)(2,1)}, f32[1,1]{1,0:T(1,128)}) custom-call(f32[512,1024]{1,0:T(8,128)} %get-tuple-element.22.refs_0_, bf16[528,1024]{1,0:T(8,128)(2,1)} %collective-permute-done.3.refs_1_, bf16[272,1024]{1,0:T(8,128)(2,1)} %copy-done.3, bf16[16,1024]{1,0:T(8,128)(2,1)} %fusion.32.refs_3_, ...), custom_call_target="tpu_custom_call" | custom-call | tf_op jit(solution)/shard_map/pallas_call | solution.py:472
  62.0 2.4 %collective-permute-start.9 = (bf16[272,1024]{1,0:T(8,128)(2,1)}, bf16[272,1024]{1,0:T(8,128)(2,1)S(1)}, u32[]{:S(2)}, u32[]{:S(2)}) collective-permute-start(bf16[272,1024]{1,0:T(8,128)(2,1)} %get-tuple-element.26.refs_10_), channel_id=1, source_target_pairs={{0,2},{1,3},{2,0},{3,1},{4,6},{5,7},{6,4},{7,5},{8,10},{9,11},{10,... | collective-permute-start | bytes 1671176 | tf_op jit(solution)/shard_map/ppermute | solution.py:505
  64.4 2.8 %collective-permute-start.8 = (bf16[256,1024]{1,0:T(8,128)(2,1)}, bf16[256,1024]{1,0:T(8,128)(2,1)}, u32[]{:S(2)}, u32[]{:S(2)}) collective-permute-start(bf16[256,1024]{1,0:T(8,128)(2,1)} %get-tuple-element.27.refs_11_), channel_id=1, source_target_pairs={{0,16},{1,17},{2,18},{3,19},{4,20},{5,21},{6,22},{7,23},{8,9},{9,8... | collective-permute-start | bytes 1572872 | tf_op jit(solution)/shard_map/ppermute | solution.py:505
  67.2 10.0 %shard_map.101 = (bf16[512,1024]{1,0:T(8,128)(2,1)}, f32[512,1024]{1,0:T(8,128)}, f32[1,1]{1,0:T(1,128)}) custom-call(f32[3,189]{1,0:T(4,128)} %bitcast.39, s32[3,12]{1,0:T(4,128)} %copy-done.5, f32[12]{0:T(128)} %copy-done.7, s32[3,12]{1,0:T(4,128)} %copy-done.6, f32[12]{0:T(128)} %copy-done.8, bf16[12,512,512]{2,1,0:T(8,128)(2,1)} %refs_5_.7, ...), custom_call_target="tpu_custom_call" | custom-call | flops 1048576 | bytes 1048576 | tf_op jit(solution)/shard_map/pallas_call | solution.py:377
  77.2 2.1 %collective-permute-start.6 = (bf16[512,1024]{1,0:T(8,128)(2,1)}, bf16[512,1024]{1,0:T(8,128)(2,1)}, u32[]{:S(2)}, u32[]{:S(2)}) collective-permute-start(bf16[512,1024]{1,0:T(8,128)(2,1)} %get-tuple-element.29.refs_7_), channel_id=1, source_target_pairs={{0,1},{1,0},{2,3},{3,2},{4,5},{5,4},{6,7},{7,6},{8,24},{9,25},{10,... | collective-permute-start | bytes 3145736 | tf_op jit(solution)/shard_map/ppermute | solution.py:505
  80.1 3.6 %shard_map.102 = (bf16[272,1024]{1,0:T(8,128)(2,1)}, bf16[256,1024]{1,0:T(8,128)(2,1)}, f32[1,1]{1,0:T(1,128)}) custom-call(f32[512,1024]{1,0:T(8,128)} %get-tuple-element.25.refs_4_.refs_0_, bf16[512,1024]{1,0:T(8,128)(2,1)} %collective-permute-done.5.refs_5_.refs_1_, bf16[256,1024]{1,0:T(8,128)(2,1)} %collective-permute-done.8.refs_2_, ...), custom_call_target="tpu_custom_call" | custom-call | tf_op jit(solution)/shard_map/pallas_call | solution.py:472
  83.7 1.4 %collective-permute-start.12 = (bf16[272,1024]{1,0:T(8,128)(2,1)}, bf16[272,1024]{1,0:T(8,128)(2,1)}, u32[]{:S(2)}, u32[]{:S(2)}) collective-permute-start(bf16[272,1024]{1,0:T(8,128)(2,1)} %get-tuple-element.34), channel_id=1, source_target_pairs={{0,4},{1,5},{2,6},{3,7},{4,0},{5,1},{6,2},{7,3},{8,12},{9,13},{10,... | collective-permute-start | bytes 1671176 | tf_op jit(solution)/shard_map/ppermute | solution.py:505
  85.1 1.6 %collective-permute-start.10 = (bf16[256,1024]{1,0:T(8,128)(2,1)}, bf16[256,1024]{1,0:T(8,128)(2,1)S(1)}, u32[]{:S(2)}, u32[]{:S(2)}) collective-permute-start(bf16[256,1024]{1,0:T(8,128)(2,1)} %get-tuple-element.31), channel_id=1, source_target_pairs={{0,16},{1,17},{2,18},{3,19},{4,20},{5,21},{6,22},{7,23},{8,9},{9,8... | collective-permute-start | bytes 1572872 | tf_op jit(solution)/shard_map/ppermute | solution.py:505
  86.7 9.9 %collective-permute-done.10.refs_2_ = bf16[256,1024]{1,0:T(8,128)(2,1)S(1)} collective-permute-done((bf16[256,1024]{1,0:T(8,128)(2,1)}, bf16[256,1024]{1,0:T(8,128)(2,1)S(1)}, u32[]{:S(2)}, u32[]{:S(2)}) %collective-permute-start.10) | collective-permute-done | bytes 524320 | tf_op jit(solution)/shard_map/ppermute | solution.py:505
  97.3 2.9 %shard_map.103 = (bf16[256,1024]{1,0:T(8,128)(2,1)}, f32[1,1]{1,0:T(1,128)}) custom-call(f32[512,1024]{1,0:T(8,128)} %get-tuple-element.30.refs_5_.refs_0_, bf16[512,1024]{1,0:T(8,128)(2,1)} %collective-permute-done.7.refs_6_.refs_1_, bf16[256,1024]{1,0:T(8,128)(2,1)} %copy-done.4), custom_call_target="tpu_custom_call" | custom-call | tf_op jit(solution)/shard_map/pallas_call | solution.py:472
  100.3 2.7 %shard_map.104 = (bf16[256,1024]{1,0:T(8,128)(2,1)}, f32[1,1]{1,0:T(1,128)}) custom-call(f32[512,1024]{1,0:T(8,128)} %get-tuple-element.28.refs_0_, bf16[512,1024]{1,0:T(8,128)(2,1)} %collective-permute-done.6.refs_1_, bf16[256,1024]{1,0:T(8,128)(2,1)} %get-tuple-element.32.refs_2_), custom_call_target="tpu_custom_call" | custom-call | tf_op jit(solution)/shard_map/pallas_call | solution.py:472
  103.0 1.8 %collective-permute-start.11 = (bf16[256,1024]{1,0:T(8,128)(2,1)}, bf16[256,1024]{1,0:T(8,128)(2,1)}, u32[]{:S(2)}, u32[]{:S(2)}) collective-permute-start(bf16[256,1024]{1,0:T(8,128)(2,1)} %get-tuple-element.33), channel_id=1, source_target_pairs={{0,16},{1,17},{2,18},{3,19},{4,20},{5,21},{6,22},{7,23},{8,9},{9,8... | collective-permute-start | bytes 1572872 | tf_op jit(solution)/shard_map/ppermute | solution.py:505
  105.5 4.7 %collective-permute-done.12 = bf16[272,1024]{1,0:T(8,128)(2,1)} collective-permute-done((bf16[272,1024]{1,0:T(8,128)(2,1)}, bf16[272,1024]{1,0:T(8,128)(2,1)}, u32[]{:S(2)}, u32[]{:S(2)}) %collective-permute-start.12) | collective-permute-done | bytes 557088 | tf_op jit(solution)/shard_map/ppermute | solution.py:505
  112.6 1.6 %convert_add_fusion = f32[256,1024]{1,0:T(8,128)S(1)} fusion(bf16[256,1024]{1,0:T(8,128)(2,1)} %collective-permute-done.11, f32[512,1024]{1,0:T(8,128)S(1)} %copy-done, bf16[272,1024]{1,0:T(8,128)(2,1)} %collective-permute-done.12, bf16[512,1024]{1,0:T(8,128)(2,1)} %collective-permute-done.6.refs_1_), kind=kLoop, calls=%fused_computation.5 | loop fusion | flops 1572864 | bytes 3670016 | tf_op jit(solution)/shard_map/add | solution.py:629
  114.2 6.9 %collective-permute-done.13 = bf16[256,1024]{1,0:T(8,128)(2,1)S(1)} collective-permute-done((bf16[256,1024]{1,0:T(8,128)(2,1)}, bf16[256,1024]{1,0:T(8,128)(2,1)S(1)}, u32[]{:S(2)}, u32[]{:S(2)}) %collective-permute-start.13) | collective-permute-done | bytes 524320 | tf_op jit(solution)/shard_map/ppermute | solution.py:505
  (61 shorter events, 12.6 us)
Async XLA Ops:
  0.6 14.4 %collective-permute-start.2 = (bf16[12,512,512]{2,1,0:T(8,128)(2,1)}, bf16[12,512,512]{2,1,0:T(8,128)(2,1)}, u32[]{:S(2)}, u32[]{:S(2)}) collective-permute-start(bf16[12,512,512]{2,1,0:T(8,128)(2,1)} %refs_5_.7), channel_id=1, source_target_pairs={{0,8},{1,9},{2,10},{3,11},{4,12},{5,13},{6,14},{7,15},{8,0},{9,1},... | collective-permute-start | bytes 18874376 | tf_op jit(solution)/shard_map/ppermute | solution.py:505
  2.6 1.9 %copy-start.5 = (s32[3,12]{1,0:T(4,128)}, s32[3,12]{1,0:T(4,128)S(1)}, u32[]{:S(2)}) copy-start(s32[3,12]{1,0:T(4,128)S(1)} %pad_add_fusion.refs_1_) | copy-start | bytes 436
  2.6 11.6 %collective-permute-start = (s32[3,12]{1,0:T(4,128)S(1)}, s32[3,12]{1,0:T(4,128)S(1)}, u32[]{:S(2)}, u32[]{:S(2)}) collective-permute-start(s32[3,12]{1,0:T(4,128)S(1)} %pad_add_fusion.refs_1_), channel_id=1, source_target_pairs={{0,8},{1,9},{2,10},{3,11},{4,12},{5,13},{6,14},{7,15},{8,0},{9,1},... | collective-permute-start | bytes 440 | tf_op jit(solution)/shard_map/ppermute | solution.py:505
  3.4 1.2 copy-start.7
  3.4 10.8 %collective-permute-start.1 = (f32[12]{0:T(128)S(1)}, f32[12]{0:T(128)S(1)}, u32[]{:S(2)}, u32[]{:S(2)}) collective-permute-start(f32[12]{0:T(128)S(1)} %convert_element_type.95.refs_2_), channel_id=1, source_target_pairs={{0,8},{1,9},{2,10},{3,11},{4,12},{5,13},{6,14},{7,15},{8,0},{9,1},... | collective-permute-start | bytes 152 | tf_op jit(solution)/shard_map/ppermute | solution.py:505
  14.2 0.8 copy-start.8
  14.2 0.8 copy-start.6
  25.5 15.5 %collective-permute-start.3 = (bf16[528,1024]{1,0:T(8,128)(2,1)}, bf16[528,1024]{1,0:T(8,128)(2,1)}, u32[]{:S(2)}, u32[]{:S(2)}) collective-permute-start(bf16[528,1024]{1,0:T(8,128)(2,1)} %get-tuple-element.20.refs_9_), channel_id=1, source_target_pairs={{0,1},{1,0},{2,3},{3,2},{4,5},{5,4},{6,7},{7,6},{8,24},{9,25},{10,... | collective-permute-start | bytes 3244040 | tf_op jit(solution)/shard_map/ppermute | solution.py:505
  37.1 21.5 %collective-permute-start.5 = (bf16[512,1024]{1,0:T(8,128)(2,1)}, bf16[512,1024]{1,0:T(8,128)(2,1)}, u32[]{:S(2)}, u32[]{:S(2)}) collective-permute-start(bf16[512,1024]{1,0:T(8,128)(2,1)} %get-tuple-element.21.refs_3_.refs_9_), channel_id=1, source_target_pairs={{0,1},{1,0},{2,3},{3,2},{4,5},{5,4},{6,7},{7,6},{8,24},{9,25},{10,... | collective-permute-start | bytes 3145736 | tf_op jit(solution)/shard_map/ppermute | solution.py:505
  45.1 12.7 %collective-permute-start.4 = (bf16[272,1024]{1,0:T(8,128)(2,1)}, bf16[272,1024]{1,0:T(8,128)(2,1)S(1)}, u32[]{:S(2)}, u32[]{:S(2)}) collective-permute-start(bf16[272,1024]{1,0:T(8,128)(2,1)} %get-tuple-element.23.refs_10_), channel_id=1, source_target_pairs={{0,16},{1,17},{2,18},{3,19},{4,20},{5,21},{6,22},{7,23},{8,9},{9,8... | collective-permute-start | bytes 1671176 | tf_op jit(solution)/shard_map/ppermute | solution.py:505
  57.5 22.6 %collective-permute-start.7 = (bf16[512,1024]{1,0:T(8,128)(2,1)}, bf16[512,1024]{1,0:T(8,128)(2,1)}, u32[]{:S(2)}, u32[]{:S(2)}) collective-permute-start(bf16[512,1024]{1,0:T(8,128)(2,1)} %get-tuple-element.24.refs_6_.refs_9_), channel_id=1, source_target_pairs={{0,1},{1,0},{2,3},{3,2},{4,5},{5,4},{6,7},{7,6},{8,24},{9,25},{10,... | collective-permute-start | bytes 3145736 | tf_op jit(solution)/shard_map/ppermute | solution.py:505
  57.8 0.8 copy-start.3
  62.0 17.3 %collective-permute-start.9 = (bf16[272,1024]{1,0:T(8,128)(2,1)}, bf16[272,1024]{1,0:T(8,128)(2,1)S(1)}, u32[]{:S(2)}, u32[]{:S(2)}) collective-permute-start(bf16[272,1024]{1,0:T(8,128)(2,1)} %get-tuple-element.26.refs_10_), channel_id=1, source_target_pairs={{0,2},{1,3},{2,0},{3,1},{4,6},{5,7},{6,4},{7,5},{8,10},{9,11},{10,... | collective-permute-start | bytes 1671176 | tf_op jit(solution)/shard_map/ppermute | solution.py:505
  64.4 15.7 %collective-permute-start.8 = (bf16[256,1024]{1,0:T(8,128)(2,1)}, bf16[256,1024]{1,0:T(8,128)(2,1)}, u32[]{:S(2)}, u32[]{:S(2)}) collective-permute-start(bf16[256,1024]{1,0:T(8,128)(2,1)} %get-tuple-element.27.refs_11_), channel_id=1, source_target_pairs={{0,16},{1,17},{2,18},{3,19},{4,20},{5,21},{6,22},{7,23},{8,9},{9,8... | collective-permute-start | bytes 1572872 | tf_op jit(solution)/shard_map/ppermute | solution.py:505
  77.2 23.2 %collective-permute-start.6 = (bf16[512,1024]{1,0:T(8,128)(2,1)}, bf16[512,1024]{1,0:T(8,128)(2,1)}, u32[]{:S(2)}, u32[]{:S(2)}) collective-permute-start(bf16[512,1024]{1,0:T(8,128)(2,1)} %get-tuple-element.29.refs_7_), channel_id=1, source_target_pairs={{0,1},{1,0},{2,3},{3,2},{4,5},{5,4},{6,7},{7,6},{8,24},{9,25},{10,... | collective-permute-start | bytes 3145736 | tf_op jit(solution)/shard_map/ppermute | solution.py:505
  79.3 0.8 copy-start.2
  83.7 26.5 %collective-permute-start.12 = (bf16[272,1024]{1,0:T(8,128)(2,1)}, bf16[272,1024]{1,0:T(8,128)(2,1)}, u32[]{:S(2)}, u32[]{:S(2)}) collective-permute-start(bf16[272,1024]{1,0:T(8,128)(2,1)} %get-tuple-element.34), channel_id=1, source_target_pairs={{0,4},{1,5},{2,6},{3,7},{4,0},{5,1},{6,2},{7,3},{8,12},{9,13},{10,... | collective-permute-start | bytes 1671176 | tf_op jit(solution)/shard_map/ppermute | solution.py:505
  85.1 11.5 %collective-permute-start.10 = (bf16[256,1024]{1,0:T(8,128)(2,1)}, bf16[256,1024]{1,0:T(8,128)(2,1)S(1)}, u32[]{:S(2)}, u32[]{:S(2)}) collective-permute-start(bf16[256,1024]{1,0:T(8,128)(2,1)} %get-tuple-element.31), channel_id=1, source_target_pairs={{0,16},{1,17},{2,18},{3,19},{4,20},{5,21},{6,22},{7,23},{8,9},{9,8... | collective-permute-start | bytes 1572872 | tf_op jit(solution)/shard_map/ppermute | solution.py:505
  96.5 0.8 copy-start.4
  100.2 20.9 %collective-permute-start.13 = (bf16[256,1024]{1,0:T(8,128)(2,1)}, bf16[256,1024]{1,0:T(8,128)(2,1)S(1)}, u32[]{:S(2)}, u32[]{:S(2)}) collective-permute-start(bf16[256,1024]{1,0:T(8,128)(2,1)} %get-tuple-element.32.refs_2_), channel_id=1, source_target_pairs={{0,2},{1,3},{2,0},{3,1},{4,6},{5,7},{6,4},{7,5},{8,10},{9,11},{10,... | collective-permute-start | bytes 1572872 | tf_op jit(solution)/shard_map/ppermute | solution.py:505
  103.0 9.6 %copy-start = (f32[512,1024]{1,0:T(8,128)S(1)}, f32[512,1024]{1,0:T(8,128)}, u32[]{:S(2)}) copy-start(f32[512,1024]{1,0:T(8,128)} %get-tuple-element.28.refs_0_) | copy-start | bytes 6291460
  103.0 9.6 %collective-permute-start.11 = (bf16[256,1024]{1,0:T(8,128)(2,1)}, bf16[256,1024]{1,0:T(8,128)(2,1)}, u32[]{:S(2)}, u32[]{:S(2)}) collective-permute-start(bf16[256,1024]{1,0:T(8,128)(2,1)} %get-tuple-element.33), channel_id=1, source_target_pairs={{0,16},{1,17},{2,18},{3,19},{4,20},{5,21},{6,22},{7,23},{8,9},{9,8... | collective-permute-start | bytes 1572872 | tf_op jit(solution)/shard_map/ppermute | solution.py:505
  111.8 10.6 %copy-start.1 = (f32[256,1024]{1,0:T(8,128)}, f32[256,1024]{1,0:T(8,128)S(1)}, u32[]{:S(2)}) copy-start(f32[256,1024]{1,0:T(8,128)S(1)} %fusion.1) | copy-start | bytes 3145732

commit v4 on v3

--- a/solution.py
+++ b/solution.py
@@ -368,7 +368,7 @@
     if split:
         out_shape = [
             jax.ShapeDtypeStruct((rows + extra, SIDE), jnp.bfloat16),
-            jax.ShapeDtypeStruct((rows, SIDE), jnp.float32),
+            jax.ShapeDtypeStruct((rows, SIDE), jnp.bfloat16),
         ]
     else:
         out_shape = [jax.ShapeDtypeStruct((QUARTER_COLS, rows, LANES), jnp.float32)]
@@ -451,7 +451,7 @@
                 for copy in copies[n][h]:
                     copy.wait()
                 rows = pl.ds(h * size, size)
-                total = wide[n, rows, :]
+                total = wide[n, rows, :].astype(jnp.float32)
                 for m in range(len(starts)):
                     total = total + narrow[where + m, rows, :].astype(jnp.float32)
                 staged[n, rows, :] = total.astype(jnp.bfloat16)
@@ -475,7 +475,7 @@
         in_specs=[hbm] * (len(operands) + len(after)),
         out_specs=[hbm] * len(shapes) + [pl.BlockSpec(memory_space=pltpu.SMEM)],
         scratch_shapes=[
-            pltpu.VMEM((len(jobs), stripe, SIDE), jnp.float32),
+            pltpu.VMEM((len(jobs), stripe, SIDE), jobs[0][0].dtype),
             pltpu.VMEM((count - len(jobs), stripe, SIDE), jnp.bfloat16),
             pltpu.VMEM((len(jobs), stripe, SIDE), jnp.bfloat16),
             pltpu.SemaphoreType.DMA((count, halves)),
@@ -622,7 +622,7 @@
         reach *= 2
 
     base, row, addends, _ = own_job(entries[-1], carried[0])
-    result = base[row : row + stripe]
+    result = base[row : row + stripe].astype(jnp.float32)
     for value, start in addends:
         if value is addends[-1][0]:
             result = lax.optimization_barrier(result)

time: 123 us -> 122 us (level)
  starting transfers between devices: 19.4 us -> 13.5 us
  waiting for transfers between devices: 24.8 us -> 30.4 us
  Pallas kernels: 64.8 us -> 63.4 us
    ppermute x14, starting transfers between devices: 19.4 us -> 13.5 us  [swap(): return lax.ppermute(value, ('expo', 'patch'), route)]
    ppermute x14, waiting for transfers between devices: 24.8 us -> 30.4 us  [swap(): return lax.ppermute(value, ('expo', 'patch'), route)]
  transfers between devices with their start and end apart: 14 -> 14, of which waited for: 5 -> 7; matrix products, arithmetic and copies ran while one was open for 8% -> 8% of each run, Pallas kernels for 44% -> 45%
where the time goes in v4:
time: 122 us; the launch traced here: 121 us
  Pallas kernels  63.4 us (52%)
  waiting for transfers between devices  30.4 us (25%)
  starting transfers between devices  13.5 us (11%)
  other arithmetic  7.14 us (6%)
  local copies, waits for them, and re-layouts  3.85 us (3%)
  between operations  1.53 us (1%)
    pallas_call x5, Pallas kernels, make_quarter(): pl.pallas_call(functools.partial(quarter_kernel, geom, step, sources, has...  49.1 us
    ppermute x14, waiting for transfers between devices, swap(): return lax.ppermute(value, ('expo', 'patch'), route)  30.4 us
    pallas_call x5, Pallas kernels, merge(): pl.pallas_call(kernel, out_shape=shapes + [jax.ShapeDtypeStruct((1, 1), j...  14.3 us
    ppermute x14, starting transfers between devices, swap(): return lax.ppermute(value, ('expo', 'patch'), route)  13.5 us
  transfers between devices with their start and end apart: 14, of which 7 were waited for; matrix products, arithmetic and copies ran while one was open for 8% of the time, Pallas kernels for 45%

profile of v4, /device:TPU:0, one launch (start us, length us, event | category | flops | bytes accessed | tf_op | source)
XLA Modules:
  0.0 120.6 jit_solution(5031995124898430863)
XLA Ops:
  4.5 8.4 %shard_map.95 = (f32[16,512,128]{2,1,0:T(8,128)}, f32[1,1]{1,0:T(1,128)}) custom-call(f32[3,189]{1,0:T(4,128)} %bitcast.35, s32[3,12]{1,0:T(4,128)} %copy-done.5, f32[12]{0:T(128)} %copy-done.7, bf16[12,512,512]{2,1,0:T(8,128)(2,1)} %refs_5_.7, bf16[432,176]{1,0:T(8,128)(2,1)} %constant.132.clone.refs_4_.refs_7_, ...), custom_call_target="tpu_custom_call" | custom-call | flops 1048576 | bytes 1048576 | tf_op jit(solution)/shard_map/pallas_call | solution.py:377
  13.8 9.2 %shard_map.96 = (bf16[528,1024]{1,0:T(8,128)(2,1)}, bf16[512,1024]{1,0:T(8,128)(2,1)}, f32[1,1]{1,0:T(1,128)}) custom-call(f32[3,189]{1,0:T(4,128)} %bitcast.36, s32[3,12]{1,0:T(4,128)} %copy-done.6, f32[12]{0:T(128)} %copy-done.8, bf16[12,512,512]{2,1,0:T(8,128)(2,1)} %collective-permute-done.2.refs_3_.refs_6_, ...), custom_call_target="tpu_custom_call" | custom-call | flops 1048576 | bytes 1048576 | tf_op jit(solution)/shard_map/pallas_call | solution.py:377
  23.0 2.9 %collective-permute-start.3 = (bf16[528,1024]{1,0:T(8,128)(2,1)}, bf16[528,1024]{1,0:T(8,128)(2,1)}, u32[]{:S(2)}, u32[]{:S(2)}) collective-permute-start(bf16[528,1024]{1,0:T(8,128)(2,1)} %get-tuple-element.20.refs_9_), channel_id=1, source_target_pairs={{0,1},{1,0},{2,3},{3,2},{4,5},{5,4},{6,7},{7,6},{8,24},{9,25},{10,... | collective-permute-start | bytes 3244040 | tf_op jit(solution)/shard_map/ppermute | solution.py:505
  25.9 11.2 %shard_map.97 = (bf16[512,1024]{1,0:T(8,128)(2,1)}, bf16[512,1024]{1,0:T(8,128)(2,1)}, f32[1,1]{1,0:T(1,128)}) custom-call(f32[3,189]{1,0:T(4,128)} %bitcast.37, s32[3,12]{1,0:T(4,128)} %copy-done.5, f32[12]{0:T(128)} %copy-done.7, s32[3,12]{1,0:T(4,128)} %copy-done.6, f32[12]{0:T(128)} %copy-done.8, bf16[12,512,512]{2,1,0:T(8,128)(2,1)} %refs_5_.7, ...), custom_call_target="tpu_custom_call" | custom-call | flops 1048576 | bytes 1048576 | tf_op jit(solution)/shard_map/pallas_call | solution.py:377
  37.1 0.9 collective-permute-start.5
  38.0 1.3 %collective-permute-done.3.refs_1_ = bf16[528,1024]{1,0:T(8,128)(2,1)} collective-permute-done((bf16[528,1024]{1,0:T(8,128)(2,1)}, bf16[528,1024]{1,0:T(8,128)(2,1)}, u32[]{:S(2)}, u32[]{:S(2)}) %collective-permute-start.3) | collective-permute-done | bytes 1081376 | tf_op jit(solution)/shard_map/ppermute | solution.py:505
  40.7 2.7 %shard_map.98 = (bf16[272,1024]{1,0:T(8,128)(2,1)}, f32[1,1]{1,0:T(1,128)}) custom-call(bf16[512,1024]{1,0:T(8,128)(2,1)} %get-tuple-element.22.refs_0_, bf16[528,1024]{1,0:T(8,128)(2,1)} %collective-permute-done.3.refs_1_, bf16[16,1024]{1,0:T(8,128)(2,1)} %fusion.29.refs_2_, bf16[512,1024]{1,0:T(8,128)(2,1)} %get-tuple-element.21.refs_3_.refs_9_), custom_call_target="tpu_custom_call" | custom-call | tf_op jit(solution)/shard_map/pallas_call | solution.py:472
  43.8 9.8 %shard_map.99 = (bf16[512,1024]{1,0:T(8,128)(2,1)}, bf16[512,1024]{1,0:T(8,128)(2,1)}, f32[1,1]{1,0:T(1,128)}) custom-call(f32[3,189]{1,0:T(4,128)} %bitcast.38, s32[3,12]{1,0:T(4,128)} %copy-done.5, f32[12]{0:T(128)} %copy-done.7, s32[3,12]{1,0:T(4,128)} %copy-done.6, f32[12]{0:T(128)} %copy-done.8, bf16[12,512,512]{2,1,0:T(8,128)(2,1)} %refs_5_.7, ...), custom_call_target="tpu_custom_call" | custom-call | flops 1048576 | bytes 1048576 | tf_op jit(solution)/shard_map/pallas_call | solution.py:377
  53.6 1.8 %collective-permute-start.7 = (bf16[512,1024]{1,0:T(8,128)(2,1)}, bf16[512,1024]{1,0:T(8,128)(2,1)}, u32[]{:S(2)}, u32[]{:S(2)}) collective-permute-start(bf16[512,1024]{1,0:T(8,128)(2,1)} %get-tuple-element.24.refs_6_.refs_9_), channel_id=1, source_target_pairs={{0,1},{1,0},{2,3},{3,2},{4,5},{5,4},{6,7},{7,6},{8,24},{9,25},{10,... | collective-permute-start | bytes 3145736 | tf_op jit(solution)/shard_map/ppermute | solution.py:505
  56.1 2.1 %collective-permute-done.5.refs_5_.refs_1_ = bf16[512,1024]{1,0:T(8,128)(2,1)} collective-permute-done((bf16[512,1024]{1,0:T(8,128)(2,1)}, bf16[512,1024]{1,0:T(8,128)(2,1)}, u32[]{:S(2)}, u32[]{:S(2)}) %collective-permute-start.5) | collective-permute-done | bytes 1048608 | tf_op jit(solution)/shard_map/ppermute | solution.py:505
  58.3 3.1 %shard_map.100 = (bf16[272,1024]{1,0:T(8,128)(2,1)}, bf16[256,1024]{1,0:T(8,128)(2,1)}, f32[1,1]{1,0:T(1,128)}) custom-call(bf16[512,1024]{1,0:T(8,128)(2,1)} %get-tuple-element.22.refs_0_, bf16[528,1024]{1,0:T(8,128)(2,1)} %collective-permute-done.3.refs_1_, bf16[272,1024]{1,0:T(8,128)(2,1)} %copy-done.3, bf16[16,1024]{1,0:T(8,128)(2,1)} %fusion.32.refs_3_, ...), custom_call_target="tpu_custom_call" | custom-call | tf_op jit(solution)/shard_map/pallas_call | solution.py:472
  61.4 2.5 %collective-permute-start.8 = (bf16[256,1024]{1,0:T(8,128)(2,1)}, bf16[256,1024]{1,0:T(8,128)(2,1)}, u32[]{:S(2)}, u32[]{:S(2)}) collective-permute-start(bf16[256,1024]{1,0:T(8,128)(2,1)} %get-tuple-element.27.refs_11_), channel_id=1, source_target_pairs={{0,16},{1,17},{2,18},{3,19},{4,20},{5,21},{6,22},{7,23},{8,9},{9,8... | collective-permute-start | bytes 1572872 | tf_op jit(solution)/shard_map/ppermute | solution.py:505
  63.9 10.5 %shard_map.101 = (bf16[512,1024]{1,0:T(8,128)(2,1)}, bf16[512,1024]{1,0:T(8,128)(2,1)}, f32[1,1]{1,0:T(1,128)}) custom-call(f32[3,189]{1,0:T(4,128)} %bitcast.39, s32[3,12]{1,0:T(4,128)} %copy-done.5, f32[12]{0:T(128)} %copy-done.7, s32[3,12]{1,0:T(4,128)} %copy-done.6, f32[12]{0:T(128)} %copy-done.8, bf16[12,512,512]{2,1,0:T(8,128)(2,1)} %refs_5_.7, ...), custom_call_target="tpu_custom_call" | custom-call | flops 1048576 | bytes 1048576 | tf_op jit(solution)/shard_map/pallas_call | solution.py:377
  74.5 1.6 %collective-permute-done.9.refs_3_ = bf16[272,1024]{1,0:T(8,128)(2,1)S(1)} collective-permute-done((bf16[272,1024]{1,0:T(8,128)(2,1)}, bf16[272,1024]{1,0:T(8,128)(2,1)S(1)}, u32[]{:S(2)}, u32[]{:S(2)}) %collective-permute-start.9) | collective-permute-done | bytes 557088 | tf_op jit(solution)/shard_map/ppermute | solution.py:505
  76.9 3.3 %shard_map.102 = (bf16[272,1024]{1,0:T(8,128)(2,1)}, bf16[256,1024]{1,0:T(8,128)(2,1)}, f32[1,1]{1,0:T(1,128)}) custom-call(bf16[512,1024]{1,0:T(8,128)(2,1)} %get-tuple-element.25.refs_4_.refs_0_, bf16[512,1024]{1,0:T(8,128)(2,1)} %collective-permute-done.5.refs_5_.refs_1_, bf16[256,1024]{1,0:T(8,128)(2,1)} %collective-permute-done.8.refs_2_, ...), custom_call_target="tpu_custom_call" | custom-call | tf_op jit(solution)/shard_map/pallas_call | solution.py:472
  80.2 3.2 %collective-permute-start.12 = (bf16[272,1024]{1,0:T(8,128)(2,1)}, bf16[272,1024]{1,0:T(8,128)(2,1)}, u32[]{:S(2)}, u32[]{:S(2)}) collective-permute-start(bf16[272,1024]{1,0:T(8,128)(2,1)} %get-tuple-element.34), channel_id=1, source_target_pairs={{0,4},{1,5},{2,6},{3,7},{4,0},{5,1},{6,2},{7,3},{8,12},{9,13},{10,... | collective-permute-start | bytes 1671176 | tf_op jit(solution)/shard_map/ppermute | solution.py:505
  83.6 12.7 %collective-permute-done.10.refs_2_ = bf16[256,1024]{1,0:T(8,128)(2,1)S(1)} collective-permute-done((bf16[256,1024]{1,0:T(8,128)(2,1)}, bf16[256,1024]{1,0:T(8,128)(2,1)S(1)}, u32[]{:S(2)}, u32[]{:S(2)}) %collective-permute-start.10) | collective-permute-done | bytes 524320 | tf_op jit(solution)/shard_map/ppermute | solution.py:505
  97.0 2.7 %shard_map.103 = (bf16[256,1024]{1,0:T(8,128)(2,1)}, f32[1,1]{1,0:T(1,128)}) custom-call(bf16[512,1024]{1,0:T(8,128)(2,1)} %get-tuple-element.30.refs_5_.refs_0_, bf16[512,1024]{1,0:T(8,128)(2,1)} %collective-permute-done.7.refs_6_.refs_1_, bf16[256,1024]{1,0:T(8,128)(2,1)} %copy-done.4), custom_call_target="tpu_custom_call" | custom-call | tf_op jit(solution)/shard_map/pallas_call | solution.py:472
  99.9 2.5 %shard_map.104 = (bf16[256,1024]{1,0:T(8,128)(2,1)}, f32[1,1]{1,0:T(1,128)}) custom-call(bf16[512,1024]{1,0:T(8,128)(2,1)} %get-tuple-element.28.refs_0_, bf16[512,1024]{1,0:T(8,128)(2,1)} %collective-permute-done.6.refs_1_, bf16[256,1024]{1,0:T(8,128)(2,1)} %get-tuple-element.32.refs_2_), custom_call_target="tpu_custom_call" | custom-call | tf_op jit(solution)/shard_map/pallas_call | solution.py:472
  103.5 4.8 %collective-permute-done.12 = bf16[272,1024]{1,0:T(8,128)(2,1)} collective-permute-done((bf16[272,1024]{1,0:T(8,128)(2,1)}, bf16[272,1024]{1,0:T(8,128)(2,1)}, u32[]{:S(2)}, u32[]{:S(2)}) %collective-permute-start.12) | collective-permute-done | bytes 557088 | tf_op jit(solution)/shard_map/ppermute | solution.py:505
  109.9 2.0 %collective-permute-done.11 = bf16[256,1024]{1,0:T(8,128)(2,1)S(1)} collective-permute-done((bf16[256,1024]{1,0:T(8,128)(2,1)}, bf16[256,1024]{1,0:T(8,128)(2,1)S(1)}, u32[]{:S(2)}, u32[]{:S(2)}) %collective-permute-start.11) | collective-permute-done | bytes 524320 | tf_op jit(solution)/shard_map/ppermute | solution.py:505
  111.9 1.5 %convert_add_fusion = f32[256,1024]{1,0:T(8,128)S(1)} fusion(bf16[256,1024]{1,0:T(8,128)(2,1)S(1)} %collective-permute-done.11, bf16[272,1024]{1,0:T(8,128)(2,1)} %collective-permute-done.12, bf16[512,1024]{1,0:T(8,128)(2,1)} %collective-permute-done.6.refs_1_, bf16[512,1024]{1,0:T(8,128)(2,1)S(1)} %copy-done), kind=kLoop, calls=%fused_computation.5 | loop fusion | flops 1835008 | bytes 3145728 | tf_op jit(solution)/shard_map/add | solution.py:629
  113.4 5.9 %collective-permute-done.13 = bf16[256,1024]{1,0:T(8,128)(2,1)S(1)} collective-permute-done((bf16[256,1024]{1,0:T(8,128)(2,1)}, bf16[256,1024]{1,0:T(8,128)(2,1)S(1)}, u32[]{:S(2)}, u32[]{:S(2)}) %collective-permute-start.13) | collective-permute-done | bytes 524320 | tf_op jit(solution)/shard_map/ppermute | solution.py:505
  119.3 1.3 %divide_bitcast_fusion = f32[1,256,1024]{2,1,0:T(8,128)} fusion(f32[256,1024]{1,0:T(8,128)S(1)} %fusion.1, f32[256,1024]{1,0:T(8,128)S(1)} %convert_add_fusion, bf16[256,1024]{1,0:T(8,128)(2,1)S(1)} %collective-permute-done.13), kind=kLoop, calls=%fused_computation.4 | loop fusion | flops 1048576 | bytes 3670016 | tf_op jit(solution)/shard_map/broadcast_in_dim | solution.py:647
  (61 shorter events, 11.3 us)
Async XLA Ops:
  0.6 13.2 %collective-permute-start.2 = (bf16[12,512,512]{2,1,0:T(8,128)(2,1)}, bf16[12,512,512]{2,1,0:T(8,128)(2,1)}, u32[]{:S(2)}, u32[]{:S(2)}) collective-permute-start(bf16[12,512,512]{2,1,0:T(8,128)(2,1)} %refs_5_.7), channel_id=1, source_target_pairs={{0,8},{1,9},{2,10},{3,11},{4,12},{5,13},{6,14},{7,15},{8,0},{9,1},... | collective-permute-start | bytes 18874376 | tf_op jit(solution)/shard_map/ppermute | solution.py:505
  2.6 1.9 %copy-start.5 = (s32[3,12]{1,0:T(4,128)}, s32[3,12]{1,0:T(4,128)S(1)}, u32[]{:S(2)}) copy-start(s32[3,12]{1,0:T(4,128)S(1)} %pad_add_fusion.refs_1_) | copy-start | bytes 436
  2.6 10.4 %collective-permute-start = (s32[3,12]{1,0:T(4,128)S(1)}, s32[3,12]{1,0:T(4,128)S(1)}, u32[]{:S(2)}, u32[]{:S(2)}) collective-permute-start(s32[3,12]{1,0:T(4,128)S(1)} %pad_add_fusion.refs_1_), channel_id=1, source_target_pairs={{0,8},{1,9},{2,10},{3,11},{4,12},{5,13},{6,14},{7,15},{8,0},{9,1},... | collective-permute-start | bytes 440 | tf_op jit(solution)/shard_map/ppermute | solution.py:505
  3.4 1.2 copy-start.7
  3.4 9.6 %collective-permute-start.1 = (f32[12]{0:T(128)S(1)}, f32[12]{0:T(128)S(1)}, u32[]{:S(2)}, u32[]{:S(2)}) collective-permute-start(f32[12]{0:T(128)S(1)} %convert_element_type.98.refs_2_), channel_id=1, source_target_pairs={{0,8},{1,9},{2,10},{3,11},{4,12},{5,13},{6,14},{7,15},{8,0},{9,1},... | collective-permute-start | bytes 152 | tf_op jit(solution)/shard_map/ppermute | solution.py:505
  13.0 0.8 copy-start.8
  13.0 0.8 copy-start.6
  23.0 16.3 %collective-permute-start.3 = (bf16[528,1024]{1,0:T(8,128)(2,1)}, bf16[528,1024]{1,0:T(8,128)(2,1)}, u32[]{:S(2)}, u32[]{:S(2)}) collective-permute-start(bf16[528,1024]{1,0:T(8,128)(2,1)} %get-tuple-element.20.refs_9_), channel_id=1, source_target_pairs={{0,1},{1,0},{2,3},{3,2},{4,5},{5,4},{6,7},{7,6},{8,24},{9,25},{10,... | collective-permute-start | bytes 3244040 | tf_op jit(solution)/shard_map/ppermute | solution.py:505
  37.1 21.1 %collective-permute-start.5 = (bf16[512,1024]{1,0:T(8,128)(2,1)}, bf16[512,1024]{1,0:T(8,128)(2,1)}, u32[]{:S(2)}, u32[]{:S(2)}) collective-permute-start(bf16[512,1024]{1,0:T(8,128)(2,1)} %get-tuple-element.21.refs_3_.refs_9_), channel_id=1, source_target_pairs={{0,1},{1,0},{2,3},{3,2},{4,5},{5,4},{6,7},{7,6},{8,24},{9,25},{10,... | collective-permute-start | bytes 3145736 | tf_op jit(solution)/shard_map/ppermute | solution.py:505
  43.4 12.0 %collective-permute-start.4 = (bf16[272,1024]{1,0:T(8,128)(2,1)}, bf16[272,1024]{1,0:T(8,128)(2,1)S(1)}, u32[]{:S(2)}, u32[]{:S(2)}) collective-permute-start(bf16[272,1024]{1,0:T(8,128)(2,1)} %get-tuple-element.23.refs_10_), channel_id=1, source_target_pairs={{0,16},{1,17},{2,18},{3,19},{4,20},{5,21},{6,22},{7,23},{8,9},{9,8... | collective-permute-start | bytes 1671176 | tf_op jit(solution)/shard_map/ppermute | solution.py:505
  53.6 23.3 %collective-permute-start.7 = (bf16[512,1024]{1,0:T(8,128)(2,1)}, bf16[512,1024]{1,0:T(8,128)(2,1)}, u32[]{:S(2)}, u32[]{:S(2)}) collective-permute-start(bf16[512,1024]{1,0:T(8,128)(2,1)} %get-tuple-element.24.refs_6_.refs_9_), channel_id=1, source_target_pairs={{0,1},{1,0},{2,3},{3,2},{4,5},{5,4},{6,7},{7,6},{8,24},{9,25},{10,... | collective-permute-start | bytes 3145736 | tf_op jit(solution)/shard_map/ppermute | solution.py:505
  55.4 2.9 %copy-start.3 = (bf16[272,1024]{1,0:T(8,128)(2,1)}, bf16[272,1024]{1,0:T(8,128)(2,1)S(1)}, u32[]{:S(2)}) copy-start(bf16[272,1024]{1,0:T(8,128)(2,1)S(1)} %collective-permute-done.4.refs_2_) | copy-start | bytes 1671172
  61.4 14.7 %collective-permute-start.9 = (bf16[272,1024]{1,0:T(8,128)(2,1)}, bf16[272,1024]{1,0:T(8,128)(2,1)S(1)}, u32[]{:S(2)}, u32[]{:S(2)}) collective-permute-start(bf16[272,1024]{1,0:T(8,128)(2,1)} %get-tuple-element.26.refs_10_), channel_id=1, source_target_pairs={{0,2},{1,3},{2,0},{3,1},{4,6},{5,7},{6,4},{7,5},{8,10},{9,11},{10,... | collective-permute-start | bytes 1671176 | tf_op jit(solution)/shard_map/ppermute | solution.py:505
  61.4 15.5 %collective-permute-start.8 = (bf16[256,1024]{1,0:T(8,128)(2,1)}, bf16[256,1024]{1,0:T(8,128)(2,1)}, u32[]{:S(2)}, u32[]{:S(2)}) collective-permute-start(bf16[256,1024]{1,0:T(8,128)(2,1)} %get-tuple-element.27.refs_11_), channel_id=1, source_target_pairs={{0,16},{1,17},{2,18},{3,19},{4,20},{5,21},{6,22},{7,23},{8,9},{9,8... | collective-permute-start | bytes 1572872 | tf_op jit(solution)/shard_map/ppermute | solution.py:505
  74.4 25.4 %collective-permute-start.6 = (bf16[512,1024]{1,0:T(8,128)(2,1)}, bf16[512,1024]{1,0:T(8,128)(2,1)}, u32[]{:S(2)}, u32[]{:S(2)}) collective-permute-start(bf16[512,1024]{1,0:T(8,128)(2,1)} %get-tuple-element.29.refs_7_), channel_id=1, source_target_pairs={{0,1},{1,0},{2,3},{3,2},{4,5},{5,4},{6,7},{7,6},{8,24},{9,25},{10,... | collective-permute-start | bytes 3145736 | tf_op jit(solution)/shard_map/ppermute | solution.py:505
  76.1 0.8 copy-start.2
  80.2 28.1 %collective-permute-start.12 = (bf16[272,1024]{1,0:T(8,128)(2,1)}, bf16[272,1024]{1,0:T(8,128)(2,1)}, u32[]{:S(2)}, u32[]{:S(2)}) collective-permute-start(bf16[272,1024]{1,0:T(8,128)(2,1)} %get-tuple-element.34), channel_id=1, source_target_pairs={{0,4},{1,5},{2,6},{3,7},{4,0},{5,1},{6,2},{7,3},{8,12},{9,13},{10,... | collective-permute-start | bytes 1671176 | tf_op jit(solution)/shard_map/ppermute | solution.py:505
  83.4 12.9 %collective-permute-start.10 = (bf16[256,1024]{1,0:T(8,128)(2,1)}, bf16[256,1024]{1,0:T(8,128)(2,1)S(1)}, u32[]{:S(2)}, u32[]{:S(2)}) collective-permute-start(bf16[256,1024]{1,0:T(8,128)(2,1)} %get-tuple-element.31), channel_id=1, source_target_pairs={{0,16},{1,17},{2,18},{3,19},{4,20},{5,21},{6,22},{7,23},{8,9},{9,8... | collective-permute-start | bytes 1572872 | tf_op jit(solution)/shard_map/ppermute | solution.py:505
  96.2 0.8 copy-start.4
  99.8 19.5 %collective-permute-start.13 = (bf16[256,1024]{1,0:T(8,128)(2,1)}, bf16[256,1024]{1,0:T(8,128)(2,1)S(1)}, u32[]{:S(2)}, u32[]{:S(2)}) collective-permute-start(bf16[256,1024]{1,0:T(8,128)(2,1)} %get-tuple-element.32.refs_2_), channel_id=1, source_target_pairs={{0,2},{1,3},{2,0},{3,1},{4,6},{5,7},{6,4},{7,5},{8,10},{9,11},{10,... | collective-permute-start | bytes 1572872 | tf_op jit(solution)/shard_map/ppermute | solution.py:505
  102.4 9.5 %copy-start = (bf16[512,1024]{1,0:T(8,128)(2,1)S(1)}, bf16[512,1024]{1,0:T(8,128)(2,1)}, u32[]{:S(2)}) copy-start(bf16[512,1024]{1,0:T(8,128)(2,1)} %get-tuple-element.28.refs_0_) | copy-start | bytes 3145732
  102.4 9.5 %collective-permute-start.11 = (bf16[256,1024]{1,0:T(8,128)(2,1)}, bf16[256,1024]{1,0:T(8,128)(2,1)S(1)}, u32[]{:S(2)}, u32[]{:S(2)}) collective-permute-start(bf16[256,1024]{1,0:T(8,128)(2,1)} %get-tuple-element.33), channel_id=1, source_target_pairs={{0,16},{1,17},{2,18},{3,19},{4,20},{5,21},{6,22},{7,23},{8,9},{9,8... | collective-permute-start | bytes 1572872 | tf_op jit(solution)/shard_map/ppermute | solution.py:505
  109.9 9.4 %copy-start.1 = (f32[256,1024]{1,0:T(8,128)}, f32[256,1024]{1,0:T(8,128)S(1)}, u32[]{:S(2)}) copy-start(f32[256,1024]{1,0:T(8,128)S(1)} %fusion.1) | copy-start | bytes 3145732

commit v5 on v4

--- a/solution.py
+++ b/solution.py
@@ -97,8 +97,7 @@
             cols = pl.ds(n * (QUARTER_COLS // 4), QUARTER_COLS // 4)
             far = other.at[cols]
             if out:
-                mine = canvas.at[pl.ds(COL_PAD + cols.start, cols.size), pl.ds(row_pad, rows), :]
-                copies.append(pltpu.make_async_copy(mine, far, side_sems.at[2 + n]))
+                copies.append(pltpu.make_async_copy(stages[0].at[cols], far, side_sems.at[2 + n]))
             else:
                 copies.append(pltpu.make_async_copy(far, early_ref.at[cols], side_sems.at[2 + n]))
         return copies
@@ -120,7 +119,7 @@
             )
         )
     token_ref[0, 0] = 0.0
-    for load in loads + late:
+    for load in loads:
         load.start()
 
     stripe_bits = stripe.bit_length() - 1
@@ -199,6 +198,8 @@
                 tile_buf[slot, top:bottom, :] = jnp.zeros((bottom - top, BLOCK), tile_buf.dtype)
     start(0, 0)
     start(1, 1)
+    for load in late:
+        load.start()
     canvas[COL_PAD : COL_PAD + QUARTER_COLS, row_pad : row_pad + rows, :] = jnp.zeros(
         (QUARTER_COLS, rows, LANES), jnp.float32
     )
@@ -318,7 +319,10 @@
 
     if not split:
         stores = canvas_copies(outs[0], True)
-        for store in stores:
+        for n, store in enumerate(stores):
+            low, size = n * (QUARTER_COLS // 4), QUARTER_COLS // 4
+            piece = canvas[COL_PAD + low : COL_PAD + low + size, row_pad : row_pad + rows, :]
+            stages[0][low : low + size] = piece.astype(jnp.bfloat16)
             store.start()
         for store in stores:
             store.wait()
@@ -341,7 +345,8 @@
                 piece = canvas[COL_PAD + side * TILE_COLS + j, pl.ds(at, stripe), :]
                 if has_start:
                     from_row = pl.multiple_of(slot * stripe, stripe)
-                    piece = piece + early_ref[side * TILE_COLS + j, pl.ds(from_row, stripe), :]
+                    early = early_ref[side * TILE_COLS + j, pl.ds(from_row, stripe), :]
+                    piece = piece + early.astype(jnp.float32)
                 stages[kind][i, :, j * LANES : (j + 1) * LANES] = piece.astype(out.dtype)
             for n in range(STREAMS):
                 size = stripe // STREAMS
@@ -371,8 +376,8 @@
             jax.ShapeDtypeStruct((rows, SIDE), jnp.bfloat16),
         ]
     else:
-        out_shape = [jax.ShapeDtypeStruct((QUARTER_COLS, rows, LANES), jnp.float32)]
-    stages = [pltpu.VMEM((slots, stripe, SIDE), item.dtype) for item in out_shape] if split else []
+        out_shape = [jax.ShapeDtypeStruct((QUARTER_COLS, rows, LANES), jnp.bfloat16)]
+    stages = [pltpu.VMEM((slots, stripe, SIDE) if split else item.shape, item.dtype) for item in out_shape]
     token = jax.ShapeDtypeStruct((1, 1), jnp.float32)
     return pl.pallas_call(
         functools.partial(quarter_kernel, geom, step, sources, has_start, split, len(after), fields is not None),
@@ -394,7 +399,7 @@
             pltpu.SemaphoreType.DMA((10 + STREAMS * 2 * slots,)),
         ]
         + stages
-        + ([pltpu.VMEM((QUARTER_COLS, rows, LANES), jnp.float32)] if has_start else []),
+        + ([pltpu.VMEM((QUARTER_COLS, rows, LANES), jnp.bfloat16)] if has_start else []),
         compiler_params=pltpu.CompilerParams(vmem_limit_bytes=63 * 1024 * 1024),
         cost_estimate=pl.CostEstimate(flops=1 << 20, bytes_accessed=1 << 20, transcendentals=0),
     )(table, *lists, *images, *bands, *([start] if has_start else []), *after, *([] if fields is None else [fields]))

time: 122 us -> 121 us (level); the launches traced: 121 us -> 122 us
  Pallas kernels: 63.4 us -> 61.5 us
  starting transfers between devices: 13.5 us -> 15.2 us
  waiting for transfers between devices: 30.4 us -> 31.8 us
    pallas_call x5, Pallas kernels: 49.1 us -> 47.2 us  [make_quarter(): pl.pallas_call(functools.partial(quarter_kernel, geom, step, sources, has...]
    ppermute x14, starting transfers between devices: 13.5 us -> 15.2 us  [swap(): return lax.ppermute(value, ('expo', 'patch'), route)]
    ppermute x14, waiting for transfers between devices: 30.4 us -> 31.8 us  [swap(): return lax.ppermute(value, ('expo', 'patch'), route)]
  transfers between devices with their start and end apart: 14 -> 14, of which waited for: 7 -> 7; matrix products, arithmetic and copies ran while one was open for 8% -> 8% of each run, Pallas kernels for 45% -> 43%
where the time goes in v5:
time: 121 us; the launch traced here: 122 us
  Pallas kernels  61.5 us (51%)
  waiting for transfers between devices  31.8 us (26%)
  starting transfers between devices  15.2 us (13%)
  other arithmetic  7.14 us (6%)
  local copies, waits for them, and re-layouts  3.8 us (3%)
  between operations  1.52 us (1%)
    pallas_call x5, Pallas kernels, make_quarter(): pl.pallas_call(functools.partial(quarter_kernel, geom, step, sources, has...  47.2 us
    ppermute x14, waiting for transfers between devices, swap(): return lax.ppermute(value, ('expo', 'patch'), route)  31.8 us
    ppermute x14, starting transfers between devices, swap(): return lax.ppermute(value, ('expo', 'patch'), route)  15.2 us
    pallas_call x5, Pallas kernels, merge(): pl.pallas_call(kernel, out_shape=shapes + [jax.ShapeDtypeStruct((1, 1), j...  14.3 us
  transfers between devices with their start and end apart: 14, of which 7 were waited for; matrix products, arithmetic and copies ran while one was open for 8% of the time, Pallas kernels for 43%

profile of v5, /device:TPU:0, one launch (start us, length us, event | category | flops | bytes accessed | tf_op | source)
XLA Modules:
  0.0 121.8 jit_solution(6224444080852979076)
XLA Ops:
  4.5 7.9 %shard_map.95 = (bf16[16,512,128]{2,1,0:T(8,128)(2,1)}, f32[1,1]{1,0:T(1,128)}) custom-call(f32[3,189]{1,0:T(4,128)} %bitcast.35, s32[3,12]{1,0:T(4,128)} %copy-done.5, f32[12]{0:T(128)} %copy-done.7, bf16[12,512,512]{2,1,0:T(8,128)(2,1)} %refs_5_.7, bf16[432,176]{1,0:T(8,128)(2,1)} %constant.132.clone.refs_4_.refs_7_, ...), custom_call_target="tpu_custom_call" | custom-call | flops 1048576 | bytes 1048576 | tf_op jit(solution)/shard_map/pallas_call | solution.py:382
  13.3 8.6 %shard_map.96 = (bf16[528,1024]{1,0:T(8,128)(2,1)}, bf16[512,1024]{1,0:T(8,128)(2,1)}, f32[1,1]{1,0:T(1,128)}) custom-call(f32[3,189]{1,0:T(4,128)} %bitcast.36, s32[3,12]{1,0:T(4,128)} %copy-done.6, f32[12]{0:T(128)} %copy-done.8, bf16[12,512,512]{2,1,0:T(8,128)(2,1)} %collective-permute-done.2.refs_3_.refs_6_, ...), custom_call_target="tpu_custom_call" | custom-call | flops 1048576 | bytes 1048576 | tf_op jit(solution)/shard_map/pallas_call | solution.py:382
  22.0 6.0 %collective-permute-start.3 = (bf16[528,1024]{1,0:T(8,128)(2,1)}, bf16[528,1024]{1,0:T(8,128)(2,1)}, u32[]{:S(2)}, u32[]{:S(2)}) collective-permute-start(bf16[528,1024]{1,0:T(8,128)(2,1)} %get-tuple-element.20.refs_9_), channel_id=1, source_target_pairs={{0,1},{1,0},{2,3},{3,2},{4,5},{5,4},{6,7},{7,6},{8,24},{9,25},{10,... | collective-permute-start | bytes 3244040 | tf_op jit(solution)/shard_map/ppermute | solution.py:510
  27.9 11.1 %shard_map.97 = (bf16[512,1024]{1,0:T(8,128)(2,1)}, bf16[512,1024]{1,0:T(8,128)(2,1)}, f32[1,1]{1,0:T(1,128)}) custom-call(f32[3,189]{1,0:T(4,128)} %bitcast.37, s32[3,12]{1,0:T(4,128)} %copy-done.5, f32[12]{0:T(128)} %copy-done.7, s32[3,12]{1,0:T(4,128)} %copy-done.6, f32[12]{0:T(128)} %copy-done.8, bf16[12,512,512]{2,1,0:T(8,128)(2,1)} %refs_5_.7, ...), custom_call_target="tpu_custom_call" | custom-call | flops 1048576 | bytes 1048576 | tf_op jit(solution)/shard_map/pallas_call | solution.py:382
  39.1 2.3 %collective-permute-done.3.refs_1_ = bf16[528,1024]{1,0:T(8,128)(2,1)} collective-permute-done((bf16[528,1024]{1,0:T(8,128)(2,1)}, bf16[528,1024]{1,0:T(8,128)(2,1)}, u32[]{:S(2)}, u32[]{:S(2)}) %collective-permute-start.3) | collective-permute-done | bytes 1081376 | tf_op jit(solution)/shard_map/ppermute | solution.py:510
  42.7 2.7 %shard_map.98 = (bf16[272,1024]{1,0:T(8,128)(2,1)}, f32[1,1]{1,0:T(1,128)}) custom-call(bf16[512,1024]{1,0:T(8,128)(2,1)} %get-tuple-element.22.refs_0_, bf16[528,1024]{1,0:T(8,128)(2,1)} %collective-permute-done.3.refs_1_, bf16[16,1024]{1,0:T(8,128)(2,1)} %fusion.29.refs_2_, bf16[512,1024]{1,0:T(8,128)(2,1)} %get-tuple-element.21.refs_3_.refs_9_), custom_call_target="tpu_custom_call" | custom-call | tf_op jit(solution)/shard_map/pallas_call | solution.py:477
  46.1 9.9 %shard_map.99 = (bf16[512,1024]{1,0:T(8,128)(2,1)}, bf16[512,1024]{1,0:T(8,128)(2,1)}, f32[1,1]{1,0:T(1,128)}) custom-call(f32[3,189]{1,0:T(4,128)} %bitcast.38, s32[3,12]{1,0:T(4,128)} %copy-done.5, f32[12]{0:T(128)} %copy-done.7, s32[3,12]{1,0:T(4,128)} %copy-done.6, f32[12]{0:T(128)} %copy-done.8, bf16[12,512,512]{2,1,0:T(8,128)(2,1)} %refs_5_.7, ...), custom_call_target="tpu_custom_call" | custom-call | flops 1048576 | bytes 1048576 | tf_op jit(solution)/shard_map/pallas_call | solution.py:382
  56.0 2.1 %collective-permute-start.7 = (bf16[512,1024]{1,0:T(8,128)(2,1)}, bf16[512,1024]{1,0:T(8,128)(2,1)}, u32[]{:S(2)}, u32[]{:S(2)}) collective-permute-start(bf16[512,1024]{1,0:T(8,128)(2,1)} %get-tuple-element.24.refs_6_.refs_9_), channel_id=1, source_target_pairs={{0,1},{1,0},{2,3},{3,2},{4,5},{5,4},{6,7},{7,6},{8,24},{9,25},{10,... | collective-permute-start | bytes 3145736 | tf_op jit(solution)/shard_map/ppermute | solution.py:510
  58.8 1.3 %collective-permute-done.5.refs_5_.refs_1_ = bf16[512,1024]{1,0:T(8,128)(2,1)} collective-permute-done((bf16[512,1024]{1,0:T(8,128)(2,1)}, bf16[512,1024]{1,0:T(8,128)(2,1)}, u32[]{:S(2)}, u32[]{:S(2)}) %collective-permute-start.5) | collective-permute-done | bytes 1048608 | tf_op jit(solution)/shard_map/ppermute | solution.py:510
  60.2 3.1 %shard_map.100 = (bf16[272,1024]{1,0:T(8,128)(2,1)}, bf16[256,1024]{1,0:T(8,128)(2,1)}, f32[1,1]{1,0:T(1,128)}) custom-call(bf16[512,1024]{1,0:T(8,128)(2,1)} %get-tuple-element.22.refs_0_, bf16[528,1024]{1,0:T(8,128)(2,1)} %collective-permute-done.3.refs_1_, bf16[272,1024]{1,0:T(8,128)(2,1)} %copy-done.3, bf16[16,1024]{1,0:T(8,128)(2,1)} %fusion.32.refs_3_, ...), custom_call_target="tpu_custom_call" | custom-call | tf_op jit(solution)/shard_map/pallas_call | solution.py:477
  64.0 9.7 %shard_map.101 = (bf16[512,1024]{1,0:T(8,128)(2,1)}, bf16[512,1024]{1,0:T(8,128)(2,1)}, f32[1,1]{1,0:T(1,128)}) custom-call(f32[3,189]{1,0:T(4,128)} %bitcast.39, s32[3,12]{1,0:T(4,128)} %copy-done.5, f32[12]{0:T(128)} %copy-done.7, s32[3,12]{1,0:T(4,128)} %copy-done.6, f32[12]{0:T(128)} %copy-done.8, bf16[12,512,512]{2,1,0:T(8,128)(2,1)} %refs_5_.7, ...), custom_call_target="tpu_custom_call" | custom-call | flops 1048576 | bytes 1048576 | tf_op jit(solution)/shard_map/pallas_call | solution.py:382
  73.8 4.4 %collective-permute-done.9.refs_3_ = bf16[272,1024]{1,0:T(8,128)(2,1)S(1)} collective-permute-done((bf16[272,1024]{1,0:T(8,128)(2,1)}, bf16[272,1024]{1,0:T(8,128)(2,1)S(1)}, u32[]{:S(2)}, u32[]{:S(2)}) %collective-permute-start.9) | collective-permute-done | bytes 557088 | tf_op jit(solution)/shard_map/ppermute | solution.py:510
  79.0 3.2 %shard_map.102 = (bf16[272,1024]{1,0:T(8,128)(2,1)}, bf16[256,1024]{1,0:T(8,128)(2,1)}, f32[1,1]{1,0:T(1,128)}) custom-call(bf16[512,1024]{1,0:T(8,128)(2,1)} %get-tuple-element.25.refs_4_.refs_0_, bf16[512,1024]{1,0:T(8,128)(2,1)} %collective-permute-done.5.refs_5_.refs_1_, bf16[256,1024]{1,0:T(8,128)(2,1)} %collective-permute-done.8.refs_2_, ...), custom_call_target="tpu_custom_call" | custom-call | tf_op jit(solution)/shard_map/pallas_call | solution.py:477
  82.3 0.8 collective-permute-start.12
  83.2 10.2 %collective-permute-done.10.refs_2_ = bf16[256,1024]{1,0:T(8,128)(2,1)S(1)} collective-permute-done((bf16[256,1024]{1,0:T(8,128)(2,1)}, bf16[256,1024]{1,0:T(8,128)(2,1)S(1)}, u32[]{:S(2)}, u32[]{:S(2)}) %collective-permute-start.10) | collective-permute-done | bytes 524320 | tf_op jit(solution)/shard_map/ppermute | solution.py:510
  93.3 0.8 copy-done.4
  94.1 2.8 %shard_map.103 = (bf16[256,1024]{1,0:T(8,128)(2,1)}, f32[1,1]{1,0:T(1,128)}) custom-call(bf16[512,1024]{1,0:T(8,128)(2,1)} %get-tuple-element.30.refs_5_.refs_0_, bf16[512,1024]{1,0:T(8,128)(2,1)} %collective-permute-done.7.refs_6_.refs_1_, bf16[256,1024]{1,0:T(8,128)(2,1)} %copy-done.4), custom_call_target="tpu_custom_call" | custom-call | tf_op jit(solution)/shard_map/pallas_call | solution.py:477
  96.9 3.2 %collective-permute-start.13 = (bf16[256,1024]{1,0:T(8,128)(2,1)}, bf16[256,1024]{1,0:T(8,128)(2,1)S(1)}, u32[]{:S(2)}, u32[]{:S(2)}) collective-permute-start(bf16[256,1024]{1,0:T(8,128)(2,1)} %get-tuple-element.32.refs_2_), channel_id=1, source_target_pairs={{0,2},{1,3},{2,0},{3,1},{4,6},{5,7},{6,4},{7,5},{8,10},{9,11},{10,... | collective-permute-start | bytes 1572872 | tf_op jit(solution)/shard_map/ppermute | solution.py:510
  100.1 2.5 %shard_map.104 = (bf16[256,1024]{1,0:T(8,128)(2,1)}, f32[1,1]{1,0:T(1,128)}) custom-call(bf16[512,1024]{1,0:T(8,128)(2,1)} %get-tuple-element.28.refs_0_, bf16[512,1024]{1,0:T(8,128)(2,1)} %collective-permute-done.6.refs_1_, bf16[256,1024]{1,0:T(8,128)(2,1)} %get-tuple-element.32.refs_2_), custom_call_target="tpu_custom_call" | custom-call | tf_op jit(solution)/shard_map/pallas_call | solution.py:477
  103.7 5.8 %collective-permute-done.12 = bf16[272,1024]{1,0:T(8,128)(2,1)} collective-permute-done((bf16[272,1024]{1,0:T(8,128)(2,1)}, bf16[272,1024]{1,0:T(8,128)(2,1)}, u32[]{:S(2)}, u32[]{:S(2)}) %collective-permute-start.12) | collective-permute-done | bytes 557088 | tf_op jit(solution)/shard_map/ppermute | solution.py:510
  111.1 1.0 collective-permute-done.11
  112.1 1.5 %convert_add_fusion = f32[256,1024]{1,0:T(8,128)S(1)} fusion(bf16[256,1024]{1,0:T(8,128)(2,1)S(1)} %collective-permute-done.11, bf16[272,1024]{1,0:T(8,128)(2,1)} %collective-permute-done.12, bf16[512,1024]{1,0:T(8,128)(2,1)} %collective-permute-done.6.refs_1_, bf16[512,1024]{1,0:T(8,128)(2,1)S(1)} %copy-done), kind=kLoop, calls=%fused_computation.5 | loop fusion | flops 1835008 | bytes 3145728 | tf_op jit(solution)/shard_map/add | solution.py:634
  113.7 6.9 %collective-permute-done.13 = bf16[256,1024]{1,0:T(8,128)(2,1)S(1)} collective-permute-done((bf16[256,1024]{1,0:T(8,128)(2,1)}, bf16[256,1024]{1,0:T(8,128)(2,1)S(1)}, u32[]{:S(2)}, u32[]{:S(2)}) %collective-permute-start.13) | collective-permute-done | bytes 524320 | tf_op jit(solution)/shard_map/ppermute | solution.py:510
  120.5 1.3 %divide_bitcast_fusion = f32[1,256,1024]{2,1,0:T(8,128)} fusion(f32[256,1024]{1,0:T(8,128)S(1)} %fusion.1, f32[256,1024]{1,0:T(8,128)S(1)} %convert_add_fusion, bf16[256,1024]{1,0:T(8,128)(2,1)S(1)} %collective-permute-done.13), kind=kLoop, calls=%fused_computation.4 | loop fusion | flops 1048576 | bytes 3670016 | tf_op jit(solution)/shard_map/broadcast_in_dim | solution.py:652
  (61 shorter events, 11.3 us)
Async XLA Ops:
  0.6 12.7 %collective-permute-start.2 = (bf16[12,512,512]{2,1,0:T(8,128)(2,1)}, bf16[12,512,512]{2,1,0:T(8,128)(2,1)}, u32[]{:S(2)}, u32[]{:S(2)}) collective-permute-start(bf16[12,512,512]{2,1,0:T(8,128)(2,1)} %refs_5_.7), channel_id=1, source_target_pairs={{0,8},{1,9},{2,10},{3,11},{4,12},{5,13},{6,14},{7,15},{8,0},{9,1},... | collective-permute-start | bytes 18874376 | tf_op jit(solution)/shard_map/ppermute | solution.py:510
  2.6 1.9 %copy-start.5 = (s32[3,12]{1,0:T(4,128)}, s32[3,12]{1,0:T(4,128)S(1)}, u32[]{:S(2)}) copy-start(s32[3,12]{1,0:T(4,128)S(1)} %pad_add_fusion.refs_1_) | copy-start | bytes 436
  2.6 9.9 %collective-permute-start = (s32[3,12]{1,0:T(4,128)S(1)}, s32[3,12]{1,0:T(4,128)S(1)}, u32[]{:S(2)}, u32[]{:S(2)}) collective-permute-start(s32[3,12]{1,0:T(4,128)S(1)} %pad_add_fusion.refs_1_), channel_id=1, source_target_pairs={{0,8},{1,9},{2,10},{3,11},{4,12},{5,13},{6,14},{7,15},{8,0},{9,1},... | collective-permute-start | bytes 440 | tf_op jit(solution)/shard_map/ppermute | solution.py:510
  3.4 1.2 copy-start.7
  3.4 9.1 %collective-permute-start.1 = (f32[12]{0:T(128)S(1)}, f32[12]{0:T(128)S(1)}, u32[]{:S(2)}, u32[]{:S(2)}) collective-permute-start(f32[12]{0:T(128)S(1)} %convert_element_type.98.refs_2_), channel_id=1, source_target_pairs={{0,8},{1,9},{2,10},{3,11},{4,12},{5,13},{6,14},{7,15},{8,0},{9,1},... | collective-permute-start | bytes 152 | tf_op jit(solution)/shard_map/ppermute | solution.py:510
  12.5 0.8 copy-start.8
  12.5 0.8 copy-start.6
  22.0 19.4 %collective-permute-start.3 = (bf16[528,1024]{1,0:T(8,128)(2,1)}, bf16[528,1024]{1,0:T(8,128)(2,1)}, u32[]{:S(2)}, u32[]{:S(2)}) collective-permute-start(bf16[528,1024]{1,0:T(8,128)(2,1)} %get-tuple-element.20.refs_9_), channel_id=1, source_target_pairs={{0,1},{1,0},{2,3},{3,2},{4,5},{5,4},{6,7},{7,6},{8,24},{9,25},{10,... | collective-permute-start | bytes 3244040 | tf_op jit(solution)/shard_map/ppermute | solution.py:510
  39.0 21.1 %collective-permute-start.5 = (bf16[512,1024]{1,0:T(8,128)(2,1)}, bf16[512,1024]{1,0:T(8,128)(2,1)}, u32[]{:S(2)}, u32[]{:S(2)}) collective-permute-start(bf16[512,1024]{1,0:T(8,128)(2,1)} %get-tuple-element.21.refs_3_.refs_9_), channel_id=1, source_target_pairs={{0,1},{1,0},{2,3},{3,2},{4,5},{5,4},{6,7},{7,6},{8,24},{9,25},{10,... | collective-permute-start | bytes 3145736 | tf_op jit(solution)/shard_map/ppermute | solution.py:510
  45.4 12.7 %collective-permute-start.4 = (bf16[272,1024]{1,0:T(8,128)(2,1)}, bf16[272,1024]{1,0:T(8,128)(2,1)S(1)}, u32[]{:S(2)}, u32[]{:S(2)}) collective-permute-start(bf16[272,1024]{1,0:T(8,128)(2,1)} %get-tuple-element.23.refs_10_), channel_id=1, source_target_pairs={{0,16},{1,17},{2,18},{3,19},{4,20},{5,21},{6,22},{7,23},{8,9},{9,8... | collective-permute-start | bytes 1671176 | tf_op jit(solution)/shard_map/ppermute | solution.py:510
  56.0 23.1 %collective-permute-start.7 = (bf16[512,1024]{1,0:T(8,128)(2,1)}, bf16[512,1024]{1,0:T(8,128)(2,1)}, u32[]{:S(2)}, u32[]{:S(2)}) collective-permute-start(bf16[512,1024]{1,0:T(8,128)(2,1)} %get-tuple-element.24.refs_6_.refs_9_), channel_id=1, source_target_pairs={{0,1},{1,0},{2,3},{3,2},{4,5},{5,4},{6,7},{7,6},{8,24},{9,25},{10,... | collective-permute-start | bytes 3145736 | tf_op jit(solution)/shard_map/ppermute | solution.py:510
  58.1 2.1 %copy-start.3 = (bf16[272,1024]{1,0:T(8,128)(2,1)}, bf16[272,1024]{1,0:T(8,128)(2,1)S(1)}, u32[]{:S(2)}) copy-start(bf16[272,1024]{1,0:T(8,128)(2,1)S(1)} %collective-permute-done.4.refs_2_) | copy-start | bytes 1671172
  63.2 15.0 %collective-permute-start.9 = (bf16[272,1024]{1,0:T(8,128)(2,1)}, bf16[272,1024]{1,0:T(8,128)(2,1)S(1)}, u32[]{:S(2)}, u32[]{:S(2)}) collective-permute-start(bf16[272,1024]{1,0:T(8,128)(2,1)} %get-tuple-element.26.refs_10_), channel_id=1, source_target_pairs={{0,2},{1,3},{2,0},{3,1},{4,6},{5,7},{6,4},{7,5},{8,10},{9,11},{10,... | collective-permute-start | bytes 1671176 | tf_op jit(solution)/shard_map/ppermute | solution.py:510
  63.3 15.7 %collective-permute-start.8 = (bf16[256,1024]{1,0:T(8,128)(2,1)}, bf16[256,1024]{1,0:T(8,128)(2,1)}, u32[]{:S(2)}, u32[]{:S(2)}) collective-permute-start(bf16[256,1024]{1,0:T(8,128)(2,1)} %get-tuple-element.27.refs_11_), channel_id=1, source_target_pairs={{0,16},{1,17},{2,18},{3,19},{4,20},{5,21},{6,22},{7,23},{8,9},{9,8... | collective-permute-start | bytes 1572872 | tf_op jit(solution)/shard_map/ppermute | solution.py:510
  73.8 26.4 %collective-permute-start.6 = (bf16[512,1024]{1,0:T(8,128)(2,1)}, bf16[512,1024]{1,0:T(8,128)(2,1)}, u32[]{:S(2)}, u32[]{:S(2)}) collective-permute-start(bf16[512,1024]{1,0:T(8,128)(2,1)} %get-tuple-element.29.refs_7_), channel_id=1, source_target_pairs={{0,1},{1,0},{2,3},{3,2},{4,5},{5,4},{6,7},{7,6},{8,24},{9,25},{10,... | collective-permute-start | bytes 3145736 | tf_op jit(solution)/shard_map/ppermute | solution.py:510
  78.2 0.8 copy-start.2
  82.3 27.2 %collective-permute-start.12 = (bf16[272,1024]{1,0:T(8,128)(2,1)}, bf16[272,1024]{1,0:T(8,128)(2,1)}, u32[]{:S(2)}, u32[]{:S(2)}) collective-permute-start(bf16[272,1024]{1,0:T(8,128)(2,1)} %get-tuple-element.34), channel_id=1, source_target_pairs={{0,4},{1,5},{2,6},{3,7},{4,0},{5,1},{6,2},{7,3},{8,12},{9,13},{10,... | collective-permute-start | bytes 1671176 | tf_op jit(solution)/shard_map/ppermute | solution.py:510
  83.1 10.2 %collective-permute-start.10 = (bf16[256,1024]{1,0:T(8,128)(2,1)}, bf16[256,1024]{1,0:T(8,128)(2,1)S(1)}, u32[]{:S(2)}, u32[]{:S(2)}) collective-permute-start(bf16[256,1024]{1,0:T(8,128)(2,1)} %get-tuple-element.31), channel_id=1, source_target_pairs={{0,16},{1,17},{2,18},{3,19},{4,20},{5,21},{6,22},{7,23},{8,9},{9,8... | collective-permute-start | bytes 1572872 | tf_op jit(solution)/shard_map/ppermute | solution.py:510
  93.3 0.8 copy-start.4
  96.9 23.6 %collective-permute-start.13 = (bf16[256,1024]{1,0:T(8,128)(2,1)}, bf16[256,1024]{1,0:T(8,128)(2,1)S(1)}, u32[]{:S(2)}, u32[]{:S(2)}) collective-permute-start(bf16[256,1024]{1,0:T(8,128)(2,1)} %get-tuple-element.32.refs_2_), channel_id=1, source_target_pairs={{0,2},{1,3},{2,0},{3,1},{4,6},{5,7},{6,4},{7,5},{8,10},{9,11},{10,... | collective-permute-start | bytes 1572872 | tf_op jit(solution)/shard_map/ppermute | solution.py:510
  102.6 9.5 %copy-start = (bf16[512,1024]{1,0:T(8,128)(2,1)S(1)}, bf16[512,1024]{1,0:T(8,128)(2,1)}, u32[]{:S(2)}) copy-start(bf16[512,1024]{1,0:T(8,128)(2,1)} %get-tuple-element.28.refs_0_) | copy-start | bytes 3145732
  102.7 9.5 %collective-permute-start.11 = (bf16[256,1024]{1,0:T(8,128)(2,1)}, bf16[256,1024]{1,0:T(8,128)(2,1)S(1)}, u32[]{:S(2)}, u32[]{:S(2)}) collective-permute-start(bf16[256,1024]{1,0:T(8,128)(2,1)} %get-tuple-element.33), channel_id=1, source_target_pairs={{0,16},{1,17},{2,18},{3,19},{4,20},{5,21},{6,22},{7,23},{8,9},{9,8... | collective-permute-start | bytes 1572872 | tf_op jit(solution)/shard_map/ppermute | solution.py:510
  111.1 9.4 %copy-start.1 = (f32[256,1024]{1,0:T(8,128)}, f32[256,1024]{1,0:T(8,128)S(1)}, u32[]{:S(2)}) copy-start(f32[256,1024]{1,0:T(8,128)S(1)} %fusion.1) | copy-start | bytes 3145732
